TPU v7x, 32 devices: a whole 2x2x4 slice. The times are simulated.
32 devices in a mesh: dp: 8 (over z, y), fsdp: 2 (over core), seq: 2 (over x).
Axes of the slice: x: 2, y: 2, z: 4, core: 2. Of those that a mesh axis runs over, the one named last changes fastest.
Arguments:
- states: bfloat16 [16, 1024, 768], P(('dp', 'fsdp'), 'seq'), may hold values from -6 to 6
- deleted: int32 [16, 1024], P(('dp', 'fsdp'), 'seq'), may hold values 0 or 1
- crop_lengths: int32 [16, 8], P(('dp', 'fsdp')), may hold values from 0 to 768, as said below
- query_weight: float32 [768, 768], P(('dp', 'fsdp', 'seq')), may hold values from -0.21875 to 0.21875
- query_bias: float32 [768], P(('dp', 'fsdp', 'seq')), may hold values from -3 to 3
- key_weight: float32 [768, 768], P(('dp', 'fsdp', 'seq')), may hold values from -0.21875 to 0.21875
- value_weight: float32 [768, 768], P(('dp', 'fsdp', 'seq')), may hold values from -0.21875 to 0.21875
- value_bias: float32 [768], P(('dp', 'fsdp', 'seq')), may hold values from -0.3125 to 0.3125
- output_weight: float32 [768, 768], P(('dp', 'fsdp', 'seq')), may hold values from -1.75 to 1.75
- output_bias: float32 [768], P(('dp', 'fsdp', 'seq')), may hold values from -1.75 to 1.75
- attn_gain: float32 [768], P(('dp', 'fsdp', 'seq')), may hold values from 0.5 to 1.5
- attn_shift: float32 [768], P(('dp', 'fsdp', 'seq')), may hold values from -1.75 to 1.75
- inner_weight: float32 [768, 3072], P(('dp', 'fsdp', 'seq')), may hold values from -0.21875 to 0.21875
- inner_bias: float32 [3072], P(('dp', 'fsdp', 'seq')), may hold values from -1.75 to 1.75
- outer_weight: float32 [3072, 768], P(('dp', 'fsdp', 'seq')), may hold values from -0.15625 to 0.15625
- outer_bias: float32 [768], P(('dp', 'fsdp', 'seq')), may hold values from -1.75 to 1.75
- final_gain: float32 [768], P(('dp', 'fsdp', 'seq')), may hold values from 0.5 to 1.5
- final_shift: float32 [768], P(('dp', 'fsdp', 'seq')), may hold values from -1.75 to 1.75
- cotangent: bfloat16 [16, 1024, 768], P(('dp', 'fsdp'), 'seq'), may hold values from -6 to 6
- pool_cotangent: float32 [16, 8, 768], P(('dp', 'fsdp')), may hold values from -768 to 768
Outputs:
- output: bfloat16 [16, 1024, 768], P(('dp', 'fsdp'), 'seq')
- pooled: float32 [16, 8, 768], P(('dp', 'fsdp'))
- states_grad: float32 [16, 1024, 768], P(('dp', 'fsdp'), 'seq')
- grad_query_weight: float32 [768, 768], P(('dp', 'fsdp', 'seq'))
- grad_query_bias: float32 [768], P(('dp', 'fsdp', 'seq'))
- grad_key_weight: float32 [768, 768], P(('dp', 'fsdp', 'seq'))
- grad_value_weight: float32 [768, 768], P(('dp', 'fsdp', 'seq'))
- grad_value_bias: float32 [768], P(('dp', 'fsdp', 'seq'))
- grad_output_weight: float32 [768, 768], P(('dp', 'fsdp', 'seq'))
- grad_output_bias: float32 [768], P(('dp', 'fsdp', 'seq'))
- grad_attn_gain: float32 [768], P(('dp', 'fsdp', 'seq'))
- grad_attn_shift: float32 [768], P(('dp', 'fsdp', 'seq'))
- grad_inner_weight: float32 [768, 3072], P(('dp', 'fsdp', 'seq'))
- grad_inner_bias: float32 [3072], P(('dp', 'fsdp', 'seq'))
- grad_outer_weight: float32 [3072, 768], P(('dp', 'fsdp', 'seq'))
- grad_outer_bias: float32 [768], P(('dp', 'fsdp', 'seq'))
- grad_final_gain: float32 [768], P(('dp', 'fsdp', 'seq'))
- grad_final_shift: float32 [768], P(('dp', 'fsdp', 'seq'))
Inputs may be any that keep to these rules, and one draw needn't show every extreme that they name: `crop_lengths`: in every row the crops lie back to back from the row's first token and leave one or more padding tokens at its end. The rows fall into groups of 8 consecutive rows (rows 8k to 8k + 7); in each group exactly one row holds a single crop that ends half of 512 tokens before the row's end, its other slots empty. In every other row each crop has at most 256 tokens, and each nonempty crop but the row's last has half of 256 tokens or more.
All inputs are finite; a program needn't handle non-finite values. No bound on the sum of `deleted` on one device may be relied on, other than what follows from the above.
Results may differ from a plain program's by a relative error of at most 0.014.
The roundings to bfloat16 on the way count: a program that leaves them out, or rounds other values in their place, can miss the bound.
Values may be sent and summed in bfloat16 or wider, within the bound.
No kernel may reach another device: no remote copies, remote signals or barrier semaphores. Data moves between devices by JAX's collectives and lax.ppermute only.
A program may use at most 128 MiB of HBM per device.

v0:
```python
from functools import partial

import jax
import jax.numpy as jnp
from jax import lax
from jax.sharding import PartitionSpec as P

HEADS = 12
HEAD = 64


highest = lax.Precision.HIGHEST


def layer_norm(values, gain, shift):
    centered = values - jnp.mean(values, axis=-1, keepdims=True)
    spread = jnp.mean(centered * centered, axis=-1, keepdims=True)
    return centered * lax.rsqrt(spread + 1e-06) * gain + shift


def crop_layout(lengths, deleted, places):
    crop_ends = jnp.cumsum(lengths, axis=-1, dtype=jnp.int32)
    segment = jnp.sum(
        (places[..., :, None] >= crop_ends[..., None, :]).astype(jnp.int32),
        axis=-1,
        dtype=jnp.int32,
    )
    retained = (deleted == 0) & (segment < lengths.shape[-1])
    key_tag = jnp.where(retained, segment, -1)
    return (segment, retained, key_tag)


def product(left, right):
    return jnp.dot(left, right, preferred_element_type=jnp.float32)


def column_sum(values):
    return jnp.sum(values.astype(jnp.float32), axis=0)


def sweep(carry, pieces, inner):
    count = pieces[0].shape[1]
    width = 256

    def turn(index, totals):
        offset = index * width
        parts = tuple((lax.dynamic_slice_in_dim(piece, offset, width, 1) for piece in pieces))
        return inner(totals, parts, offset)

    return lax.fori_loop(0, count // width, turn, carry)


def scores_at(query_part, key_part):
    return (
        jnp.einsum("rqhd,rkhd->rhqk", query_part, key_part, preferred_element_type=jnp.float32)
        * 0.125
    )


def allowed_at(query_tag, query_place, tags, begin):
    key_place = begin + jnp.arange(tags.shape[1], dtype=jnp.int32)
    same = tags[:, None, :] == query_tag[:, :, None]
    itself = key_place[None, None, :] == query_place[None, :, None]
    return (same | itself)[:, None]


def probs_at(raw, allowed, log_part):
    return jnp.where(allowed, jnp.exp(raw - log_part[..., None]), 0.0)


def body(
    states,
    deleted,
    crop_lengths,
    query_weight,
    query_bias,
    key_weight,
    value_weight,
    value_bias,
    output_weight,
    output_bias,
    attn_gain,
    attn_shift,
    inner_weight,
    inner_bias,
    outer_weight,
    outer_bias,
    final_gain,
    final_shift,
    cotangent,
    pool_cotangent,
):
    rows, shard, width = states.shape
    lowered = [
        master.astype(jnp.bfloat16)
        for master in (
            query_weight,
            query_bias,
            key_weight,
            value_weight,
            value_bias,
            output_weight,
            output_bias,
            attn_gain,
            attn_shift,
            inner_weight,
            inner_bias,
            outer_weight,
            outer_bias,
            final_gain,
            final_shift,
        )
    ]
    (
        w_query,
        b_query,
        w_key,
        w_value,
        b_value,
        w_out,
        b_out,
        g_attn,
        s_attn,
        w_inner,
        b_inner,
        w_outer,
        b_outer,
        g_final,
        s_final,
    ) = (
        lax.all_gather(lowered[0], ("dp", "fsdp", "seq"), axis=0, tiled=True),
        lax.all_gather(lowered[1], ("dp", "fsdp", "seq"), axis=0, tiled=True),
        lax.all_gather(lowered[2], ("dp", "fsdp", "seq"), axis=0, tiled=True),
        lax.all_gather(lowered[3], ("dp", "fsdp", "seq"), axis=0, tiled=True),
        lax.all_gather(lowered[4], ("dp", "fsdp", "seq"), axis=0, tiled=True),
        lax.all_gather(lowered[5], ("dp", "fsdp", "seq"), axis=0, tiled=True),
        lax.all_gather(lowered[6], ("dp", "fsdp", "seq"), axis=0, tiled=True),
        lax.all_gather(lowered[7], ("dp", "fsdp", "seq"), axis=0, tiled=True),
        lax.all_gather(lowered[8], ("dp", "fsdp", "seq"), axis=0, tiled=True),
        lax.all_gather(lowered[9], ("dp", "fsdp", "seq"), axis=0, tiled=True),
        lax.all_gather(lowered[10], ("dp", "fsdp", "seq"), axis=0, tiled=True),
        lax.all_gather(lowered[11], ("dp", "fsdp", "seq"), axis=0, tiled=True),
        lax.all_gather(lowered[12], ("dp", "fsdp", "seq"), axis=0, tiled=True),
        lax.all_gather(lowered[13], ("dp", "fsdp", "seq"), axis=0, tiled=True),
        lax.all_gather(lowered[14], ("dp", "fsdp", "seq"), axis=0, tiled=True),
    )
    own_start = lax.axis_index("seq") * shard
    places = own_start + jnp.arange(shard, dtype=jnp.int32)
    segment, retained, key_tag = crop_layout(crop_lengths, deleted, places)
    flat = states.reshape(rows * shard, width)
    split = (rows, shard, HEADS, HEAD)
    queries = (product(flat, w_query) + b_query).astype(jnp.bfloat16).reshape(split)
    keys = product(flat, w_key).astype(jnp.bfloat16).reshape(split)
    values = (product(flat, w_value) + b_value).astype(jnp.bfloat16).reshape(split)

    def scale_step(totals, parts, begin):
        top, total = totals
        key_part, tags = parts
        allowed = allowed_at(segment, places, tags, begin)
        masked = jnp.where(allowed, scores_at(queries, key_part), -1e30)
        new_top = jnp.maximum(top, jnp.max(masked, axis=-1))
        raised = jnp.where(allowed, jnp.exp(masked - new_top[..., None]), 0.0)
        return (new_top, total * jnp.exp(top - new_top) + jnp.sum(raised, axis=-1))

    stat_shape = (rows, HEADS, shard)
    scale_init = (jnp.full(stat_shape, -1e30, jnp.float32), jnp.zeros(stat_shape, jnp.float32))
    top, total = sweep(
        scale_init,
        (
            lax.all_gather(keys, "seq", axis=1, tiled=True),
            lax.all_gather(key_tag, "seq", axis=1, tiled=True),
        ),
        inner=scale_step,
    )
    log_total = top + jnp.log(total)

    def mix_step(totals, parts, begin):
        coarse, fine = totals
        key_part, value_part, tags = parts
        probs = probs_at(
            scores_at(queries, key_part), allowed_at(segment, places, tags, begin), log_total
        )
        probs_low = probs.astype(jnp.bfloat16)
        rest = (probs - probs_low.astype(jnp.float32)).astype(jnp.bfloat16)
        coarse = coarse + jnp.einsum(
            "rhqk,rkhd->rqhd", probs_low, value_part, preferred_element_type=jnp.float32
        )
        fine = fine + jnp.einsum(
            "rhqk,rkhd->rqhd", rest, value_part, preferred_element_type=jnp.float32
        )
        return (coarse, fine)

    empty = jnp.zeros(split, jnp.float32)
    coarse, fine = sweep(
        (empty, empty),
        (
            lax.all_gather(keys, "seq", axis=1, tiled=True),
            lax.all_gather(values, "seq", axis=1, tiled=True),
            lax.all_gather(key_tag, "seq", axis=1, tiled=True),
        ),
        inner=mix_step,
    )
    attended = coarse.astype(jnp.bfloat16).reshape(rows * shard, width)
    branch = product(attended, w_out) + b_out
    residual = states.astype(jnp.float32).reshape(rows * shard, width) + branch
    normed, attn_back = jax.vjp(
        layer_norm, residual, g_attn.astype(jnp.float32), s_attn.astype(jnp.float32)
    )
    normed_low = normed.astype(jnp.bfloat16)
    inner = product(normed_low, w_inner) + b_inner
    active_full, gelu_back = jax.vjp(partial(jax.nn.gelu, approximate=False), inner)
    active = active_full.astype(jnp.bfloat16)
    outer = product(active, w_outer) + b_outer
    result, final_back = jax.vjp(
        layer_norm, normed + outer, g_final.astype(jnp.float32), s_final.astype(jnp.float32)
    )
    output = result.astype(jnp.bfloat16).reshape(rows, shard, width)
    crops = crop_lengths.shape[1]
    member = (
        (segment[..., None] == jnp.arange(crops, dtype=jnp.int32)) & retained[..., None]
    ).astype(jnp.float32)
    partial_sums = jnp.einsum(
        "rnc,rnd->rcd",
        member,
        result.reshape(rows, shard, width),
        precision=highest,
        preferred_element_type=jnp.float32,
    )
    sums, counts = lax.psum((partial_sums, jnp.sum(member, axis=1)), "seq")
    divisor = jnp.maximum(counts, 1.0)[..., None]
    pooled = sums / divisor
    w_query, w_key, w_value, w_out, w_inner, w_outer = (
        lax.all_gather(lowered[0], ("dp", "fsdp", "seq"), axis=0, tiled=True),
        lax.all_gather(lowered[2], ("dp", "fsdp", "seq"), axis=0, tiled=True),
        lax.all_gather(lowered[3], ("dp", "fsdp", "seq"), axis=0, tiled=True),
        lax.all_gather(lowered[5], ("dp", "fsdp", "seq"), axis=0, tiled=True),
        lax.all_gather(lowered[9], ("dp", "fsdp", "seq"), axis=0, tiled=True),
        lax.all_gather(lowered[11], ("dp", "fsdp", "seq"), axis=0, tiled=True),
    )
    result_grad = cotangent.astype(jnp.float32) + jnp.einsum(
        "rnc,rcd->rnd",
        member,
        pool_cotangent / divisor,
        precision=highest,
        preferred_element_type=jnp.float32,
    )
    sum_grad, grad_final_gain, grad_final_shift = final_back(
        result_grad.reshape(rows * shard, width)
    )
    outer_grad = sum_grad.astype(jnp.bfloat16)
    grad_outer_bias = column_sum(outer_grad)
    grad_outer_weight = product(active.T, outer_grad)
    inner_grad = gelu_back(product(outer_grad, w_outer.T))[0].astype(jnp.bfloat16)
    grad_inner_bias = column_sum(inner_grad)
    grad_inner_weight = product(normed_low.T, inner_grad)
    normed_grad = sum_grad + product(inner_grad, w_inner.T)
    residual_grad, grad_attn_gain, grad_attn_shift = attn_back(normed_grad)
    branch_grad = residual_grad.astype(jnp.bfloat16)
    grad_output_bias = column_sum(branch_grad)
    grad_output_weight = product(attended.T, branch_grad)
    mixed_grad = product(branch_grad, w_out.T).astype(jnp.bfloat16).reshape(split)
    delta = jnp.sum(mixed_grad.astype(jnp.float32) * (coarse + fine), axis=-1)
    delta_local = jnp.transpose(delta, (0, 2, 1))
    all_log, all_delta = (
        lax.all_gather(jnp.transpose(log_total, (0, 2, 1)), "seq", axis=1, tiled=True),
        lax.all_gather(delta, "seq", axis=1, tiled=True),
    )

    def key_side(totals, parts, begin):
        key_grad, value_grad = totals
        query_part, grad_part, tags_part = parts
        count = tags_part.shape[1]
        log_part = jnp.transpose(lax.dynamic_slice_in_dim(all_log, begin, count, 1), (0, 2, 1))
        delta_part = jnp.transpose(lax.dynamic_slice_in_dim(all_delta, begin, count, 1), (0, 2, 1))
        query_place = begin + jnp.arange(count, dtype=jnp.int32)
        allowed = allowed_at(tags_part, query_place, key_tag, own_start)
        probs = probs_at(scores_at(query_part, keys), allowed, log_part)
        value_grad = value_grad + jnp.einsum(
            "rhqk,rqhd->rkhd",
            probs.astype(jnp.bfloat16),
            grad_part,
            preferred_element_type=jnp.float32,
        )
        prob_grad = jnp.einsum(
            "rqhd,rkhd->rhqk", grad_part, values, preferred_element_type=jnp.float32
        )
        score_grad = (probs * (prob_grad - delta_part[..., None]) * 0.125).astype(jnp.bfloat16)
        key_grad = key_grad + jnp.einsum(
            "rhqk,rqhd->rkhd", score_grad, query_part, preferred_element_type=jnp.float32
        )
        return (key_grad, value_grad)

    key_grad, value_grad = sweep(
        (empty, empty),
        (
            lax.all_gather(queries, "seq", axis=1, tiled=True),
            lax.all_gather(mixed_grad, "seq", axis=1, tiled=True),
            lax.all_gather(segment, "seq", axis=1, tiled=True),
        ),
        inner=key_side,
    )

    def query_side(query_grad, parts, begin):
        key_part, value_part, tags = parts
        probs = probs_at(
            scores_at(queries, key_part), allowed_at(segment, places, tags, begin), log_total
        )
        prob_grad = jnp.einsum(
            "rqhd,rkhd->rhqk", mixed_grad, value_part, preferred_element_type=jnp.float32
        )
        score_grad = (probs * (prob_grad - delta_local[..., None]) * 0.125).astype(jnp.bfloat16)
        return query_grad + jnp.einsum(
            "rhqk,rkhd->rqhd", score_grad, key_part, preferred_element_type=jnp.float32
        )

    query_grad = sweep(
        empty,
        (
            lax.all_gather(keys, "seq", axis=1, tiled=True),
            lax.all_gather(values, "seq", axis=1, tiled=True),
            lax.all_gather(key_tag, "seq", axis=1, tiled=True),
        ),
        inner=query_side,
    )
    query_low = query_grad.astype(jnp.bfloat16).reshape(rows * shard, width)
    key_low = key_grad.astype(jnp.bfloat16).reshape(rows * shard, width)
    value_low = value_grad.astype(jnp.bfloat16).reshape(rows * shard, width)
    grad_query_weight = product(flat.T, query_low)
    grad_query_bias = column_sum(query_low)
    grad_key_weight = product(flat.T, key_low)
    grad_value_weight = product(flat.T, value_low)
    grad_value_bias = column_sum(value_low)
    states_grad = (
        residual_grad
        + product(query_low, w_query.T)
        + product(key_low, w_key.T)
        + product(value_low, w_value.T)
    ).reshape(rows, shard, width)
    summed = (
        lax.psum_scatter(grad_query_weight, ("dp", "fsdp", "seq"), scatter_dimension=0, tiled=True),
        lax.psum_scatter(grad_query_bias, ("dp", "fsdp", "seq"), scatter_dimension=0, tiled=True),
        lax.psum_scatter(grad_key_weight, ("dp", "fsdp", "seq"), scatter_dimension=0, tiled=True),
        lax.psum_scatter(grad_value_weight, ("dp", "fsdp", "seq"), scatter_dimension=0, tiled=True),
        lax.psum_scatter(grad_value_bias, ("dp", "fsdp", "seq"), scatter_dimension=0, tiled=True),
        lax.psum_scatter(
            grad_output_weight, ("dp", "fsdp", "seq"), scatter_dimension=0, tiled=True
        ),
        lax.psum_scatter(grad_output_bias, ("dp", "fsdp", "seq"), scatter_dimension=0, tiled=True),
        lax.psum_scatter(grad_attn_gain, ("dp", "fsdp", "seq"), scatter_dimension=0, tiled=True),
        lax.psum_scatter(grad_attn_shift, ("dp", "fsdp", "seq"), scatter_dimension=0, tiled=True),
        lax.psum_scatter(grad_inner_weight, ("dp", "fsdp", "seq"), scatter_dimension=0, tiled=True),
        lax.psum_scatter(grad_inner_bias, ("dp", "fsdp", "seq"), scatter_dimension=0, tiled=True),
        lax.psum_scatter(grad_outer_weight, ("dp", "fsdp", "seq"), scatter_dimension=0, tiled=True),
        lax.psum_scatter(grad_outer_bias, ("dp", "fsdp", "seq"), scatter_dimension=0, tiled=True),
        lax.psum_scatter(grad_final_gain, ("dp", "fsdp", "seq"), scatter_dimension=0, tiled=True),
        lax.psum_scatter(grad_final_shift, ("dp", "fsdp", "seq"), scatter_dimension=0, tiled=True),
    )
    return (output, pooled, states_grad) + tuple(summed)


def solution(mesh):
    in_specs = (
        P(("dp", "fsdp"), "seq", None),
        P(("dp", "fsdp"), "seq"),
        P(("dp", "fsdp"), None),
        P(("dp", "fsdp", "seq"), None),
        P(("dp", "fsdp", "seq")),
        P(("dp", "fsdp", "seq"), None),
        P(("dp", "fsdp", "seq"), None),
        P(("dp", "fsdp", "seq")),
        P(("dp", "fsdp", "seq"), None),
        P(("dp", "fsdp", "seq")),
        P(("dp", "fsdp", "seq")),
        P(("dp", "fsdp", "seq")),
        P(("dp", "fsdp", "seq"), None),
        P(("dp", "fsdp", "seq")),
        P(("dp", "fsdp", "seq"), None),
        P(("dp", "fsdp", "seq")),
        P(("dp", "fsdp", "seq")),
        P(("dp", "fsdp", "seq")),
        P(("dp", "fsdp"), "seq", None),
        P(("dp", "fsdp"), None, None),
    )
    out_specs = (
        P(("dp", "fsdp"), "seq", None),
        P(("dp", "fsdp"), None, None),
        P(("dp", "fsdp"), "seq", None),
        P(("dp", "fsdp", "seq"), None),
        P(("dp", "fsdp", "seq")),
        P(("dp", "fsdp", "seq"), None),
        P(("dp", "fsdp", "seq"), None),
        P(("dp", "fsdp", "seq")),
        P(("dp", "fsdp", "seq"), None),
        P(("dp", "fsdp", "seq")),
        P(("dp", "fsdp", "seq")),
        P(("dp", "fsdp", "seq")),
        P(("dp", "fsdp", "seq"), None),
        P(("dp", "fsdp", "seq")),
        P(("dp", "fsdp", "seq"), None),
        P(("dp", "fsdp", "seq")),
        P(("dp", "fsdp", "seq")),
        P(("dp", "fsdp", "seq")),
    )
    return jax.shard_map(body, mesh=mesh, in_specs=in_specs, out_specs=out_specs, check_vma=False)
```

profile of v0, /device:TPU:0, one launch (start us, length us, event | category | flops | bytes accessed | tf_op | source)
XLA Modules:
  0.0 1224.5 jit_solution(4679135000949532961)
XLA Ops:
  12.0 56.4 %all-gather.18.cloned.1.call-done = bf16[768,768]{1,0:T(8,128)(2,1)} async-done(((bf16[24,768]{1,0:T(8,128)(2,1)}), bf16[768,768]{1,0:T(8,128)(2,1)}) %all-gather.18.cloned.1.call-update) | async-done | bytes 1179664 | tf_op jit(solution)/shard_map/all_gather | solution.py:133
  74.1 39.6 %all-reduce.20 = (bf16[768]{0:T(1024)(128)(2,1)S(1)}, bf16[768]{0:T(1024)(128)(2,1)S(1)}, bf16[768]{0:T(1024)(128)(2,1)S(1)}, bf16[768]{0:T(1024)(128)(2,1)S(1)}...) all-reduce(bf16[768]{0:T(1024)(128)(2,1)S(1)} %dynamic-update-slice, ...), channel_id=1, replica_groups=mesh['dp'=8,'fsdp'=2,'seq'=2] {'dp','fsdp','seq'}, use_global_device_ids=true, to_apply=%add | all-reduce | flops 9216 | bytes 36864
  113.8 11.2 all-gather.14.cloned.1.call-done
  135.5 46.2 %all-gather.22.cloned.1.call-done = bf16[768,768]{1,0:T(8,128)(2,1)} async-done(((bf16[24,768]{1,0:T(8,128)(2,1)}), bf16[768,768]{1,0:T(8,128)(2,1)}) %all-gather.22.cloned.1.call-update) | async-done | bytes 1179664 | tf_op jit(solution)/shard_map/all_gather | solution.py:131
  187.2 22.0 %all-gather.20.cloned.1.call-done = bf16[1,1024,12,64]{1,3,2,0:T(8,128)(2,1)} async-done(((bf16[1,512,12,64]{1,3,2,0:T(8,128)(2,1)}), bf16[1,1024,12,64]{1,3,2,0:T(8,128)(2,1)}) %all-gather.20.cloned.1.call-update) | async-done | bytes 1572880 | tf_op jit(solution)/shard_map/all_gather | solution.py:197
  209.2 38.7 %while.62 = (s32[]{:T(128)}, f32[1,12,512]{2,1,0:T(8,128)S(1)}, f32[1,12,512]{2,1,0:T(8,128)S(1)}, s32[1,1024]{1,0:T(1,128)S(1)}, s32[1,512]{1,0:T(1,128)S(1)}, ...) while((s32[]{:T(128)}, f32[1,12,512]{2,1,0:T(8,128)S(1)}, ...), condition=%wide.region_5.6_spmd.clone, body=%wide.region_2.5_spmd.clone.sunk | while | flops 214334208 | bytes 14486718 | solution.py:50
  209.4 5.1 fusion.201
  219.3 5.1 fusion.201
  228.9 5.1 fusion.201
  238.5 5.1 fusion.201
  248.0 56.7 %while.63 = (s32[]{:T(128)}, f32[1,512,12,64]{1,3,2,0:T(8,128)S(1)}, f32[1,512,12,64]{1,3,2,0:T(8,128)}, bf16[1,1024,12,64]{1,3,2,0:T(8,128)(2,1)}, s32[1,1024]{...) while((s32[]{:T(128)}, ...), condition=%wide.region_7.8_spmd.clone, body=%wide.region_6.7_spmd.clone.sunk | while | flops 623248128 | bytes 52751600 | solution.py:50
  248.2 5.0 fusion.207
  253.2 6.1 bitcast_add_fusion.15
  262.1 4.9 fusion.207
  267.0 6.5 bitcast_add_fusion.15
  276.4 4.9 fusion.207
  281.3 6.5 bitcast_add_fusion.15
  290.7 4.9 fusion.207
  295.6 6.5 bitcast_add_fusion.15
  308.9 52.6 %all-gather.26.cloned.1.call-done = bf16[768,3072]{1,0:T(8,128)(2,1)} async-done(((bf16[24,3072]{1,0:T(8,128)(2,1)}), bf16[768,3072]{1,0:T(8,128)(2,1)}) %all-gather.26.cloned.1.call-update) | async-done | bytes 4718608 | tf_op jit(solution)/shard_map/all_gather | solution.py:140
  361.5 32.7 %multiply_convert_fusion.4 = (bf16[512,3072]{1,0:T(8,128)(2,1)}, f32[512,3072]{1,0:T(8,128)}, f32[512,3072]{1,0:T(8,128)}) fusion(f32[3072]{0:T(1024)S(1)} %convert_element_type.238, bf16[768,3072]{1,0:T(8,128)(2,1)} %all-gather.26.cloned.1.call-done, f32[512,768]{1,0:T(8,128)} %copy-done.15, f32[768]{0:T(1024)S(1)} %convert_element_type.234, ...), kind=kOutput, calls=%fused_computation.115 | convolution fusion | flops 2521694208 | bytes 22042624 | tf_op jit(solution)/shard_map/dot_general | solution.py:34
  394.2 33.3 %all-gather.28.cloned.1.call-done = bf16[3072,768]{1,0:T(8,128)(2,1)} async-done(((bf16[96,768]{1,0:T(8,128)(2,1)}), bf16[3072,768]{1,0:T(8,128)(2,1)}) %all-gather.28.cloned.1.call-update) | async-done | bytes 4718608 | tf_op jit(solution)/shard_map/all_gather | solution.py:142
  427.5 6.5 fusion.146
  435.3 8.9 all-reduce.19
  450.6 7.9 convert_reduce_fusion
  468.1 49.3 %while.64 = (s32[]{:T(128)}, f32[1,512,12,64]{1,3,2,0:T(8,128)}, bf16[1,1024,12,64]{1,3,2,0:T(8,128)(2,1)}, s32[1,1024]{1,0:T(1,128)S(1)}, s32[1,512]{1,0:T(1,12...) while((s32[]{:T(128)}, f32[1,512,12,64]{1,3,2,0:T(8,128)}, ...), condition=%wide.region_21.22_spmd.clone, body=%wide.region_20.21_spmd.clone.sunk | while | flops 616170240 | bytes 21951216 | solution.py:50
  468.4 4.8 fusion.214
  473.1 7.5 bitcast_add_fusion.16
  480.7 4.8 fusion.214
  485.5 7.4 bitcast_add_fusion.16
  493.0 4.8 fusion.214
  497.8 7.4 bitcast_add_fusion.16
  505.3 4.8 fusion.214
  510.1 7.4 bitcast_add_fusion.16
  531.9 4.8 all-gather.1
  540.4 67.1 %while.65 = (s32[]{:T(128)}, f32[1,512,12,64]{1,3,2,0:T(8,128)}, f32[1,512,12,64]{1,3,2,0:T(8,128)S(1)}, bf16[1,1024,12,64]{1,3,2,0:T(8,128)(2,1)}, s32[1,512]{1...) while((s32[]{:T(128)}, f32[1,512,12,64]{1,3,2,0:T(8,128)}, ...), condition=%wide.region_23.24_spmd.clone, body=%wide.region_22.23_spmd.clone.sunk | while | flops 824574720 | bytes 28803812 | solution.py:50
  549.8 7.2 bitcast_add_fusion.17
  566.3 7.5 bitcast_add_fusion.17
  583.2 7.5 bitcast_add_fusion.17
  600.0 7.5 bitcast_add_fusion.17
  618.1 7.2 fusion.138
  626.4 8.2 fusion.150
  640.3 40.5 %all-reduce.18 = (f32[768]{0:T(1024)S(1)}, f32[768]{0:T(1024)S(1)}, f32[768]{0:T(1024)S(1)}, f32[768]{0:T(1024)S(1)}, f32[768]{0:T(1024)S(1)}, /*index=5*/f32[30...) all-reduce(f32[768]{0:T(1024)S(1)} %reduce_sum.250, ...), channel_id=5, replica_groups=mesh['dp'=8,'fsdp'=2,'seq'=2] {'dp','fsdp','seq'}, use_global_device_ids=true, to_apply=%region_26.27.clone | all-reduce | flops 9216 | bytes 73728
  691.9 34.0 %reduce-scatter.13.cloned.1.call-done = f32[24,768]{1,0:T(8,128)} async-done(((f32[768,768]{1,0:T(8,128)}), f32[24,768]{1,0:T(8,128)}) %reduce-scatter.13.cloned.1.call-update) | async-done | bytes 73744 | tf_op jit(solution)/shard_map/reduce_scatter | solution.py:345
  725.9 104.0 %reduce-scatter.23.cloned.1.call-done = f32[24,768]{1,0:T(8,128)} async-done(((f32[768,768]{1,0:T(8,128)}), f32[24,768]{1,0:T(8,128)}) %reduce-scatter.23.cloned.1.call-update) | async-done | bytes 73744
  829.9 104.6 %reduce-scatter.21.cloned.1.call-done = f32[24,768]{1,0:T(8,128)} async-done(((f32[768,768]{1,0:T(8,128)}), f32[24,768]{1,0:T(8,128)}) %reduce-scatter.21.cloned.1.call-update) | async-done | bytes 73744
  934.4 141.1 %reduce-scatter.15.cloned.1.call-done = f32[24,3072]{1,0:T(8,128)} async-done(((f32[768,3072]{1,0:T(8,128)}), f32[24,3072]{1,0:T(8,128)}) %reduce-scatter.15.cloned.1.call-update) | async-done | bytes 294928 | tf_op jit(solution)/shard_map/reduce_scatter | solution.py:351
  1075.5 142.0 %reduce-scatter.17.cloned.1.call-done = f32[96,768]{1,0:T(8,128)} async-done(((f32[3072,768]{1,0:T(8,128)}), f32[96,768]{1,0:T(8,128)}) %reduce-scatter.17.cloned.1.call-update) | async-done | bytes 294928 | tf_op jit(solution)/shard_map/reduce_scatter | solution.py:353
  (368 shorter events, 161.0 us)
Async XLA Ops:
  7.2 61.2 %all-gather.18.cloned.1.call-start = ((), (), s32[]{:S(2)}) async-start(), calls=%async_computation.8 | async-start | bytes 1216512 | tf_op jit(solution)/shard_map/all_gather | solution.py:133
  8.8 116.2 %all-gather.14.cloned.1.call-start = ((), (), s32[]{:S(2)}) async-start(), calls=%async_computation.6 | async-start | bytes 1216512 | tf_op jit(solution)/shard_map/all_gather | solution.py:134
  10.3 171.3 %all-gather.22.cloned.1.call-start = ((), (), s32[]{:S(2)}) async-start(), calls=%async_computation.10 | async-start | bytes 1216512 | tf_op jit(solution)/shard_map/all_gather | solution.py:131
  11.9 197.3 %all-gather.20.cloned.1.call-start = ((), (), s32[]{:S(2)}) async-start(), calls=%async_computation.9 | async-start | bytes 2359296 | tf_op jit(solution)/shard_map/all_gather | solution.py:197
  70.8 54.2 %copy-start.11 = (bf16[1,512,768]{2,1,0:T(8,128)(2,1)S(1)}, bf16[1,512,768]{2,1,0:T(8,128)(2,1)}, u32[]{:S(2)}) copy-start(bf16[1,512,768]{2,1,0:T(8,128)(2,1)} %param.28) | copy-start | bytes 2359300
  72.0 176.0 %all-gather.16.cloned.1.call-start = ((), (), s32[]{:S(2)}) async-start(), calls=%async_computation.7 | async-start | bytes 2359296 | tf_op jit(solution)/shard_map/all_gather | solution.py:198
  127.1 2.8 copy-start.33
  127.1 3.6 copy-start.50
  127.1 3.9 copy-start.38
  128.3 176.6 %all-gather.24.cloned.1.call-start = ((), (), s32[]{:S(2)}) async-start(), calls=%async_computation.11 | async-start | bytes 1216512 | tf_op jit(solution)/shard_map/all_gather | solution.py:136
  129.0 232.5 %all-gather.26.cloned.1.call-start = ((), (), s32[]{:S(2)}) async-start(), calls=%async_computation.12 | async-start | bytes 4866048 | tf_op jit(solution)/shard_map/all_gather | solution.py:140
  129.8 297.7 %all-gather.28.cloned.1.call-start = ((), (), s32[]{:S(2)}) async-start(), calls=%async_computation.13 | async-start | bytes 4866048 | tf_op jit(solution)/shard_map/all_gather | solution.py:142
  130.5 408.6 %all-gather.30.cloned.1.call-start = ((), (), s32[]{:S(2)}) async-start(), calls=%async_computation.14 | async-start | bytes 2359296 | tf_op jit(solution)/shard_map/all_gather | solution.py:296
  131.0 53.6 %copy-start.34 = (s32[1,512]{1,0:T(1,128)}, s32[1,512]{1,0:T(1,128)S(1)}, u32[]{:S(2)}) copy-start(s32[1,512]{1,0:T(1,128)S(1)} %broadcast_select_fusion) | copy-start | bytes 6148
  186.9 352.2 %all-gather.32.cloned.1.call-start = ((), (), s32[]{:S(2)}) async-start(), calls=%async_computation.15 | async-start | bytes 2359296 | tf_op jit(solution)/shard_map/all_gather | solution.py:297
  253.2 6.1 copy-start
  267.0 6.5 copy-start
  281.3 6.5 copy-start
  295.6 6.5 copy-start
  304.9 2.5 copy-start.21
  434.0 10.3 copy-start.29
  434.0 10.3 copy-start.37
  444.3 2.9 copy-start.8
  447.1 3.5 copy-start.39
  447.2 11.4 slice-start
  449.0 9.5 copy-start.30
  450.6 7.9 copy-start.16
  450.6 7.9 slice-start.1
  458.5 3.2 copy-start.51
  462.4 2.3 copy-start.40
  465.8 2.3 copy-start.1
  468.1 223.8 %reduce-scatter.19.cloned.1.call-start = ((), (), s32[]{:S(2)}) async-start(), calls=%async_computation.19 | async-start | bytes 2433024
  468.3 4.8 copy-start.10
  480.7 4.8 copy-start.10
  493.0 4.8 copy-start.10
  505.3 4.8 copy-start.10
  517.4 2.6 copy-start.12
  522.8 13.9 %copy-start.22 = (bf16[1,512,12,64]{1,3,2,0:T(8,128)(2,1)S(1)}, bf16[1,512,12,64]{1,3,2,0:T(8,128)(2,1)}, u32[]{:S(2)}) copy-start(bf16[1,512,12,64]{1,3,2,0:T(8,128)(2,1)} %copy-done.21) | copy-start | bytes 2359300
  522.8 13.9 %copy-start.26 = (bf16[512,768]{1,0:T(8,128)(2,1)S(1)}, bf16[512,768]{1,0:T(8,128)(2,1)}, u32[]{:S(2)}) copy-start(bf16[512,768]{1,0:T(8,128)(2,1)} %copy-done.25) | copy-start | bytes 2359300
  522.8 203.1 %reduce-scatter.13.cloned.1.call-start = ((), (), s32[]{:S(2)}) async-start(), calls=%async_computation.16 | async-start | bytes 2433024 | tf_op jit(solution)/shard_map/reduce_scatter | solution.py:345
  539.0 290.8 %reduce-scatter.23.cloned.1.call-start = ((), (), s32[]{:S(2)}) async-start(), calls=%async_computation.21 | async-start | bytes 2433024
  611.5 322.9 %reduce-scatter.21.cloned.1.call-start = ((), (), s32[]{:S(2)}) async-start(), calls=%async_computation.20 | async-start | bytes 2433024
  611.6 2.3 copy-start.14
  616.7 458.9 %reduce-scatter.15.cloned.1.call-start = ((), (), s32[]{:S(2)}) async-start(), calls=%async_computation.17 | async-start | bytes 9732096 | tf_op jit(solution)/shard_map/reduce_scatter | solution.py:351
  625.3 592.2 %reduce-scatter.17.cloned.1.call-start = ((), (), s32[]{:S(2)}) async-start(), calls=%async_computation.18 | async-start | bytes 9732096 | tf_op jit(solution)/shard_map/reduce_scatter | solution.py:353
  636.9 49.2 %copy-start.24 = (bf16[1,512,12,64]{1,3,2,0:T(8,128)(2,1)S(1)}, bf16[1,512,12,64]{1,3,2,0:T(8,128)(2,1)}, u32[]{:S(2)}) copy-start(bf16[1,512,12,64]{1,3,2,0:T(8,128)(2,1)} %copy-done.23) | copy-start | bytes 2359300
  686.0 2.3 copy-start.4
  686.0 2.3 copy-start.27
  (28 other events, 39.0 us)
Sparse Core Ops, SparseCore 0:
  11.5 56.8 all-gather.17
  71.9 53.0 all-gather.13
  128.5 53.1 all-gather.21
  183.1 26.1 all-gather.19
  210.6 27.1 all-gather.15
  241.2 54.1 all-gather.23
  298.9 62.5 all-gather.25
  365.0 62.4 all-gather.27
  429.0 26.7 all-gather.29
  468.2 26.0 all-gather.31
  522.9 97.8 reduce-scatter.18
  627.4 98.3 reduce-scatter.12
  731.7 98.0 reduce-scatter.22
  836.4 97.9 reduce-scatter.20
  940.7 134.7 reduce-scatter.14
  1082.9 134.6 reduce-scatter.16
where the time goes:
time: 1230 us; the launch traced here: 1220 us
  waiting for transfers between devices  748 us (61%)
  matrix products  285 us (23%)
  blocking collectives  107 us (9%)
  other arithmetic  35.5 us (3%)
  local copies, waits for them, and re-layouts  32.2 us (3%)
  between operations  15.4 us (1%)
    unnamed x19, waiting for transfers between devices  209 us
    reduce_scatter x1, waiting for transfers between devices, body(): lax.psum_scatter(grad_outer_weight, ('dp', 'fsdp', 'seq'), scatter_dimens...  142 us
    reduce_scatter x1, waiting for transfers between devices, body(): lax.psum_scatter(grad_inner_weight, ('dp', 'fsdp', 'seq'), scatter_dimens...  141 us
    dot_general x18, matrix products, product(): return jnp.dot(left, right, preferred_element_type=jnp.float32)  89.8 us
    unnamed x2, blocking collectives  80.2 us
    dot_general x16, matrix products, scores_at(): jnp.einsum('rqhd,rkhd->rhqk', query_part, key_part, preferred_element_typ...  77.8 us
    all_gather x1, waiting for transfers between devices, body(): lax.all_gather(lowered[2], ('dp', 'fsdp', 'seq'), axis=0, tiled=True)  56.4 us
    all_gather x1, waiting for transfers between devices, body(): lax.all_gather(lowered[9], ('dp', 'fsdp', 'seq'), axis=0, tiled=True)  52.6 us
  transfers between devices with their start and end apart: 16, of which 11 were waited for; matrix products, arithmetic and copies ran while one was open for 28% of the time, Pallas kernels for 0%

commit v1 on v0

--- a/solution.py
+++ b/solution.py
@@ -3,6 +3,8 @@
 import jax
 import jax.numpy as jnp
 from jax import lax
+from jax.experimental import pallas as pl
+from jax.experimental.pallas import tpu as pltpu
 from jax.sharding import PartitionSpec as P
 
 HEADS = 12
@@ -10,6 +12,10 @@
 
 
 highest = lax.Precision.HIGHEST
+DP, FSDP, SEQ = "dp", "fsdp", "seq"
+EVERY = (DP, FSDP, SEQ)
+BY_ROW, FLAT = P(EVERY, None), P(EVERY)
+ROWS = (DP, FSDP)
 
 
 def layer_norm(values, gain, shift):
@@ -128,23 +134,23 @@
         g_final,
         s_final,
     ) = (
-        lax.all_gather(lowered[0], ("dp", "fsdp", "seq"), axis=0, tiled=True),
-        lax.all_gather(lowered[1], ("dp", "fsdp", "seq"), axis=0, tiled=True),
-        lax.all_gather(lowered[2], ("dp", "fsdp", "seq"), axis=0, tiled=True),
-        lax.all_gather(lowered[3], ("dp", "fsdp", "seq"), axis=0, tiled=True),
-        lax.all_gather(lowered[4], ("dp", "fsdp", "seq"), axis=0, tiled=True),
-        lax.all_gather(lowered[5], ("dp", "fsdp", "seq"), axis=0, tiled=True),
-        lax.all_gather(lowered[6], ("dp", "fsdp", "seq"), axis=0, tiled=True),
-        lax.all_gather(lowered[7], ("dp", "fsdp", "seq"), axis=0, tiled=True),
-        lax.all_gather(lowered[8], ("dp", "fsdp", "seq"), axis=0, tiled=True),
-        lax.all_gather(lowered[9], ("dp", "fsdp", "seq"), axis=0, tiled=True),
-        lax.all_gather(lowered[10], ("dp", "fsdp", "seq"), axis=0, tiled=True),
-        lax.all_gather(lowered[11], ("dp", "fsdp", "seq"), axis=0, tiled=True),
-        lax.all_gather(lowered[12], ("dp", "fsdp", "seq"), axis=0, tiled=True),
-        lax.all_gather(lowered[13], ("dp", "fsdp", "seq"), axis=0, tiled=True),
-        lax.all_gather(lowered[14], ("dp", "fsdp", "seq"), axis=0, tiled=True),
-    )
-    own_start = lax.axis_index("seq") * shard
+        lax.all_gather(lowered[0], EVERY, axis=0, tiled=True),
+        lax.all_gather(lowered[1], EVERY, axis=0, tiled=True),
+        lax.all_gather(lowered[2], EVERY, axis=0, tiled=True),
+        lax.all_gather(lowered[3], EVERY, axis=0, tiled=True),
+        lax.all_gather(lowered[4], EVERY, axis=0, tiled=True),
+        lax.all_gather(lowered[5], EVERY, axis=0, tiled=True),
+        lax.all_gather(lowered[6], EVERY, axis=0, tiled=True),
+        lax.all_gather(lowered[7], EVERY, axis=0, tiled=True),
+        lax.all_gather(lowered[8], EVERY, axis=0, tiled=True),
+        lax.all_gather(lowered[9], EVERY, axis=0, tiled=True),
+        lax.all_gather(lowered[10], EVERY, axis=0, tiled=True),
+        lax.all_gather(lowered[11], EVERY, axis=0, tiled=True),
+        lax.all_gather(lowered[12], EVERY, axis=0, tiled=True),
+        lax.all_gather(lowered[13], EVERY, axis=0, tiled=True),
+        lax.all_gather(lowered[14], EVERY, axis=0, tiled=True),
+    )
+    own_start = lax.axis_index(SEQ) * shard
     places = own_start + jnp.arange(shard, dtype=jnp.int32)
     segment, retained, key_tag = crop_layout(crop_lengths, deleted, places)
     flat = states.reshape(rows * shard, width)
@@ -167,8 +173,8 @@
     top, total = sweep(
         scale_init,
         (
-            lax.all_gather(keys, "seq", axis=1, tiled=True),
-            lax.all_gather(key_tag, "seq", axis=1, tiled=True),
+            lax.all_gather(keys, SEQ, axis=1, tiled=True),
+            lax.all_gather(key_tag, SEQ, axis=1, tiled=True),
         ),
         inner=scale_step,
     )
@@ -194,9 +200,9 @@
     coarse, fine = sweep(
         (empty, empty),
         (
-            lax.all_gather(keys, "seq", axis=1, tiled=True),
-            lax.all_gather(values, "seq", axis=1, tiled=True),
-            lax.all_gather(key_tag, "seq", axis=1, tiled=True),
+            lax.all_gather(keys, SEQ, axis=1, tiled=True),
+            lax.all_gather(values, SEQ, axis=1, tiled=True),
+            lax.all_gather(key_tag, SEQ, axis=1, tiled=True),
         ),
         inner=mix_step,
     )
@@ -226,16 +232,16 @@
         precision=highest,
         preferred_element_type=jnp.float32,
     )
-    sums, counts = lax.psum((partial_sums, jnp.sum(member, axis=1)), "seq")
+    sums, counts = lax.psum((partial_sums, jnp.sum(member, axis=1)), SEQ)
     divisor = jnp.maximum(counts, 1.0)[..., None]
     pooled = sums / divisor
     w_query, w_key, w_value, w_out, w_inner, w_outer = (
-        lax.all_gather(lowered[0], ("dp", "fsdp", "seq"), axis=0, tiled=True),
-        lax.all_gather(lowered[2], ("dp", "fsdp", "seq"), axis=0, tiled=True),
-        lax.all_gather(lowered[3], ("dp", "fsdp", "seq"), axis=0, tiled=True),
-        lax.all_gather(lowered[5], ("dp", "fsdp", "seq"), axis=0, tiled=True),
-        lax.all_gather(lowered[9], ("dp", "fsdp", "seq"), axis=0, tiled=True),
-        lax.all_gather(lowered[11], ("dp", "fsdp", "seq"), axis=0, tiled=True),
+        lax.all_gather(lowered[0], EVERY, axis=0, tiled=True),
+        lax.all_gather(lowered[2], EVERY, axis=0, tiled=True),
+        lax.all_gather(lowered[3], EVERY, axis=0, tiled=True),
+        lax.all_gather(lowered[5], EVERY, axis=0, tiled=True),
+        lax.all_gather(lowered[9], EVERY, axis=0, tiled=True),
+        lax.all_gather(lowered[11], EVERY, axis=0, tiled=True),
     )
     result_grad = cotangent.astype(jnp.float32) + jnp.einsum(
         "rnc,rcd->rnd",
@@ -262,8 +268,8 @@
     delta = jnp.sum(mixed_grad.astype(jnp.float32) * (coarse + fine), axis=-1)
     delta_local = jnp.transpose(delta, (0, 2, 1))
     all_log, all_delta = (
-        lax.all_gather(jnp.transpose(log_total, (0, 2, 1)), "seq", axis=1, tiled=True),
-        lax.all_gather(delta, "seq", axis=1, tiled=True),
+        lax.all_gather(jnp.transpose(log_total, (0, 2, 1)), SEQ, axis=1, tiled=True),
+        lax.all_gather(delta, SEQ, axis=1, tiled=True),
     )
 
     def key_side(totals, parts, begin):
@@ -293,9 +299,9 @@
     key_grad, value_grad = sweep(
         (empty, empty),
         (
-            lax.all_gather(queries, "seq", axis=1, tiled=True),
-            lax.all_gather(mixed_grad, "seq", axis=1, tiled=True),
-            lax.all_gather(segment, "seq", axis=1, tiled=True),
+            lax.all_gather(queries, SEQ, axis=1, tiled=True),
+            lax.all_gather(mixed_grad, SEQ, axis=1, tiled=True),
+            lax.all_gather(segment, SEQ, axis=1, tiled=True),
         ),
         inner=key_side,
     )
@@ -316,9 +322,9 @@
     query_grad = sweep(
         empty,
         (
-            lax.all_gather(keys, "seq", axis=1, tiled=True),
-            lax.all_gather(values, "seq", axis=1, tiled=True),
-            lax.all_gather(key_tag, "seq", axis=1, tiled=True),
+            lax.all_gather(keys, SEQ, axis=1, tiled=True),
+            lax.all_gather(values, SEQ, axis=1, tiled=True),
+            lax.all_gather(key_tag, SEQ, axis=1, tiled=True),
         ),
         inner=query_side,
     )
@@ -337,68 +343,920 @@
         + product(value_low, w_value.T)
     ).reshape(rows, shard, width)
     summed = (
-        lax.psum_scatter(grad_query_weight, ("dp", "fsdp", "seq"), scatter_dimension=0, tiled=True),
-        lax.psum_scatter(grad_query_bias, ("dp", "fsdp", "seq"), scatter_dimension=0, tiled=True),
-        lax.psum_scatter(grad_key_weight, ("dp", "fsdp", "seq"), scatter_dimension=0, tiled=True),
-        lax.psum_scatter(grad_value_weight, ("dp", "fsdp", "seq"), scatter_dimension=0, tiled=True),
-        lax.psum_scatter(grad_value_bias, ("dp", "fsdp", "seq"), scatter_dimension=0, tiled=True),
+        lax.psum_scatter(grad_query_weight, EVERY, scatter_dimension=0, tiled=True),
+        lax.psum_scatter(grad_query_bias, EVERY, scatter_dimension=0, tiled=True),
+        lax.psum_scatter(grad_key_weight, EVERY, scatter_dimension=0, tiled=True),
+        lax.psum_scatter(grad_value_weight, EVERY, scatter_dimension=0, tiled=True),
+        lax.psum_scatter(grad_value_bias, EVERY, scatter_dimension=0, tiled=True),
         lax.psum_scatter(
-            grad_output_weight, ("dp", "fsdp", "seq"), scatter_dimension=0, tiled=True
+            grad_output_weight, EVERY, scatter_dimension=0, tiled=True
         ),
-        lax.psum_scatter(grad_output_bias, ("dp", "fsdp", "seq"), scatter_dimension=0, tiled=True),
-        lax.psum_scatter(grad_attn_gain, ("dp", "fsdp", "seq"), scatter_dimension=0, tiled=True),
-        lax.psum_scatter(grad_attn_shift, ("dp", "fsdp", "seq"), scatter_dimension=0, tiled=True),
-        lax.psum_scatter(grad_inner_weight, ("dp", "fsdp", "seq"), scatter_dimension=0, tiled=True),
-        lax.psum_scatter(grad_inner_bias, ("dp", "fsdp", "seq"), scatter_dimension=0, tiled=True),
-        lax.psum_scatter(grad_outer_weight, ("dp", "fsdp", "seq"), scatter_dimension=0, tiled=True),
-        lax.psum_scatter(grad_outer_bias, ("dp", "fsdp", "seq"), scatter_dimension=0, tiled=True),
-        lax.psum_scatter(grad_final_gain, ("dp", "fsdp", "seq"), scatter_dimension=0, tiled=True),
-        lax.psum_scatter(grad_final_shift, ("dp", "fsdp", "seq"), scatter_dimension=0, tiled=True),
+        lax.psum_scatter(grad_output_bias, EVERY, scatter_dimension=0, tiled=True),
+        lax.psum_scatter(grad_attn_gain, EVERY, scatter_dimension=0, tiled=True),
+        lax.psum_scatter(grad_attn_shift, EVERY, scatter_dimension=0, tiled=True),
+        lax.psum_scatter(grad_inner_weight, EVERY, scatter_dimension=0, tiled=True),
+        lax.psum_scatter(grad_inner_bias, EVERY, scatter_dimension=0, tiled=True),
+        lax.psum_scatter(grad_outer_weight, EVERY, scatter_dimension=0, tiled=True),
+        lax.psum_scatter(grad_outer_bias, EVERY, scatter_dimension=0, tiled=True),
+        lax.psum_scatter(grad_final_gain, EVERY, scatter_dimension=0, tiled=True),
+        lax.psum_scatter(grad_final_shift, EVERY, scatter_dimension=0, tiled=True),
     )
     return (output, pooled, states_grad) + tuple(summed)
+
+
+BF = jnp.bfloat16
+F32 = jnp.float32
+MIB = 1 << 20
+
+
+def dot(left, right, left_dim=1, right_dim=0):
+    return lax.dot_general(
+        left,
+        right,
+        (((left_dim,), (right_dim,)), ((), ())),
+        preferred_element_type=F32,
+    )
+
+
+def exact_dot(left, right, left_dim=1, right_dim=0):
+    return lax.dot_general(
+        left,
+        right,
+        (((left_dim,), (right_dim,)), ((), ())),
+        precision=highest,
+        preferred_element_type=F32,
+    )
+
+
+def crop_ends_of(lens_ref):
+    ends, total = [], jnp.int32(0)
+    for slot in range(lens_ref.shape[0]):
+        total = total + lens_ref[slot]
+        ends.append(total)
+    return ends
+
+
+def segment_of(ends, places):
+    segment = jnp.zeros(places.shape, jnp.int32)
+    for end in ends:
+        segment = segment + (places >= end).astype(jnp.int32)
+    return segment
+
+
+def window_start(ends, block):
+    middle = ends[0] * 0
+    for end in ends:
+        middle = jnp.maximum(middle, jnp.where(end <= 2 * block, end, 0))
+    return jnp.where(middle < block, 0, block)
+
+
+def pack_kernel(place, wq, wk, wv, wo, w1, w2, v24, v96, send, keep, small, p1a, p1b, p2):
+    x = place[3]
+    device = place[4]
+    half = wq.shape[1] // 2
+    for pair in range(half // 128):
+        for index, ref in enumerate((wq, wk, wv)):
+            left = ref[:, pair * 128 : pair * 128 + 128].astype(BF)
+            right = ref[:, half + pair * 128 : half + pair * 128 + 128].astype(BF)
+            begin = (pair * 3 + index) * 128
+            keep[:, begin : begin + 128] = jnp.where(x == 0, left, right)
+            send[:, begin : begin + 128] = jnp.where(x == 0, right, left)
+    width = wo.shape[1]
+    split = p1a.shape[1] - width
+    p1a[:, :width] = wo[...].astype(BF)
+    p1a[:, width:] = w1[:, :split].astype(BF)
+    p1b[...] = w1[:, split:].astype(BF)
+    p2[...] = w2[...].astype(BF)
+    part = v24.shape[1]
+    row = lax.broadcasted_iota(jnp.int32, (part, width), 0)
+    lane = lax.broadcasted_iota(jnp.int32, (part, width), 1)
+    spread = (row + device * part == lane).astype(BF)
+    first = dot(v24[...].astype(BF), spread)
+    part = v96.shape[1]
+    row = lax.broadcasted_iota(jnp.int32, (part, width), 0)
+    lane = lax.broadcasted_iota(jnp.int32, (part, width), 1)
+    rows = []
+    for index in range(8):
+        if index < v96.shape[1] * 32 // width:
+            spread = (row + device * part == lane + index * width).astype(BF)
+            rows.append(dot(v96[...].astype(BF), spread))
+    tall = lax.broadcasted_iota(jnp.int32, (8, width), 0)
+    second = jnp.zeros((8, width), F32)
+    for index, value in enumerate(rows):
+        second = jnp.where(tall == index, value[:1], second)
+    small[...] = jnp.concatenate([first, second], axis=0).astype(BF)
+
+
+def blocks_in(place, parts, store, sems, flips, first=0):
+    copies = []
+    for part, (ref, offset) in enumerate(zip(parts, flips, strict=True)):
+        for slot in range(ref.shape[0]):
+            spot = slot_place(place, offset, slot)
+            copies.append(
+                pltpu.make_async_copy(
+                    ref.at[slot], store.at[spot], sems.at[first + part * ref.shape[0] + slot]
+                )
+            )
+    return copies
+
+
+def xor(value, bits):
+    if bits & 1:
+        value = value + 1 - 2 * lax.rem(value, 2)
+    if bits & 2:
+        value = lax.rem(value + 2, 4)
+    return value
+
+
+def slot_place(place, flip, slot):
+    flip_y, flip_c, flip_x = flip
+    z = xor(place[0], slot % 4)
+    y = xor(place[1], flip_y ^ (slot // 4))
+    c = xor(place[2], flip_c)
+    spot = (z * 2 + y) * 2 + c
+    if flip_x is None:
+        return spot
+    return spot * 2 + xor(place[3], flip_x)
+
+
+PAIR_FLIPS = ((0, 0, None), (1, 0, None), (0, 1, None), (1, 1, None))
+FULL_FLIPS = ((0, 0, 0), (0, 0, 1), (0, 1, 0), (0, 1, 1))
+
+
+def tag_row(ends, x, own, other):
+    half = own.shape[1]
+    parts = []
+    for index in range(2):
+        deleted = jnp.where(x == index, own[...], other[...])
+        places = index * half + lax.broadcasted_iota(jnp.int32, (1, half), 1)
+        segment = segment_of(ends, places)
+        parts.append(jnp.where((deleted == 0) & (segment < len(ends)), segment, -1))
+    return parts
+
+
+def attend_block(ends, tags, q_ref, k_ref, v_ref, index, block, special):
+    wide = 3 * block
+    lane_low = lax.broadcasted_iota(jnp.int32, (block, 128), 1) < 64
+    key_low = lax.broadcasted_iota(jnp.int32, (wide, 128), 1) < 64
+    start = jnp.where(index <= 1, 0, jnp.where(index == 2, special, block))
+    start = pl.multiple_of(start, block)
+    begin = pl.multiple_of(index * block, block)
+    places = begin + lax.broadcasted_iota(jnp.int32, (block, 1), 0)
+    key_places = start + lax.broadcasted_iota(jnp.int32, (1, wide), 1)
+    allowed = (tags[0:1, pl.ds(start, wide)] == segment_of(ends, places)) | (key_places == places)
+    bias = jnp.where(allowed, 0.0, -1e30)
+    outs = []
+    for pair in range(q_ref.shape[1] // 128):
+        columns = slice(pair * 128, pair * 128 + 128)
+        queries = q_ref[pl.ds(begin, block), columns] * jnp.asarray(0.125, BF)
+        keys = k_ref[pl.ds(start, wide), columns]
+        values = v_ref[pl.ds(start, wide), columns]
+        total = jnp.zeros((block, 128), F32)
+        for side in range(2):
+            mine = lane_low if side == 0 else ~lane_low
+            key_mine = key_low if side == 0 else ~key_low
+            scores = dot(jnp.where(mine, queries, 0), keys, 1, 1) + bias
+            top = jnp.max(scores, axis=1, keepdims=True)
+            raised = jnp.exp(scores - top)
+            scale = 1.0 / jnp.sum(raised, axis=1, keepdims=True)
+            probs = (raised * scale).astype(BF)
+            total = total + dot(probs, jnp.where(key_mine, values, 0))
+        outs.append(total.astype(BF))
+    return jnp.concatenate(outs, axis=1)
+
+
+def attend_half(ends, tags, q_ref, k_ref, v_ref, side, out):
+    block = out.shape[0] // 2
+    special = window_start(ends, block)
+
+    def turn(step, carry):
+        spot = pl.multiple_of(step * block, block)
+        out[pl.ds(spot, block), :] = attend_block(
+            ends, tags, q_ref, k_ref, v_ref, side * 2 + step, block, special
+        )
+        return carry
+
+    lax.fori_loop(0, 2, turn, 0)
+
+
+def fill_tags(ends, x, del_own, del_other, tags):
+    half = del_own.shape[1]
+    for index, part in enumerate(tag_row(ends, x, del_own, del_other)):
+        tags[0:1, index * half : (index + 1) * half] = part
+
+
+def attend_kernel(
+    place, lens, del_own, del_other, st_own, st_other, a0, a1, a2, a3,
+    q_out, k_out, v_out, mixed, small_out,
+    store, rows, tags, sems, row_sems,
+):
+    x = place[3]
+    copies = blocks_in(place, (a0, a1, a2, a3), store, sems, PAIR_FLIPS)
+    for copy in copies:
+        copy.start()
+    own_copy = pltpu.make_async_copy(st_own, rows.at[x], row_sems.at[0])
+    other_copy = pltpu.make_async_copy(st_other, rows.at[1 - x], row_sems.at[1])
+    own_copy.start()
+    other_copy.start()
+    ends = crop_ends_of(lens)
+    half = del_own.shape[1]
+    fill_tags(ends, x, del_own, del_other, tags)
+    for copy in copies:
+        copy.wait()
+    own_copy.wait()
+    other_copy.wait()
+
+    depth = store.shape[2] // 3
+    small_out[...] = jnp.sum(store[:, 48:, :768].astype(F32), axis=0)
+    split = pl.multiple_of(x * depth, depth)
+    bias_q = small_out[0:1, pl.ds(split, depth)]
+    bias_v = small_out[1:2, pl.ds(split, depth)]
+    weight = store[:, :48, :].reshape(768, 3 * depth)
+
+    def project(index, carry):
+        begin = pl.multiple_of(index * half, half)
+        product_ = dot(rows[index], weight)
+        for pair in range(depth // 128):
+            columns = slice(pair * 128, pair * 128 + 128)
+            at = pair * 384
+            q_out[pl.ds(begin, half), columns] = (
+                product_[:, at : at + 128] + bias_q[:, columns]
+            ).astype(BF)
+            k_out[pl.ds(begin, half), columns] = product_[:, at + 128 : at + 256].astype(BF)
+            v_out[pl.ds(begin, half), columns] = (
+                product_[:, at + 256 : at + 384] + bias_v[:, columns]
+            ).astype(BF)
+        return carry
+
+    lax.fori_loop(0, 2, project, 0)
+    attend_half(ends, tags, q_out, k_out, v_out, 1 - x, mixed)
+
+
+def attend_own_kernel(place, lens, del_own, del_other, q_in, k_in, v_in, mixed, tags):
+    x = place[3]
+    ends = crop_ends_of(lens)
+    fill_tags(ends, x, del_own, del_other, tags)
+    attend_half(ends, tags, q_in, k_in, v_in, x, mixed)
+
+
+def norm_parts(values):
+    centered = values - jnp.mean(values, axis=-1, keepdims=True)
+    spread = jnp.mean(centered * centered, axis=-1, keepdims=True)
+    scale = lax.rsqrt(spread + 1e-06)
+    return centered * scale, scale
+
+
+def norm_back(grad, gain, unit, scale):
+    lifted = grad * gain
+    return scale * (
+        lifted
+        - jnp.mean(lifted, axis=-1, keepdims=True)
+        - unit * jnp.mean(lifted * unit, axis=-1, keepdims=True)
+    )
+
+
+def gelu_parts(inner):
+    phi = 0.5 * (1.0 + lax.erf(inner * 0.7071067811865476))
+    density = jnp.exp(inner * inner * -0.5) * 0.3989422804014327
+    return inner * phi, phi + inner * density
+
+
+def feed_kernel(
+    place, lens, del_own, del_other, states, mix_own, mix_other, small, cot, pool_cot,
+    p0, p1, p2, p3, r0, r1, r2, r3, f0, f1, f2, f3,
+    output, pooled, residual_out, mg_own, mg_other, small_out, active, inner_low, low, outer_low, branch_low,
+    w1, w2, slope, unit_a, scale_a, outer, grad, sems1, sems2,
+):
+    x = place[3]
+    width = states.shape[1]
+    count = states.shape[0]
+    hidden = 4 * width
+    part = width
+    flat = p0.shape[2]
+    in1 = blocks_in(place, (p0, p1, p2, p3), w1.at[:, :, :flat], sems1, PAIR_FLIPS)
+    in1 += blocks_in(place, (r0, r1, r2, r3), w1.at[:, :, flat:], sems1, PAIR_FLIPS, 16)
+    in2 = blocks_in(place, (f0, f1, f2, f3), w2, sems2, FULL_FLIPS)
+    for copy in in1 + in2:
+        copy.start()
+    ends = crop_ends_of(lens)
+    tags = tag_row(ends, x, del_own, del_other)
+    slots = lax.broadcasted_iota(jnp.int32, (len(ends), count), 0)
+    members = [(tag == slots).astype(F32) for tag in tags]
+    counts = sum(jnp.sum(member, axis=1, keepdims=True) for member in members)
+    divisor = jnp.maximum(counts, 1.0)
+    member = jnp.where(x == 0, members[0], members[1])
+    for copy in in1:
+        copy.wait()
+
+    def out_weight(side):
+        return w1[pl.ds(side * 8, 8), :, :width].reshape(width // 2, width)
+
+    branch = dot(mix_own[...], out_weight(x)) + dot(mix_other[...], out_weight(1 - x))
+    branch = branch + small[2:3, :]
+    unit, scale = norm_parts(states[...].astype(F32) + branch)
+    unit_a[...] = unit
+    scale_a[...] = scale
+    value = unit * small[3:4, :] + small[4:5, :]
+    low[...] = value.astype(BF)
+    outer[...] = value + small[5:6, :]
+    for copy in in2:
+        copy.wait()
+
+    def ahead(index, carry):
+        begin = pl.multiple_of(index * part, part)
+        weight = w1[:, :, pl.ds(width + begin, part)].reshape(width, part)
+        inner = dot(low[...], weight) + small[pl.ds(8 + index, 1), :]
+        act, bend = gelu_parts(inner)
+        act = act.astype(BF)
+        active[index] = act
+        slope[index] = bend
+        outer[...] += dot(act, w2[pl.ds(index * 8, 8)].reshape(part, width))
+        return carry
+
+    lax.fori_loop(0, hidden // part, ahead, 0)
+
+    unit, scale = norm_parts(outer[...])
+    result = unit * small[6:7, :] + small[7:8, :]
+    output[...] = result.astype(BF)
+    pooled[...] = exact_dot(member, result) / divisor
+    grad_in = cot[...].astype(F32) + exact_dot(member, pool_cot[...] / divisor, 0, 0)
+    small_out[0:2, :] = jnp.zeros((2, width), F32)
+    small_out[12:16, :] = jnp.zeros((4, width), F32)
+    small_out[6:7, :] = jnp.sum(grad_in * unit, axis=0, keepdims=True)
+    small_out[7:8, :] = jnp.sum(grad_in, axis=0, keepdims=True)
+    total = norm_back(grad_in, small[6:7, :], unit, scale)
+    grad[...] = total
+    outer_low[...] = total.astype(BF)
+    small_out[5:6, :] = jnp.sum(outer_low[...].astype(F32), axis=0, keepdims=True)
+
+    def back(index, carry):
+        begin = pl.multiple_of(index * part, part)
+        weight = w2[pl.ds(index * 8, 8)].reshape(part, width)
+        inner = (dot(outer_low[...], weight, 1, 1) * slope[index]).astype(BF)
+        inner_low[index] = inner
+        small_out[pl.ds(8 + index, 1), :] = jnp.sum(inner.astype(F32), axis=0, keepdims=True)
+        weight = w1[:, :, pl.ds(width + begin, part)].reshape(width, part)
+        grad[...] += dot(inner, weight, 1, 1)
+        return carry
+
+    lax.fori_loop(0, hidden // part, back, 0)
+
+    total = grad[...]
+    unit = unit_a[...]
+    small_out[3:4, :] = jnp.sum(total * unit, axis=0, keepdims=True)
+    small_out[4:5, :] = jnp.sum(total, axis=0, keepdims=True)
+    residual = norm_back(total, small[3:4, :], unit, scale_a[...])
+    residual_out[...] = residual
+    branch_low[...] = residual.astype(BF)
+    small_out[2:3, :] = jnp.sum(branch_low[...].astype(F32), axis=0, keepdims=True)
+    mg_own[...] = dot(branch_low[...], out_weight(x), 1, 1).astype(BF)
+    mg_other[...] = dot(branch_low[...], out_weight(1 - x), 1, 1).astype(BF)
+
+
+def outer_sum_kernel(place, active, outer_low, ka, kb, sa, sb, store, sems):
+    width = outer_low.shape[1]
+
+    def turn(index, carry):
+        product_ = dot(active[index], outer_low[...], 0, 0).astype(BF)
+        store[pl.ds(index * 8, 8)] = product_.reshape(8, width // 8, width)
+        return carry
+
+    lax.fori_loop(0, active.shape[0], turn, 0)
+    copies = blocks_out(place, (ka, kb, sa, sb), store, sems, FULL_FLIPS, 0)
+    for copy in copies:
+        copy.start()
+    for copy in copies:
+        copy.wait()
+
+
+def inner_sum_kernel(
+    place, low, inner_low, branch_low, mix_own, mix_other, ka, kb, sa, sb, store, sems
+):
+    x = place[3]
+    width = low.shape[1]
+    for side, mix in ((x, mix_own), (1 - x, mix_other)):
+        product_ = dot(mix[...], branch_low[...], 0, 0).astype(BF)
+        store[pl.ds(side * 8, 8), :, :width] = product_.reshape(8, width // 16, width)
+
+    def turn(index, carry):
+        begin = pl.multiple_of((1 + index) * width, width)
+        product_ = dot(low[...], inner_low[index], 0, 0).astype(BF)
+        store[:, :, pl.ds(begin, width)] = product_.reshape(16, width // 16, width)
+        return carry
+
+    lax.fori_loop(0, inner_low.shape[0], turn, 0)
+    copies = blocks_out(place, (ka, kb, sa, sb), store, sems, PAIR_FLIPS, 0)
+    for copy in copies:
+        copy.start()
+    for copy in copies:
+        copy.wait()
+
+
+def blocks_out(place, parts, store, sems, flips, first):
+    copies = []
+    for part, (ref, offset) in enumerate(zip(parts, flips, strict=True)):
+        for slot in range(ref.shape[0]):
+            spot = slot_place(place, offset, slot)
+            copies.append(
+                pltpu.make_async_copy(
+                    store.at[spot], ref.at[slot], sems.at[first + part * ref.shape[0] + slot]
+                )
+            )
+    return copies
+
+
+def retreat_kernel(
+    place, lens, del_own, del_other, q_in, k_in, v_in, mg_own, mg_other, low, tags, dk, dv
+):
+    x = place[3]
+    ends = crop_ends_of(lens)
+    half = del_own.shape[1]
+    for index, part in enumerate(tag_row(ends, x, del_own, del_other)):
+        tall = jnp.transpose(jnp.broadcast_to(part.astype(F32), (8, half)))
+        tags[index * half : (index + 1) * half, :] = tall[:, :1]
+    dk[...] = jnp.zeros_like(dk)
+    dv[...] = jnp.zeros_like(dv)
+    block = half // 2
+    wide = 3 * block
+    special = window_start(ends, block)
+    lane_low = lax.broadcasted_iota(jnp.int32, (block, 128), 1) < 64
+    key_low = lax.broadcasted_iota(jnp.int32, (wide, 128), 1) < 64
+
+    def turn(index, carry):
+        start = jnp.where(index <= 1, 0, jnp.where(index == 2, special, block))
+        start = pl.multiple_of(start, block)
+        begin = pl.multiple_of(index * block, block)
+        spot = pl.multiple_of(lax.rem(index, 2) * block, block)
+        places = begin + lax.broadcasted_iota(jnp.int32, (1, block), 1)
+        key_places = start + lax.broadcasted_iota(jnp.int32, (wide, 1), 0)
+        allowed = (tags[pl.ds(start, wide), :] == segment_of(ends, places).astype(F32)) | (
+            key_places == places
+        )
+        bias = jnp.where(allowed, 0.0, -1e30)
+        queries = q_in[pl.ds(begin, block), :]
+        keys = k_in[pl.ds(start, wide), :]
+        values = v_in[pl.ds(start, wide), :]
+        near = lax.div(index, 2) == x
+        grads = jnp.where(near, mg_own[pl.ds(spot, block), :], mg_other[pl.ds(spot, block), :])
+        q_total = jnp.zeros((block, 128), F32)
+        k_total = jnp.zeros((wide, 128), F32)
+        v_total = jnp.zeros((wide, 128), F32)
+        for side in range(2):
+            mine = lane_low if side == 0 else ~lane_low
+            key_mine = key_low if side == 0 else ~key_low
+            q_mine = jnp.where(mine, queries, 0)
+            g_mine = jnp.where(mine, grads, 0)
+            scores = dot(keys, q_mine * jnp.asarray(0.125, BF), 1, 1) + bias
+            top = jnp.max(scores, axis=0, keepdims=True)
+            raised = jnp.exp(scores - top)
+            probs = raised * (1.0 / jnp.sum(raised, axis=0, keepdims=True))
+            prob_grad = dot(values, g_mine, 1, 1)
+            delta = jnp.sum(probs * prob_grad, axis=0, keepdims=True)
+            score_grad = (probs * (prob_grad - delta) * 0.125).astype(BF)
+            v_total = v_total + dot(probs.astype(BF), g_mine)
+            k_total = k_total + dot(score_grad, q_mine)
+            q_total = q_total + dot(score_grad, jnp.where(key_mine, keys, 0), 0, 0)
+        low[pl.ds(begin, block), :128] = q_total.astype(BF)
+        dk[pl.ds(start, wide), :] += k_total
+        dv[pl.ds(start, wide), :] += v_total
+        return carry
+
+    lax.fori_loop(0, 4, turn, 0)
+    low[:, 128:256] = dk[...].astype(BF)
+    low[:, 256:] = dv[...].astype(BF)
+
+
+def project_sum_kernel(
+    place, st_own, st_other, low0, low1, low2, ka, kb, sa, sb, rows, store, row_sems, sems
+):
+    x = place[3]
+    row_copies = [
+        pltpu.make_async_copy(st_own, rows.at[x], row_sems.at[0]),
+        pltpu.make_async_copy(st_other, rows.at[1 - x], row_sems.at[1]),
+    ]
+    for copy in row_copies:
+        copy.start()
+    lows = (low0, low1, low2)
+    wide = low0.shape[1]
+    lane_rows = lax.broadcasted_iota(jnp.int32, (24, 128), 0)
+    extra = jnp.zeros((24, 128), F32)
+    for index, ref in enumerate(lows):
+        sums = jnp.sum(ref[...].astype(F32), axis=0, keepdims=True)
+        extra = jnp.where(lane_rows == index, sums[:, :128], extra)
+        extra = jnp.where(lane_rows == 3 + index, sums[:, 256:], extra)
+    extra = jnp.concatenate([extra, extra], axis=0).astype(BF)
+    store[:, :, 3 * wide :] = jnp.broadcast_to(extra[None], (16, 48, 128))
+    for copy in row_copies:
+        copy.wait()
+    tokens = rows[...].reshape(2 * st_own.shape[0], st_own.shape[1])
+    for index, ref in enumerate(lows):
+        columns = slice(index * wide, (index + 1) * wide)
+        store[:, :, columns] = dot(tokens, ref[...], 0, 0).astype(BF).reshape(16, 48, wide)
+    copies = blocks_out(place, (ka, kb, sa, sb), store, sems, PAIR_FLIPS, 0)
+    for copy in copies:
+        copy.start()
+    for copy in copies:
+        copy.wait()
+
+
+def states_sum_kernel(
+    place, low0, low1, low2, residual, a0, a1, a2, a3, states_out, states_send, store, sems
+):
+    x = place[3]
+    copies = blocks_in(place, (a0, a1, a2, a3), store, sems, PAIR_FLIPS)
+    for copy in copies:
+        copy.start()
+    for copy in copies:
+        copy.wait()
+    half = residual.shape[0]
+    lows = (low0, low1, low2)
+    wide = low0.shape[1]
+
+    def share(side):
+        begin = pl.multiple_of(side * half, half)
+        total = jnp.zeros(residual.shape, F32)
+        for index, ref in enumerate(lows):
+            weight = store[:, :48, index * wide : (index + 1) * wide].reshape(768, wide)
+            total = total + dot(ref[pl.ds(begin, half), :], weight, 1, 1)
+        return total
+
+    states_send[...] = share(1 - x).astype(BF)
+    states_out[...] = residual[...] + share(x)
+
+
+def swap(value, axis):
+    return lax.ppermute(value, axis, [(0, 1), (1, 0)])
+
+
+def hop(value, planes, bits):
+    return lax.ppermute(value, DP, [(i, i ^ bits) for i in range(planes)])
+
+
+def add(*terms):
+    return sum((term.astype(F32) for term in terms[1:]), terms[0].astype(F32)).astype(BF)
+
+
+def call(kernel, outs, inputs, specs, scratch, name, micros=0, grid=()):
+    return pl.pallas_call(
+        kernel,
+        out_shape=[jax.ShapeDtypeStruct(shape, kind) for shape, kind, _ in outs],
+        in_specs=[
+            pl.BlockSpec(memory_space=SPACES[key]) if isinstance(key, str) else key
+            for key in specs
+        ],
+        out_specs=[pl.BlockSpec(memory_space=SPACES[key]) for _, _, key in outs],
+        scratch_shapes=scratch,
+        grid=grid,
+        compiler_params=pltpu.CompilerParams(vmem_limit_bytes=60 * MIB),
+        cost_estimate=pl.CostEstimate(
+            flops=int(micros * 1.1e9), bytes_accessed=int(micros * 3e6), transcendentals=0
+        ),
+        name=name,
+    )(*inputs)
+
+
+SPACES = {"s": pltpu.SMEM, "v": pltpu.VMEM, "a": pl.ANY}
+
+
+def after(value, *others):
+    return lax.optimization_barrier((value,) + others)[0]
+
+
+def column(rows, index):
+    return pl.BlockSpec((rows, 128), lambda step: (0, index))
+
+
+def halves_body(
+    states, deleted, crop_lengths,
+    query_weight, query_bias, key_weight, value_weight, value_bias, output_weight, output_bias,
+    attn_gain, attn_shift, inner_weight, inner_bias, outer_weight, outer_bias, final_gain,
+    final_shift, cotangent, pool_cotangent,
+):
+    planes = 8
+    count, width = states.shape[1:]
+    half = width // 2
+    hidden = inner_weight.shape[1]
+    part = query_weight.shape[0]
+    long = outer_weight.shape[0]
+    crops = crop_lengths.shape[1]
+    tall = 3 * half
+    flat = (width + hidden) // 2
+    dma = pltpu.SemaphoreType.DMA
+    dp, c, x = lax.axis_index(DP), lax.axis_index(FSDP), lax.axis_index(SEQ)
+    device = (dp * 2 + c) * 2 + x
+    place = jnp.stack([dp // 2, dp % 2, c, x, device]).astype(jnp.int32)
+    lens = crop_lengths[0]
+    own = states[0]
+
+    v24 = jnp.stack(
+        [query_bias, value_bias, output_bias, attn_gain, attn_shift, outer_bias, final_gain, final_shift]
+    )
+    v96 = jnp.broadcast_to(inner_bias[None], (8, long))
+    send, keep, small, p1a, p1b, p2 = call(
+        pack_kernel,
+        [
+            ((part, tall), BF, "v"),
+            ((part, tall), BF, "v"),
+            ((16, width), BF, "v"),
+            ((part, flat), BF, "v"),
+            ((part, flat), BF, "v"),
+            ((long, width), BF, "v"),
+        ],
+        (place, query_weight, key_weight, value_weight, output_weight, inner_weight, outer_weight, v24, v96),
+        "svvvvvvvv",
+        [],
+        "pack",
+        2,
+    )
+
+    def pair_up(mine, theirs):
+        return jnp.where(
+            x == 0,
+            jnp.concatenate([mine, theirs], axis=0),
+            jnp.concatenate([theirs, mine], axis=0),
+        )
+
+    def along_z(block):
+        return jnp.stack(
+            [block, hop(block, planes, 2), hop(block, planes, 4), hop(block, planes, 6)]
+        )
+
+    del_other = swap(deleted, SEQ)
+    both = pair_up(keep, swap(send, SEQ))
+    tail = jnp.pad(add(small, swap(small, SEQ)), ((0, 0), (0, tall - width)))
+    both_a = jnp.concatenate([both, tail], axis=0)
+    quad_2 = along_z(p2)
+    quad_a = along_z(both_a)
+    other = swap(after(own, both_a), SEQ)
+    quad_ay = after(hop(quad_a, planes, 1), other)
+    parts_a = (quad_a, quad_ay, swap(quad_a, FSDP), swap(quad_ay, FSDP))
+    octet = jnp.concatenate([quad_2, hop(quad_2, planes, 1)], axis=0)
+    from_x = after(swap(after(p1a, both_a), SEQ), quad_a, other, del_other)
+    quad_1 = along_z(pair_up(p1a, from_x))
+    from_x = after(swap(after(p1b, both_a), SEQ), quad_1)
+    quad_b = along_z(pair_up(p1b, from_x))
+
+    marks = (place, lens, deleted, del_other)
+    queries, keys, values, mix_send, small = call(
+        attend_kernel,
+        [((2 * count, half), BF, "v")] * 3 + [((count, half), BF, "v"), ((16, width), F32, "v")],
+        marks + (after(own, octet, quad_1), other) + parts_a,
+        "ssvvaaaaaa",
+        [
+            pltpu.VMEM((16, 64, tall), BF),
+            pltpu.VMEM((2, count, width), BF),
+            pltpu.VMEM((1, 2 * count), jnp.int32),
+            dma((16,)),
+            dma((2,)),
+        ],
+        "attend",
+        0,
+    )
+    mix_other = swap(mix_send, SEQ)
+    quad_1y = after(hop(quad_1, planes, 1), mix_send)
+    (mix_own,) = call(
+        attend_own_kernel,
+        [((count, half), BF, "v")],
+        marks + (after(queries, quad_b), keys, values),
+        "ssvvvvv",
+        [pltpu.VMEM((1, 2 * count), jnp.int32)],
+        "attend_own",
+        0,
+    )
+
+    octet_x = after(swap(octet, SEQ), mix_own)
+    quad_by = after(hop(quad_b, planes, 1), mix_own)
+    parts_2 = (octet, octet_x, swap(octet, FSDP), swap(octet_x, FSDP))
+    parts_1 = (quad_1, quad_1y, swap(quad_1, FSDP), swap(quad_1y, FSDP))
+    parts_1 += (quad_b, quad_by, swap(quad_b, FSDP), swap(quad_by, FSDP))
+    four = ((hidden // width, count, width), BF, "v")
+    tokens = ((count, width), BF, "v")
+    (
+        output, pooled, residual, mg_own, mg_send, small_grad,
+        active, inner_low, low, outer_low, branch_low,
+    ) = call(
+        feed_kernel,
+        [
+            tokens,
+            ((crops, width), F32, "v"),
+            ((count, width), F32, "v"),
+            ((count, half), BF, "v"),
+            ((count, half), BF, "v"),
+            ((16, width), F32, "v"),
+            four, four, tokens, tokens, tokens,
+        ],
+        marks
+        + (own, mix_own, mix_other, small, cotangent[0], pool_cotangent[0])
+        + parts_1
+        + parts_2,
+        "ssvvvvvvvv" + "a" * 12,
+        [
+            pltpu.VMEM((16, 2 * part, width + hidden), BF),
+            pltpu.VMEM((32, long, width), BF),
+            pltpu.VMEM((hidden // width, count, width), F32),
+            pltpu.VMEM((count, width), F32),
+            pltpu.VMEM((count, 1), F32),
+            pltpu.VMEM((count, width), F32),
+            pltpu.VMEM((count, width), F32),
+            dma((32,)),
+            dma((32,)),
+        ],
+        "feed",
+        28,
+    )
+    mg_other = swap(mg_send, SEQ)
+
+    blocks_2 = ((8, long, width), BF, "a")
+    keep_2a, keep_2b, send_2a, send_2b = call(
+        outer_sum_kernel,
+        [blocks_2] * 4,
+        (place, active, outer_low),
+        "svv",
+        [pltpu.VMEM((32, long, width), BF), dma((32,))],
+        "outer_sum",
+        0,
+    )
+    blocks_1 = ((4, 2 * part, width + hidden), BF, "a")
+    keep_1a, keep_1b, send_1a, send_1b = call(
+        inner_sum_kernel,
+        [blocks_1] * 4,
+        (place, after(low, keep_2a, mg_other), inner_low, branch_low, mix_own, mix_other),
+        "svvvvv",
+        [pltpu.VMEM((16, 2 * part, width + hidden), BF), dma((16,))],
+        "inner_sum",
+        0,
+    )
+
+    t1_2 = add(keep_2b, swap(send_2b, FSDP))
+    t1_1 = add(keep_1b, swap(send_1b, FSDP))
+    smalls = small_grad + swap(small_grad, FSDP)
+
+    lows = []
+    gates = [(t1_2, t1_1, smalls)]
+    for pair in range(half // 128):
+        queries = after(queries, *gates[pair])
+        specs = [pl.BlockSpec(memory_space=pltpu.SMEM)] * 2
+        specs += [pl.BlockSpec(memory_space=pltpu.VMEM)] * 2
+        specs += [column(2 * count, pair)] * 3 + [column(count, pair)] * 2
+        (result,) = call(
+            retreat_kernel,
+            [((2 * count, 3 * 128), BF, "v")],
+            marks + (queries, keys, values, mg_own, mg_other),
+            specs,
+            [
+                pltpu.VMEM((2 * count, 1), F32),
+                pltpu.VMEM((2 * count, 128), F32),
+                pltpu.VMEM((2 * count, 128), F32),
+            ],
+            "retreat",
+            0,
+            (1,),
+        )
+        lows.append(result)
+        smalls = smalls + after(hop(smalls, planes, 1 << pair), result)
+        gates.append((result, smalls))
+
+    t0_2 = add(keep_2a, swap(send_2a, FSDP))
+    t0_1 = add(keep_1a, swap(send_1a, FSDP))
+    u_2 = add(t0_2, after(swap(t1_2, SEQ), lows[2]))
+    u_1 = add(t0_1, after(hop(t1_1, planes, 1), lows[2]))
+    lows = [after(value, u_2, u_1) for value in lows]
+    wide = tall + 128
+    keep_a, keep_b, send_a, send_b = call(
+        project_sum_kernel,
+        [((4, 2 * part, wide), BF, "a")] * 4,
+        (place, own, other) + tuple(lows),
+        "saavvv",
+        [
+            pltpu.VMEM((2, count, width), BF),
+            pltpu.VMEM((16, 2 * part, wide), BF),
+            dma((2,)),
+            dma((16,)),
+        ],
+        "project_sum",
+        0,
+    )
+    states_part, states_send = call(
+        states_sum_kernel,
+        [((count, width), F32, "v"), tokens],
+        (place,) + tuple(after(value, keep_a) for value in lows) + (residual,) + parts_a,
+        "svvvvaaaa",
+        [pltpu.VMEM((16, 64, tall), BF), dma((16,))],
+        "states_sum",
+        0,
+    )
+    states_grad = states_part + swap(states_send, SEQ).astype(F32)
+
+    def last_z(u):
+        return add(u[0], hop(u[1], planes, 2), hop(u[2], planes, 4), hop(u[3], planes, 6))
+
+    t1 = add(keep_b, swap(send_b, FSDP))
+    t0 = add(keep_a, swap(send_a, FSDP))
+    v = last_z(add(t0, hop(t1, planes, 1))).reshape(2, part, wide)
+    mine = jnp.where(x == 0, v[0], v[1])
+    theirs = swap(jnp.where(x == 0, v[1], v[0]), SEQ)
+    left = jnp.where(x == 0, mine, theirs).astype(F32)
+    right = jnp.where(x == 0, theirs, mine).astype(F32)
+
+    def gathered(index):
+        columns = [
+            side[:, (pair * 3 + index) * 128 : (pair * 3 + index + 1) * 128]
+            for side in (left, right)
+            for pair in range(half // 128)
+        ]
+        return jnp.concatenate(columns, axis=1)
+
+    grad_query_weight, grad_key_weight, grad_value_weight = (gathered(i) for i in range(3))
+    bias_grads = jnp.stack([left[:6, tall:], right[:6, tall:]]).reshape(2, 2, half)
+    bias_grads = jnp.transpose(bias_grads, (1, 0, 2)).reshape(2, width)
+
+    u1_2, u0_2 = u_2[4:], u_2[:4]
+    v = add(u0_2, hop(u1_2, planes, 1))
+    grad_outer_weight = (
+        v[0].astype(F32)
+        + hop(v[1], planes, 2).astype(F32)
+        + hop(v[2], planes, 4).astype(F32)
+        + hop(v[3], planes, 6).astype(F32)
+    )
+    v = last_z(u_1).reshape(2, part, width + hidden)
+    mine = jnp.where(x == 0, v[0], v[1])
+    theirs = swap(jnp.where(x == 0, v[1], v[0]), SEQ)
+    total = mine.astype(F32) + theirs.astype(F32)
+    grad_output_weight, grad_inner_weight = total[:, :width], total[:, width:]
+
+    smalls = smalls + swap(smalls, SEQ)
+    vectors = lax.dynamic_slice(smalls[:8], (0, device * part), (8, part))
+    bias_grads = lax.dynamic_slice(bias_grads, (0, device * part), (2, part))
+    grad_inner_bias = lax.dynamic_slice(
+        smalls[8:12].reshape(hidden), (device * long,), (long,)
+    )
+    pooled = pooled + swap(pooled, SEQ)
+    return (
+        output[None],
+        pooled[None],
+        states_grad[None],
+        grad_query_weight,
+        bias_grads[0],
+        grad_key_weight,
+        grad_value_weight,
+        bias_grads[1],
+        grad_output_weight,
+        vectors[2],
+        vectors[3],
+        vectors[4],
+        grad_inner_weight,
+        grad_inner_bias,
+        grad_outer_weight,
+        vectors[5],
+        vectors[6],
+        vectors[7],
+    )
 
 
 def solution(mesh):
     in_specs = (
-        P(("dp", "fsdp"), "seq", None),
-        P(("dp", "fsdp"), "seq"),
-        P(("dp", "fsdp"), None),
-        P(("dp", "fsdp", "seq"), None),
-        P(("dp", "fsdp", "seq")),
-        P(("dp", "fsdp", "seq"), None),
-        P(("dp", "fsdp", "seq"), None),
-        P(("dp", "fsdp", "seq")),
-        P(("dp", "fsdp", "seq"), None),
-        P(("dp", "fsdp", "seq")),
-        P(("dp", "fsdp", "seq")),
-        P(("dp", "fsdp", "seq")),
-        P(("dp", "fsdp", "seq"), None),
-        P(("dp", "fsdp", "seq")),
-        P(("dp", "fsdp", "seq"), None),
-        P(("dp", "fsdp", "seq")),
-        P(("dp", "fsdp", "seq")),
-        P(("dp", "fsdp", "seq")),
-        P(("dp", "fsdp"), "seq", None),
-        P(("dp", "fsdp"), None, None),
+        P(ROWS, SEQ, None),
+        P(ROWS, SEQ),
+        P(ROWS, None),
+        BY_ROW,
+        FLAT,
+        BY_ROW,
+        BY_ROW,
+        FLAT,
+        BY_ROW,
+        FLAT,
+        FLAT,
+        FLAT,
+        BY_ROW,
+        FLAT,
+        BY_ROW,
+        FLAT,
+        FLAT,
+        FLAT,
+        P(ROWS, SEQ, None),
+        P(ROWS, None, None),
     )
     out_specs = (
-        P(("dp", "fsdp"), "seq", None),
-        P(("dp", "fsdp"), None, None),
-        P(("dp", "fsdp"), "seq", None),
-        P(("dp", "fsdp", "seq"), None),
-        P(("dp", "fsdp", "seq")),
-        P(("dp", "fsdp", "seq"), None),
-        P(("dp", "fsdp", "seq"), None),
-        P(("dp", "fsdp", "seq")),
-        P(("dp", "fsdp", "seq"), None),
-        P(("dp", "fsdp", "seq")),
-        P(("dp", "fsdp", "seq")),
-        P(("dp", "fsdp", "seq")),
-        P(("dp", "fsdp", "seq"), None),
-        P(("dp", "fsdp", "seq")),
-        P(("dp", "fsdp", "seq"), None),
-        P(("dp", "fsdp", "seq")),
-        P(("dp", "fsdp", "seq")),
-        P(("dp", "fsdp", "seq")),
-    )
-    return jax.shard_map(body, mesh=mesh, in_specs=in_specs, out_specs=out_specs, check_vma=False)
+        P(ROWS, SEQ, None),
+        P(ROWS, None, None),
+        P(ROWS, SEQ, None),
+        BY_ROW,
+        FLAT,
+        BY_ROW,
+        BY_ROW,
+        FLAT,
+        BY_ROW,
+        FLAT,
+        FLAT,
+        FLAT,
+        BY_ROW,
+        FLAT,
+        BY_ROW,
+        FLAT,
+        FLAT,
+        FLAT,
+    )
+    shape = mesh.shape
+    halves = (shape[DP], shape[FSDP], shape[SEQ]) == (8, 2, 2)
+    chosen = halves_body if halves else body
+    return jax.shard_map(chosen, mesh=mesh, in_specs=in_specs, out_specs=out_specs, check_vma=False)

time: 1230 us -> 319 us (0.26)
  waiting for transfers between devices: 748 us -> 87.6 us
  matrix products: 285 us -> 0 us
  Pallas kernels: 0 us -> 115 us
  blocking collectives: 107 us -> 0 us
  starting transfers between devices: 1.17 us -> 79.8 us
  other arithmetic: 35.5 us -> 15.5 us
  local copies, waits for them, and re-layouts: 32.2 us -> 15.4 us
  between operations: 15.4 us -> 1.79 us
    reduce_scatter x3 -> x0, waiting for transfers between devices: 317 us -> none  [the longest x1 142 us: body(): lax.psum_scatter(grad_outer_weight, ('dp', 'fsdp', 'seq'), scatter_dimens...]
    dot_general x56 -> x0, matrix products: 285 us -> none  [the longest x18 89.8 us: product(): return jnp.dot(left, right, preferred_element_type=jnp.float32)]
    all_gather x10 -> x0, waiting for transfers between devices: 222 us -> none  [the longest x1 56.4 us: body(): lax.all_gather(lowered[2], ('dp', 'fsdp', 'seq'), axis=0, tiled=True)]
    unnamed x19 -> x0, waiting for transfers between devices: 209 us -> none
    pallas_call x0 -> x11, Pallas kernels: none -> 115 us  [call(): pl.pallas_call(kernel, out_shape=[jax.ShapeDtypeStruct(shape, kind) for s...]
    ppermute x0 -> x61, waiting for transfers between devices: none -> 87.6 us  [the longest x31 61.9 us: hop(): return lax.ppermute(value, DP, [(i, i ^ bits) for i in range(planes)])]
    unnamed x2 -> x0, blocking collectives: 80.2 us -> none
    ppermute x0 -> x61, starting transfers between devices: none -> 79.8 us  [the longest x31 58.1 us: hop(): return lax.ppermute(value, DP, [(i, i ^ bits) for i in range(planes)])]
  transfers between devices with their start and end apart: 16 -> 61, of which waited for: 11 -> 21; matrix products, arithmetic and copies ran while one was open for 28% -> 8% of each run, Pallas kernels for 0% -> 27%
where the time goes in v1:
time: 319 us; the launch traced here: 315 us
  Pallas kernels  115 us (36%)
  waiting for transfers between devices  87.6 us (27%)
  starting transfers between devices  79.8 us (25%)
  other arithmetic  15.5 us (5%)
  local copies, waits for them, and re-layouts  15.4 us (5%)
    pallas_call x11, Pallas kernels, call(): pl.pallas_call(kernel, out_shape=[jax.ShapeDtypeStruct(shape, kind) for s...  115 us
    ppermute x31, waiting for transfers between devices, hop(): return lax.ppermute(value, DP, [(i, i ^ bits) for i in range(planes)])  61.9 us
    ppermute x31, starting transfers between devices, hop(): return lax.ppermute(value, DP, [(i, i ^ bits) for i in range(planes)])  58.1 us
    ppermute x30, waiting for transfers between devices, swap(): return lax.ppermute(value, axis, [(0, 1), (1, 0)])  25.8 us
    ppermute x30, starting transfers between devices, swap(): return lax.ppermute(value, axis, [(0, 1), (1, 0)])  21.8 us
    convert_element_type x10, other arithmetic, add(): sum((term.astype(F32) for term in terms[1:]), terms[0].astype(F32))  7.23 us
  transfers between devices with their start and end apart: 61, of which 21 were waited for; matrix products, arithmetic and copies ran while one was open for 8% of the time, Pallas kernels for 27%

profile of v1, /device:TPU:0, one launch (start us, length us, event | category | flops | bytes accessed | tf_op | source)
XLA Modules:
  0.0 314.7 jit_solution(8121966564969610185)
XLA Ops:
  3.9 2.2 pack.1
  6.1 3.0 collective-permute-start.1
  9.1 2.6 collective-permute-start.2
  11.7 1.7 collective-permute-start.5
  15.3 2.2 collective-permute-done.6
  19.9 3.5 %collective-permute-start.9 = (bf16[64,1152]{1,0:T(8,128)(2,1)S(1)}, bf16[64,1152]{1,0:T(8,128)(2,1)S(1)}, u32[]{:S(2)}, u32[]{:S(2)}) collective-permute-start(bf16[64,1152]{1,0:T(8,128)(2,1)S(1)} %get-tuple-element.154), channel_id=1, source_target_pairs={{0,16},{4,20},{8,24},{12,28},{16,0},{20,4},{24,8},{28,12},{1,17},{... | collective-permute-start | bytes 442376 | tf_op jit(solution)/shard_map/ppermute | solution.py:892
  30.3 5.7 %collective-permute-done.9 = bf16[64,1152]{1,0:T(8,128)(2,1)S(1)} collective-permute-done((bf16[64,1152]{1,0:T(8,128)(2,1)S(1)}, bf16[64,1152]{1,0:T(8,128)(2,1)S(1)}, u32[]{:S(2)}, u32[]{:S(2)}) %collective-permute-start.9) | collective-permute-done | bytes 147488 | tf_op jit(solution)/shard_map/ppermute | solution.py:892
  43.3 6.9 %collective-permute-start.12 = (bf16[48,1920]{1,0:T(8,128)(2,1)S(1)}, bf16[48,1920]{1,0:T(8,128)(2,1)S(1)}, u32[]{:S(2)}, u32[]{:S(2)}) collective-permute-start(bf16[48,1920]{1,0:T(8,128)(2,1)S(1)} %maximum_select_fusion.1), channel_id=1, source_target_pairs={{0,8},{4,12},{8,0},{12,4},{16,24},{20,28},{24,16},{28,20},{1,9},{5... | collective-permute-start | bytes 552968 | tf_op jit(solution)/shard_map/ppermute | solution.py:892
  50.7 1.9 collective-permute-start.14
  53.7 6.2 %collective-permute-start.29 = (bf16[8,96,768]{2,1,0:T(8,128)(2,1)}, bf16[8,96,768]{2,1,0:T(8,128)(2,1)S(1)}, u32[]{:S(2)}, u32[]{:S(2)}) collective-permute-start(bf16[8,96,768]{2,1,0:T(8,128)(2,1)} %constant_dynamic-update-slice_fusion.f0), channel_id=1, source_target_pairs={{0,1},{1,0},{2,3},{3,2},{4,5},{5,4},{6,7},{7,6},{8,9},{9,8},{10,11... | collective-permute-start | bytes 3538952 | tf_op jit(solution)/shard_map/ppermute | solution.py:888
  60.6 1.8 collective-permute-done.14
  63.4 4.8 %collective-permute-start.19 = (bf16[48,1920]{1,0:T(8,128)(2,1)S(1)}, bf16[48,1920]{1,0:T(8,128)(2,1)S(1)}, u32[]{:S(2)}, u32[]{:S(2)}) collective-permute-start(bf16[48,1920]{1,0:T(8,128)(2,1)S(1)} %maximum_select_fusion.3), channel_id=1, source_target_pairs={{0,8},{4,12},{8,0},{12,4},{16,24},{20,28},{24,16},{28,20},{1,9},{5... | collective-permute-start | bytes 552968 | tf_op jit(solution)/shard_map/ppermute | solution.py:892
  69.2 2.5 collective-permute-done.19
  71.7 1.9 collective-permute-start.21
  73.6 8.4 %collective-permute-done.20 = bf16[48,1920]{1,0:T(8,128)(2,1)S(1)} collective-permute-done((bf16[48,1920]{1,0:T(8,128)(2,1)S(1)}, bf16[48,1920]{1,0:T(8,128)(2,1)S(1)}, u32[]{:S(2)}, u32[]{:S(2)}) %collective-permute-start.20) | collective-permute-done | bytes 184352 | tf_op jit(solution)/shard_map/ppermute | solution.py:892
  85.3 12.1 %attend.1 = (bf16[1024,384]{1,0:T(8,128)(2,1)}, bf16[1024,384]{1,0:T(8,128)(2,1)}, bf16[1024,384]{1,0:T(8,128)(2,1)}, bf16[512,384]{1,0:T(8,128)(2,1)}, f32[16,768]{1,0:T(8,128)}) custom-call(s32[5]{0:T(128)} %stack.115.place, s32[8]{0:T(128)} %bitcast.118, s32[1,512]{1,0:T(1,128)} %del_own.11, s32[1,512]{1,0:T(1,128)} %copy-done.19, ...), custom_call_target="tpu_custom_call" | custom-call | tf_op jit(solution)/shard_map/attend/pallas_call | solution.py:900
  97.4 8.1 %attend_own.1.mix_own = bf16[512,384]{1,0:T(8,128)(2,1)} custom-call(s32[5]{0:T(128)} %stack.115.place, s32[8]{0:T(128)} %bitcast.119, s32[1,512]{1,0:T(1,128)} %del_own.11, s32[1,512]{1,0:T(1,128)} %copy-done.19, bf16[1024,384]{1,0:T(8,128)(2,1)} %get-tuple-element.123.q_in, bf16[1024,384]{1,0:T(8,128)(2,1)} %get-tuple-element.95.k_in, ...), custom_call_target="tpu_custom_call" | custom-call | tf_op jit(solution)/shard_map/attend_own/pallas_call | solution.py:900
  105.9 2.4 collective-permute-start.22
  108.8 9.0 %collective-permute-done.22.mix_other = bf16[512,384]{1,0:T(8,128)(2,1)S(1)} collective-permute-done((bf16[512,384]{1,0:T(8,128)(2,1)S(1)}, bf16[512,384]{1,0:T(8,128)(2,1)S(1)}, u32[]{:S(2)}, u32[]{:S(2)}) %collective-permute-start.22) | collective-permute-done | bytes 393248 | tf_op jit(solution)/shard_map/ppermute | solution.py:888
  117.8 2.4 collective-permute-done.28.r3
  121.5 28.5 %feed.1 = (bf16[512,768]{1,0:T(8,128)(2,1)}, f32[8,768]{1,0:T(8,128)}, f32[512,768]{1,0:T(8,128)}, bf16[512,384]{1,0:T(8,128)(2,1)}, bf16[512,384]{1,0:T(8,128)(...) custom-call(s32[5]{0:T(128)} %stack.115.place, ...), custom_call_target="tpu_custom_call" | custom-call | flops 30799998976 | bytes 84000000 | tf_op jit(solution)/shard_map/feed/pallas_call | solution.py:900
  150.1 1.8 collective-permute-start.34
  151.9 7.8 %outer_sum.1 = (bf16[8,96,768]{2,1,0:T(8,128)(2,1)}, bf16[8,96,768]{2,1,0:T(8,128)(2,1)}, bf16[8,96,768]{2,1,0:T(8,128)(2,1)}, bf16[8,96,768]{2,1,0:T(8,128)(2,1)}) custom-call(s32[5]{0:T(128)} %stack.115.place, bf16[4,512,768]{2,1,0:T(8,128)(2,1)} %get-tuple-element.104.active, bf16[512,768]{1,0:T(8,128)(2,1)} %get-tuple-element.105.outer_low), custom_call_target="tpu_custom_call" | custom-call | tf_op jit(solution)/shard_map/outer_sum/pallas_call | solution.py:900
  159.8 1.7 collective-permute-done.34.mg_other
  161.5 9.6 %inner_sum.1 = (bf16[4,48,3840]{2,1,0:T(8,128)(2,1)}, bf16[4,48,3840]{2,1,0:T(8,128)(2,1)}, bf16[4,48,3840]{2,1,0:T(8,128)(2,1)}, bf16[4,48,3840]{2,1,0:T(8,128)(2,1)}) custom-call(s32[5]{0:T(128)} %stack.115.place, bf16[512,768]{1,0:T(8,128)(2,1)} %get-tuple-element.111.low, bf16[4,512,768]{2,1,0:T(8,128)(2,1)} %get-tuple-element.112.inner_low, ...), custom_call_target="tpu_custom_call" | custom-call | tf_op jit(solution)/shard_map/inner_sum/pallas_call | solution.py:900
  171.5 1.8 collective-permute-start.38
  173.8 2.4 collective-permute-done.36
  178.4 10.5 %retreat.3.low0 = bf16[1024,384]{1,0:T(8,128)(2,1)} custom-call(s32[5]{0:T(128)} %stack.115.place, s32[8]{0:T(128)} %bitcast.121, s32[1,512]{1,0:T(1,128)} %del_own.11, s32[1,512]{1,0:T(1,128)} %copy-done.19, bf16[1024,384]{1,0:T(8,128)(2,1)} %get-tuple-element.123.q_in, bf16[1024,384]{1,0:T(8,128)(2,1)} %get-tuple-element.95.k_in, ...), custom_call_target="tpu_custom_call" | custom-call | tf_op jit(solution)/shard_map/retreat/pallas_call | solution.py:900
  188.9 2.5 collective-permute-start.40
  192.0 10.3 %retreat.4.low1 = bf16[1024,384]{1,0:T(8,128)(2,1)} custom-call(s32[5]{0:T(128)} %stack.115.place, s32[8]{0:T(128)} %bitcast.122, s32[1,512]{1,0:T(1,128)} %del_own.11, s32[1,512]{1,0:T(1,128)} %copy-done.19, bf16[1024,384]{1,0:T(8,128)(2,1)} %get-tuple-element.123.q_in, bf16[1024,384]{1,0:T(8,128)(2,1)} %get-tuple-element.95.k_in, ...), custom_call_target="tpu_custom_call" | custom-call | tf_op jit(solution)/shard_map/retreat/pallas_call | solution.py:900
  202.9 10.3 %retreat.5.low2 = bf16[1024,384]{1,0:T(8,128)(2,1)} custom-call(s32[5]{0:T(128)} %stack.115.place, s32[8]{0:T(128)} %bitcast.123, s32[1,512]{1,0:T(1,128)} %del_own.11, s32[1,512]{1,0:T(1,128)} %copy-done.19, bf16[1024,384]{1,0:T(8,128)(2,1)} %get-tuple-element.123.q_in, bf16[1024,384]{1,0:T(8,128)(2,1)} %get-tuple-element.95.k_in, ...), custom_call_target="tpu_custom_call" | custom-call | tf_op jit(solution)/shard_map/retreat/pallas_call | solution.py:900
  213.3 1.7 add_convert_fusion.3
  218.0 4.9 %collective-permute-done.55 = f32[16,768]{1,0:T(8,128)S(1)} collective-permute-done((f32[16,768]{1,0:T(8,128)}, f32[16,768]{1,0:T(8,128)S(1)}, u32[]{:S(2)}, u32[]{:S(2)}) %collective-permute-start.55) | collective-permute-done | bytes 49184 | tf_op jit(solution)/shard_map/ppermute | solution.py:892
  225.2 2.7 collective-permute-done.56
  228.5 9.6 %collective-permute-done.57 = bf16[4,96,768]{2,1,0:T(8,128)(2,1)S(1)} collective-permute-done((bf16[4,96,768]{2,1,0:T(8,128)(2,1)}, bf16[4,96,768]{2,1,0:T(8,128)(2,1)S(1)}, u32[]{:S(2)}, u32[]{:S(2)}) %collective-permute-start.57) | collective-permute-done | bytes 589856 | tf_op jit(solution)/shard_map/ppermute | solution.py:892
  238.7 2.1 collective-permute-start.59
  240.9 1.9 collective-permute-start.60
  242.8 2.3 add_convert_fusion
  246.1 2.5 collective-permute-start.52
  248.5 1.9 collective-permute-start.53
  252.7 7.1 %project_sum.1 = (bf16[4,48,1280]{2,1,0:T(8,128)(2,1)}, bf16[4,48,1280]{2,1,0:T(8,128)(2,1)}, bf16[4,48,1280]{2,1,0:T(8,128)(2,1)}, bf16[4,48,1280]{2,1,0:T(8,128)(2,1)}) custom-call(s32[5]{0:T(128)} %stack.115.place, bf16[512,768]{1,0:T(8,128)(2,1)} %bitcast.99, bf16[512,768]{1,0:T(8,128)(2,1)} %copy-done.3, bf16[1024,384]{1,0:T(8,128)(2,1)} %retreat.3.low0, ...), custom_call_target="tpu_custom_call" | custom-call | tf_op jit(solution)/shard_map/project_sum/pallas_call | solution.py:900
  260.4 7.9 %states_sum.1 = (f32[512,768]{1,0:T(8,128)}, bf16[512,768]{1,0:T(8,128)(2,1)}) custom-call(s32[5]{0:T(128)} %stack.115.place, bf16[1024,384]{1,0:T(8,128)(2,1)} %retreat.3.low0, bf16[1024,384]{1,0:T(8,128)(2,1)} %retreat.4.low1, bf16[1024,384]{1,0:T(8,128)(2,1)} %retreat.5.low2, f32[512,768]{1,0:T(8,128)} %get-tuple-element.135.residual, ...), custom_call_target="tpu_custom_call" | custom-call | tf_op jit(solution)/shard_map/states_sum/pallas_call | solution.py:900
  268.4 10.3 %collective-permute-done.52 = bf16[48,3840]{1,0:T(8,128)(2,1)S(1)} collective-permute-done((bf16[48,3840]{1,0:T(8,128)(2,1)}, bf16[48,3840]{1,0:T(8,128)(2,1)S(1)}, u32[]{:S(2)}, u32[]{:S(2)}) %collective-permute-start.52) | collective-permute-done | bytes 368672 | tf_op jit(solution)/shard_map/ppermute | solution.py:892
  279.8 9.8 %collective-permute-done.46 = bf16[4,48,1280]{2,1,0:T(8,128)(2,1)S(1)} collective-permute-done((bf16[4,48,1280]{2,1,0:T(8,128)(2,1)S(1)}, bf16[4,48,1280]{2,1,0:T(8,128)(2,1)S(1)}, u32[]{:S(2)}, u32[]{:S(2)}) %collective-permute-start.46) | collective-permute-done | bytes 491552 | tf_op jit(solution)/shard_map/ppermute | solution.py:892
  289.8 8.5 %collective-permute-start.47 = (bf16[48,1280]{1,0:T(8,128)(2,1)S(1)}, bf16[48,1280]{1,0:T(8,128)(2,1)S(1)}, u32[]{:S(2)}, u32[]{:S(2)}) collective-permute-start(bf16[48,1280]{1,0:T(8,128)(2,1)S(1)} %get-tuple-element.148), channel_id=1, source_target_pairs={{0,8},{4,12},{8,0},{12,4},{16,24},{20,28},{24,16},{28,20},{1,9},{5... | collective-permute-start | bytes 368648 | tf_op jit(solution)/shard_map/ppermute | solution.py:892
  298.9 1.9 collective-permute-start.49
  302.2 6.2 %collective-permute-done.48 = bf16[48,1280]{1,0:T(8,128)(2,1)S(1)} collective-permute-done((bf16[48,1280]{1,0:T(8,128)(2,1)S(1)}, bf16[48,1280]{1,0:T(8,128)(2,1)S(1)}, u32[]{:S(2)}, u32[]{:S(2)}) %collective-permute-start.48) | collective-permute-done | bytes 122912 | tf_op jit(solution)/shard_map/ppermute | solution.py:892
  309.9 2.9 collective-permute-done.50
  (210 shorter events, 52.0 us)
Async XLA Ops:
  6.1 17.3 %collective-permute-start.1 = (bf16[96,768]{1,0:T(8,128)(2,1)}, bf16[96,768]{1,0:T(8,128)(2,1)S(1)}, u32[]{:S(2)}, u32[]{:S(2)}) collective-permute-start(bf16[96,768]{1,0:T(8,128)(2,1)} %get-tuple-element.80), channel_id=1, source_target_pairs={{0,8},{4,12},{8,0},{12,4},{16,24},{20,28},{24,16},{28,20},{1,9},{5... | collective-permute-start | bytes 442376 | tf_op jit(solution)/shard_map/ppermute | solution.py:892
  9.1 14.5 %collective-permute-start.2 = (bf16[96,768]{1,0:T(8,128)(2,1)}, bf16[96,768]{1,0:T(8,128)(2,1)S(1)}, u32[]{:S(2)}, u32[]{:S(2)}) collective-permute-start(bf16[96,768]{1,0:T(8,128)(2,1)} %get-tuple-element.80), channel_id=1, source_target_pairs={{0,16},{4,20},{8,24},{12,28},{16,0},{20,4},{24,8},{28,12},{1,17},{... | collective-permute-start | bytes 442376 | tf_op jit(solution)/shard_map/ppermute | solution.py:892
  11.7 13.2 %collective-permute-start.3 = (bf16[96,768]{1,0:T(8,128)(2,1)}, bf16[96,768]{1,0:T(8,128)(2,1)S(1)}, u32[]{:S(2)}, u32[]{:S(2)}) collective-permute-start(bf16[96,768]{1,0:T(8,128)(2,1)} %get-tuple-element.80), channel_id=1, source_target_pairs={{0,24},{4,28},{8,16},{12,20},{16,8},{20,12},{24,0},{28,4},{1,25},{... | collective-permute-start | bytes 442376 | tf_op jit(solution)/shard_map/ppermute | solution.py:892
  19.2 10.3 %collective-permute-start.8 = (bf16[64,1152]{1,0:T(8,128)(2,1)S(1)}, bf16[64,1152]{1,0:T(8,128)(2,1)S(1)}, u32[]{:S(2)}, u32[]{:S(2)}) collective-permute-start(bf16[64,1152]{1,0:T(8,128)(2,1)S(1)} %get-tuple-element.154), channel_id=1, source_target_pairs={{0,8},{4,12},{8,0},{12,4},{16,24},{20,28},{24,16},{28,20},{1,9},{5... | collective-permute-start | bytes 442376 | tf_op jit(solution)/shard_map/ppermute | solution.py:892
  19.9 16.1 %collective-permute-start.9 = (bf16[64,1152]{1,0:T(8,128)(2,1)S(1)}, bf16[64,1152]{1,0:T(8,128)(2,1)S(1)}, u32[]{:S(2)}, u32[]{:S(2)}) collective-permute-start(bf16[64,1152]{1,0:T(8,128)(2,1)S(1)} %get-tuple-element.154), channel_id=1, source_target_pairs={{0,16},{4,20},{8,24},{12,28},{16,0},{20,4},{24,8},{28,12},{1,17},{... | collective-permute-start | bytes 442376 | tf_op jit(solution)/shard_map/ppermute | solution.py:892
  23.4 14.1 %collective-permute-start.10 = (bf16[64,1152]{1,0:T(8,128)(2,1)S(1)}, bf16[64,1152]{1,0:T(8,128)(2,1)S(1)}, u32[]{:S(2)}, u32[]{:S(2)}) collective-permute-start(bf16[64,1152]{1,0:T(8,128)(2,1)S(1)} %get-tuple-element.154), channel_id=1, source_target_pairs={{0,24},{4,28},{8,16},{12,20},{16,8},{20,12},{24,0},{28,4},{1,25},{... | collective-permute-start | bytes 442376 | tf_op jit(solution)/shard_map/ppermute | solution.py:892
  23.6 19.6 %collective-permute-start.11 = (bf16[512,768]{1,0:T(8,128)(2,1)S(1)}, bf16[512,768]{1,0:T(8,128)(2,1)S(1)}, u32[]{:S(2)}, u32[]{:S(2)}) collective-permute-start(bf16[512,768]{1,0:T(8,128)(2,1)S(1)} %bitcast.100), channel_id=1, source_target_pairs={{0,1},{1,0},{2,3},{3,2},{4,5},{5,4},{6,7},{7,6},{8,9},{9,8},{10,11... | collective-permute-start | bytes 2359304 | tf_op jit(solution)/shard_map/ppermute | solution.py:888
  25.9 12.3 %collective-permute-start.4 = (bf16[4,96,768]{2,1,0:T(8,128)(2,1)S(1)}, bf16[4,96,768]{2,1,0:T(8,128)(2,1)S(1)}, u32[]{:S(2)}, u32[]{:S(2)}) collective-permute-start(bf16[4,96,768]{2,1,0:T(8,128)(2,1)S(1)} %pad_maximum_fusion.2), channel_id=1, source_target_pairs={{0,4},{4,0},{8,12},{12,8},{16,20},{20,16},{24,28},{28,24},{1,5},{5... | collective-permute-start | bytes 1769480 | tf_op jit(solution)/shard_map/ppermute | solution.py:892
  29.5 12.7 %collective-permute-start = (s32[1,512]{1,0:T(1,128)S(1)}, s32[1,512]{1,0:T(1,128)S(1)}, u32[]{:S(2)}, u32[]{:S(2)}) collective-permute-start(s32[1,512]{1,0:T(1,128)S(1)} %copy-done.18), channel_id=1, source_target_pairs={{0,1},{1,0},{2,3},{3,2},{4,5},{5,4},{6,7},{7,6},{8,9},{9,8},{10,11... | collective-permute-start | bytes 6152 | tf_op jit(solution)/shard_map/ppermute | solution.py:888
  37.5 25.8 %collective-permute-start.18 = (bf16[24,1920]{1,0:T(8,128)(2,1)S(1)}, bf16[24,1920]{1,0:T(8,128)(2,1)S(1)}, u32[]{:S(2)}, u32[]{:S(2)}) collective-permute-start(bf16[24,1920]{1,0:T(8,128)(2,1)S(1)} %copy-done.16), channel_id=1, source_target_pairs={{0,1},{1,0},{2,3},{3,2},{4,5},{5,4},{6,7},{7,6},{8,9},{9,8},{10,11... | collective-permute-start | bytes 276488 | tf_op jit(solution)/shard_map/ppermute | solution.py:888
  38.2 30.5 %collective-permute-start.15 = (bf16[4,64,1152]{2,1,0:T(8,128)(2,1)S(1)}, bf16[4,64,1152]{2,1,0:T(8,128)(2,1)S(1)}, u32[]{:S(2)}, u32[]{:S(2)}) collective-permute-start(bf16[4,64,1152]{2,1,0:T(8,128)(2,1)S(1)} %pad_maximum_fusion.3.a0), channel_id=1, source_target_pairs={{0,4},{4,0},{8,12},{12,8},{16,20},{20,16},{24,28},{28,24},{1,5},{5... | collective-permute-start | bytes 1769480 | tf_op jit(solution)/shard_map/ppermute | solution.py:892
  43.3 10.4 %collective-permute-start.12 = (bf16[48,1920]{1,0:T(8,128)(2,1)S(1)}, bf16[48,1920]{1,0:T(8,128)(2,1)S(1)}, u32[]{:S(2)}, u32[]{:S(2)}) collective-permute-start(bf16[48,1920]{1,0:T(8,128)(2,1)S(1)} %maximum_select_fusion.1), channel_id=1, source_target_pairs={{0,8},{4,12},{8,0},{12,4},{16,24},{20,28},{24,16},{28,20},{1,9},{5... | collective-permute-start | bytes 552968 | tf_op jit(solution)/shard_map/ppermute | solution.py:892
  50.2 10.4 %collective-permute-start.13 = (bf16[48,1920]{1,0:T(8,128)(2,1)S(1)}, bf16[48,1920]{1,0:T(8,128)(2,1)S(1)}, u32[]{:S(2)}, u32[]{:S(2)}) collective-permute-start(bf16[48,1920]{1,0:T(8,128)(2,1)S(1)} %maximum_select_fusion.1), channel_id=1, source_target_pairs={{0,16},{4,20},{8,24},{12,28},{16,0},{20,4},{24,8},{28,12},{1,17},{... | collective-permute-start | bytes 552968 | tf_op jit(solution)/shard_map/ppermute | solution.py:892
  50.7 11.6 %collective-permute-start.14 = (bf16[48,1920]{1,0:T(8,128)(2,1)S(1)}, bf16[48,1920]{1,0:T(8,128)(2,1)S(1)}, u32[]{:S(2)}, u32[]{:S(2)}) collective-permute-start(bf16[48,1920]{1,0:T(8,128)(2,1)S(1)} %maximum_select_fusion.1), channel_id=1, source_target_pairs={{0,24},{4,28},{8,16},{12,20},{16,8},{20,12},{24,0},{28,4},{1,25},{... | collective-permute-start | bytes 552968 | tf_op jit(solution)/shard_map/ppermute | solution.py:892
  53.7 51.8 %collective-permute-start.29 = (bf16[8,96,768]{2,1,0:T(8,128)(2,1)}, bf16[8,96,768]{2,1,0:T(8,128)(2,1)S(1)}, u32[]{:S(2)}, u32[]{:S(2)}) collective-permute-start(bf16[8,96,768]{2,1,0:T(8,128)(2,1)} %constant_dynamic-update-slice_fusion.f0), channel_id=1, source_target_pairs={{0,1},{1,0},{2,3},{3,2},{4,5},{5,4},{6,7},{7,6},{8,9},{9,8},{10,11... | collective-permute-start | bytes 3538952 | tf_op jit(solution)/shard_map/ppermute | solution.py:888
  68.2 13.8 %collective-permute-start.20 = (bf16[48,1920]{1,0:T(8,128)(2,1)S(1)}, bf16[48,1920]{1,0:T(8,128)(2,1)S(1)}, u32[]{:S(2)}, u32[]{:S(2)}) collective-permute-start(bf16[48,1920]{1,0:T(8,128)(2,1)S(1)} %maximum_select_fusion.3), channel_id=1, source_target_pairs={{0,16},{4,20},{8,24},{12,28},{16,0},{20,4},{24,8},{28,12},{1,17},{... | collective-permute-start | bytes 552968 | tf_op jit(solution)/shard_map/ppermute | solution.py:892
  68.7 15.6 %collective-permute-start.16 = (bf16[4,64,1152]{2,1,0:T(8,128)(2,1)S(1)}, bf16[4,64,1152]{2,1,0:T(8,128)(2,1)S(1)}, u32[]{:S(2)}, u32[]{:S(2)}) collective-permute-start(bf16[4,64,1152]{2,1,0:T(8,128)(2,1)S(1)} %pad_maximum_fusion.3.a0), channel_id=1, source_target_pairs={{0,2},{2,0},{1,3},{3,1},{4,6},{6,4},{5,7},{7,5},{8,10},{10,8},{9,1... | collective-permute-start | bytes 1769480 | tf_op jit(solution)/shard_map/ppermute | solution.py:888
  68.7 15.5 %collective-permute-start.17 = (bf16[4,64,1152]{2,1,0:T(8,128)(2,1)S(1)}, bf16[4,64,1152]{2,1,0:T(8,128)(2,1)S(1)}, u32[]{:S(2)}, u32[]{:S(2)}) collective-permute-start(bf16[4,64,1152]{2,1,0:T(8,128)(2,1)S(1)} %collective-permute-done.15.a1), channel_id=1, source_target_pairs={{0,2},{2,0},{1,3},{3,1},{4,6},{6,4},{5,7},{7,5},{8,10},{10,8},{9,1... | collective-permute-start | bytes 1769480 | tf_op jit(solution)/shard_map/ppermute | solution.py:888
  71.7 10.8 %collective-permute-start.21 = (bf16[48,1920]{1,0:T(8,128)(2,1)S(1)}, bf16[48,1920]{1,0:T(8,128)(2,1)S(1)}, u32[]{:S(2)}, u32[]{:S(2)}) collective-permute-start(bf16[48,1920]{1,0:T(8,128)(2,1)S(1)} %maximum_select_fusion.3), channel_id=1, source_target_pairs={{0,24},{4,28},{8,16},{12,20},{16,8},{20,12},{24,0},{28,4},{1,25},{... | collective-permute-start | bytes 552968 | tf_op jit(solution)/shard_map/ppermute | solution.py:892
  81.9 23.9 %collective-permute-start.23 = (bf16[4,48,1920]{2,1,0:T(8,128)(2,1)}, bf16[4,48,1920]{2,1,0:T(8,128)(2,1)}, u32[]{:S(2)}, u32[]{:S(2)}) collective-permute-start(bf16[4,48,1920]{2,1,0:T(8,128)(2,1)} %pad_maximum_fusion.p0), channel_id=1, source_target_pairs={{0,4},{4,0},{8,12},{12,8},{16,20},{20,16},{24,28},{28,24},{1,5},{5... | collective-permute-start | bytes 2211848 | tf_op jit(solution)/shard_map/ppermute | solution.py:892
  82.6 25.7 %collective-permute-start.26 = (bf16[4,48,1920]{2,1,0:T(8,128)(2,1)S(1)}, bf16[4,48,1920]{2,1,0:T(8,128)(2,1)}, u32[]{:S(2)}, u32[]{:S(2)}) collective-permute-start(bf16[4,48,1920]{2,1,0:T(8,128)(2,1)S(1)} %pad_maximum_fusion.1.r0), channel_id=1, source_target_pairs={{0,4},{4,0},{8,12},{12,8},{16,20},{20,16},{24,28},{28,24},{1,5},{5... | collective-permute-start | bytes 2211848 | tf_op jit(solution)/shard_map/ppermute | solution.py:892
  84.2 24.1 %collective-permute-start.24 = (bf16[4,48,1920]{2,1,0:T(8,128)(2,1)}, bf16[4,48,1920]{2,1,0:T(8,128)(2,1)}, u32[]{:S(2)}, u32[]{:S(2)}) collective-permute-start(bf16[4,48,1920]{2,1,0:T(8,128)(2,1)} %pad_maximum_fusion.p0), channel_id=1, source_target_pairs={{0,2},{2,0},{1,3},{3,1},{4,6},{6,4},{5,7},{7,5},{8,10},{10,8},{9,1... | collective-permute-start | bytes 2211848 | tf_op jit(solution)/shard_map/ppermute | solution.py:888
  84.3 33.5 %collective-permute-start.30 = (bf16[8,96,768]{2,1,0:T(8,128)(2,1)}, bf16[8,96,768]{2,1,0:T(8,128)(2,1)}, u32[]{:S(2)}, u32[]{:S(2)}) collective-permute-start(bf16[8,96,768]{2,1,0:T(8,128)(2,1)} %constant_dynamic-update-slice_fusion.f0), channel_id=1, source_target_pairs={{0,2},{2,0},{1,3},{3,1},{4,6},{6,4},{5,7},{7,5},{8,10},{10,8},{9,1... | collective-permute-start | bytes 3538952 | tf_op jit(solution)/shard_map/ppermute | solution.py:888
  105.5 14.7 %collective-permute-start.31 = (bf16[8,96,768]{2,1,0:T(8,128)(2,1)S(1)}, bf16[8,96,768]{2,1,0:T(8,128)(2,1)S(1)}, u32[]{:S(2)}, u32[]{:S(2)}) collective-permute-start(bf16[8,96,768]{2,1,0:T(8,128)(2,1)S(1)} %collective-permute-done.29.f1), channel_id=1, source_target_pairs={{0,2},{2,0},{1,3},{3,1},{4,6},{6,4},{5,7},{7,5},{8,10},{10,8},{9,1... | collective-permute-start | bytes 3538952 | tf_op jit(solution)/shard_map/ppermute | solution.py:888
  105.9 11.9 %collective-permute-start.22 = (bf16[512,384]{1,0:T(8,128)(2,1)S(1)}, bf16[512,384]{1,0:T(8,128)(2,1)S(1)}, u32[]{:S(2)}, u32[]{:S(2)}) collective-permute-start(bf16[512,384]{1,0:T(8,128)(2,1)S(1)} %copy-done.29), channel_id=1, source_target_pairs={{0,1},{1,0},{2,3},{3,2},{4,5},{5,4},{6,7},{7,6},{8,9},{9,8},{10,11... | collective-permute-start | bytes 1179656 | tf_op jit(solution)/shard_map/ppermute | solution.py:888
  150.1 11.4 %collective-permute-start.34 = (bf16[512,384]{1,0:T(8,128)(2,1)}, bf16[512,384]{1,0:T(8,128)(2,1)S(1)}, u32[]{:S(2)}, u32[]{:S(2)}) collective-permute-start(bf16[512,384]{1,0:T(8,128)(2,1)} %get-tuple-element.110), channel_id=1, source_target_pairs={{0,1},{1,0},{2,3},{3,2},{4,5},{5,4},{6,7},{7,6},{8,9},{9,8},{10,11... | collective-permute-start | bytes 1179656 | tf_op jit(solution)/shard_map/ppermute | solution.py:888
  159.7 11.5 %collective-permute-start.33 = (bf16[8,96,768]{2,1,0:T(8,128)(2,1)}, bf16[8,96,768]{2,1,0:T(8,128)(2,1)S(1)}, u32[]{:S(2)}, u32[]{:S(2)}) collective-permute-start(bf16[8,96,768]{2,1,0:T(8,128)(2,1)} %get-tuple-element.107), channel_id=1, source_target_pairs={{0,2},{2,0},{1,3},{3,1},{4,6},{6,4},{5,7},{7,5},{8,10},{10,8},{9,1... | collective-permute-start | bytes 3538952 | tf_op jit(solution)/shard_map/ppermute | solution.py:888
  171.5 41.8 %collective-permute-start.38 = (bf16[8,96,768]{2,1,0:T(8,128)(2,1)S(1)}, bf16[8,96,768]{2,1,0:T(8,128)(2,1)S(1)}, u32[]{:S(2)}, u32[]{:S(2)}) collective-permute-start(bf16[8,96,768]{2,1,0:T(8,128)(2,1)S(1)} %add_convert_fusion.5), channel_id=1, source_target_pairs={{0,1},{1,0},{2,3},{3,2},{4,5},{5,4},{6,7},{7,6},{8,9},{9,8},{10,11... | collective-permute-start | bytes 3538952 | tf_op jit(solution)/shard_map/ppermute | solution.py:888
  173.3 40.0 %collective-permute-start.37 = (bf16[8,96,768]{2,1,0:T(8,128)(2,1)}, bf16[8,96,768]{2,1,0:T(8,128)(2,1)}, u32[]{:S(2)}, u32[]{:S(2)}) collective-permute-start(bf16[8,96,768]{2,1,0:T(8,128)(2,1)} %get-tuple-element.119), channel_id=1, source_target_pairs={{0,2},{2,0},{1,3},{3,1},{4,6},{6,4},{5,7},{7,5},{8,10},{10,8},{9,1... | collective-permute-start | bytes 3538952 | tf_op jit(solution)/shard_map/ppermute | solution.py:888
  176.3 12.7 %collective-permute-start.39 = (f32[16,768]{1,0:T(8,128)S(1)}, f32[16,768]{1,0:T(8,128)S(1)}, u32[]{:S(2)}, u32[]{:S(2)}) collective-permute-start(f32[16,768]{1,0:T(8,128)S(1)} %add.111), channel_id=1, source_target_pairs={{0,4},{4,0},{8,12},{12,8},{16,20},{20,16},{24,28},{28,24},{1,5},{5... | collective-permute-start | bytes 147464 | tf_op jit(solution)/shard_map/ppermute | solution.py:892
  188.9 13.4 %collective-permute-start.40 = (f32[16,768]{1,0:T(8,128)S(1)}, f32[16,768]{1,0:T(8,128)S(1)}, u32[]{:S(2)}, u32[]{:S(2)}) collective-permute-start(f32[16,768]{1,0:T(8,128)S(1)} %add.113), channel_id=1, source_target_pairs={{0,8},{4,12},{8,0},{12,4},{16,24},{20,28},{24,16},{28,20},{1,9},{5... | collective-permute-start | bytes 147464 | tf_op jit(solution)/shard_map/ppermute | solution.py:892
  191.5 51.3 %collective-permute-start.42 = (bf16[4,48,3840]{2,1,0:T(8,128)(2,1)}, bf16[4,48,3840]{2,1,0:T(8,128)(2,1)}, u32[]{:S(2)}, u32[]{:S(2)}) collective-permute-start(bf16[4,48,3840]{2,1,0:T(8,128)(2,1)} %add_convert_fusion.2), channel_id=1, source_target_pairs={{0,4},{4,0},{8,12},{12,8},{16,20},{20,16},{24,28},{28,24},{1,5},{5... | collective-permute-start | bytes 4423688 | tf_op jit(solution)/shard_map/ppermute | solution.py:892
  192.0 50.8 %collective-permute-start.41 = (bf16[4,48,3840]{2,1,0:T(8,128)(2,1)}, bf16[4,48,3840]{2,1,0:T(8,128)(2,1)}, u32[]{:S(2)}, u32[]{:S(2)}) collective-permute-start(bf16[4,48,3840]{2,1,0:T(8,128)(2,1)} %get-tuple-element.126), channel_id=1, source_target_pairs={{0,2},{2,0},{1,3},{3,1},{4,6},{6,4},{5,7},{7,5},{8,10},{10,8},{9,1... | collective-permute-start | bytes 4423688 | tf_op jit(solution)/shard_map/ppermute | solution.py:888
  215.9 22.2 %collective-permute-start.57 = (bf16[4,96,768]{2,1,0:T(8,128)(2,1)}, bf16[4,96,768]{2,1,0:T(8,128)(2,1)S(1)}, u32[]{:S(2)}, u32[]{:S(2)}) collective-permute-start(bf16[4,96,768]{2,1,0:T(8,128)(2,1)} %slice.245), channel_id=1, source_target_pairs={{0,4},{4,0},{8,12},{12,8},{16,20},{20,16},{24,28},{28,24},{1,5},{5... | collective-permute-start | bytes 1769480 | tf_op jit(solution)/shard_map/ppermute | solution.py:892
  238.3 10.2 %collective-permute-start.58 = (bf16[96,768]{1,0:T(8,128)(2,1)S(1)}, bf16[96,768]{1,0:T(8,128)(2,1)S(1)}, u32[]{:S(2)}, u32[]{:S(2)}) collective-permute-start(bf16[96,768]{1,0:T(8,128)(2,1)S(1)} %get-tuple-element.145), channel_id=1, source_target_pairs={{0,8},{4,12},{8,0},{12,4},{16,24},{20,28},{24,16},{28,20},{1,9},{5... | collective-permute-start | bytes 442376 | tf_op jit(solution)/shard_map/ppermute | solution.py:892
  238.7 13.1 %collective-permute-start.59 = (bf16[96,768]{1,0:T(8,128)(2,1)S(1)}, bf16[96,768]{1,0:T(8,128)(2,1)S(1)}, u32[]{:S(2)}, u32[]{:S(2)}) collective-permute-start(bf16[96,768]{1,0:T(8,128)(2,1)S(1)} %get-tuple-element.147), channel_id=1, source_target_pairs={{0,16},{4,20},{8,24},{12,28},{16,0},{20,4},{24,8},{28,12},{1,17},{... | collective-permute-start | bytes 442376 | tf_op jit(solution)/shard_map/ppermute | solution.py:892
  240.9 11.0 %collective-permute-start.60 = (bf16[96,768]{1,0:T(8,128)(2,1)S(1)}, bf16[96,768]{1,0:T(8,128)(2,1)S(1)}, u32[]{:S(2)}, u32[]{:S(2)}) collective-permute-start(bf16[96,768]{1,0:T(8,128)(2,1)S(1)} %get-tuple-element.146), channel_id=1, source_target_pairs={{0,24},{4,28},{8,16},{12,20},{16,8},{20,12},{24,0},{28,4},{1,25},{... | collective-permute-start | bytes 442376 | tf_op jit(solution)/shard_map/ppermute | solution.py:892
  246.0 22.3 %collective-permute-start.51 = (bf16[48,3840]{1,0:T(8,128)(2,1)}, bf16[48,3840]{1,0:T(8,128)(2,1)S(1)}, u32[]{:S(2)}, u32[]{:S(2)}) collective-permute-start(bf16[48,3840]{1,0:T(8,128)(2,1)} %get-tuple-element.142), channel_id=1, source_target_pairs={{0,8},{4,12},{8,0},{12,4},{16,24},{20,28},{24,16},{28,20},{1,9},{5... | collective-permute-start | bytes 1105928 | tf_op jit(solution)/shard_map/ppermute | solution.py:892
  246.1 32.7 %collective-permute-start.52 = (bf16[48,3840]{1,0:T(8,128)(2,1)}, bf16[48,3840]{1,0:T(8,128)(2,1)S(1)}, u32[]{:S(2)}, u32[]{:S(2)}) collective-permute-start(bf16[48,3840]{1,0:T(8,128)(2,1)} %get-tuple-element.144), channel_id=1, source_target_pairs={{0,16},{4,20},{8,24},{12,28},{16,0},{20,4},{24,8},{28,12},{1,17},{... | collective-permute-start | bytes 1105928 | tf_op jit(solution)/shard_map/ppermute | solution.py:892
  248.5 30.2 %collective-permute-start.53 = (bf16[48,3840]{1,0:T(8,128)(2,1)S(1)}, bf16[48,3840]{1,0:T(8,128)(2,1)S(1)}, u32[]{:S(2)}, u32[]{:S(2)}) collective-permute-start(bf16[48,3840]{1,0:T(8,128)(2,1)S(1)} %get-tuple-element.143), channel_id=1, source_target_pairs={{0,24},{4,28},{8,16},{12,20},{16,8},{20,12},{24,0},{28,4},{1,25},{... | collective-permute-start | bytes 1105928 | tf_op jit(solution)/shard_map/ppermute | solution.py:892
  259.8 19.2 %collective-permute-start.45 = (bf16[4,48,1280]{2,1,0:T(8,128)(2,1)}, bf16[4,48,1280]{2,1,0:T(8,128)(2,1)S(1)}, u32[]{:S(2)}, u32[]{:S(2)}) collective-permute-start(bf16[4,48,1280]{2,1,0:T(8,128)(2,1)} %get-tuple-element.140), channel_id=1, source_target_pairs={{0,2},{2,0},{1,3},{3,1},{4,6},{6,4},{5,7},{7,5},{8,10},{10,8},{9,1... | collective-permute-start | bytes 1474568 | tf_op jit(solution)/shard_map/ppermute | solution.py:888
  259.9 19.9 %collective-permute-start.44 = (bf16[4,48,1280]{2,1,0:T(8,128)(2,1)}, bf16[4,48,1280]{2,1,0:T(8,128)(2,1)S(1)}, u32[]{:S(2)}, u32[]{:S(2)}) collective-permute-start(bf16[4,48,1280]{2,1,0:T(8,128)(2,1)} %get-tuple-element.138), channel_id=1, source_target_pairs={{0,2},{2,0},{1,3},{3,1},{4,6},{6,4},{5,7},{7,5},{8,10},{10,8},{9,1... | collective-permute-start | bytes 1474568 | tf_op jit(solution)/shard_map/ppermute | solution.py:888
  268.3 40.3 %collective-permute-start.43 = (bf16[512,768]{1,0:T(8,128)(2,1)}, bf16[512,768]{1,0:T(8,128)(2,1)S(1)}, u32[]{:S(2)}, u32[]{:S(2)}) collective-permute-start(bf16[512,768]{1,0:T(8,128)(2,1)} %get-tuple-element.137), channel_id=1, source_target_pairs={{0,1},{1,0},{2,3},{3,2},{4,5},{5,4},{6,7},{7,6},{8,9},{9,8},{10,11... | collective-permute-start | bytes 2359304 | tf_op jit(solution)/shard_map/ppermute | solution.py:888
  279.1 10.5 %collective-permute-start.46 = (bf16[4,48,1280]{2,1,0:T(8,128)(2,1)S(1)}, bf16[4,48,1280]{2,1,0:T(8,128)(2,1)S(1)}, u32[]{:S(2)}, u32[]{:S(2)}) collective-permute-start(bf16[4,48,1280]{2,1,0:T(8,128)(2,1)S(1)} %add_convert_fusion.8), channel_id=1, source_target_pairs={{0,4},{4,0},{8,12},{12,8},{16,20},{20,16},{24,28},{28,24},{1,5},{5... | collective-permute-start | bytes 1474568 | tf_op jit(solution)/shard_map/ppermute | solution.py:892
  279.7 21.1 %collective-permute-start.54 = (bf16[24,3840]{1,0:T(8,128)(2,1)S(1)}, bf16[24,3840]{1,0:T(8,128)(2,1)S(1)}, u32[]{:S(2)}, u32[]{:S(2)}) collective-permute-start(bf16[24,3840]{1,0:T(8,128)(2,1)S(1)} %broadcast_select_fusion), channel_id=1, source_target_pairs={{0,1},{1,0},{2,3},{3,2},{4,5},{5,4},{6,7},{7,6},{8,9},{9,8},{10,11... | collective-permute-start | bytes 552968 | tf_op jit(solution)/shard_map/ppermute | solution.py:888
  289.8 12.4 %collective-permute-start.47 = (bf16[48,1280]{1,0:T(8,128)(2,1)S(1)}, bf16[48,1280]{1,0:T(8,128)(2,1)S(1)}, u32[]{:S(2)}, u32[]{:S(2)}) collective-permute-start(bf16[48,1280]{1,0:T(8,128)(2,1)S(1)} %get-tuple-element.148), channel_id=1, source_target_pairs={{0,8},{4,12},{8,0},{12,4},{16,24},{20,28},{24,16},{28,20},{1,9},{5... | collective-permute-start | bytes 368648 | tf_op jit(solution)/shard_map/ppermute | solution.py:892
  298.3 10.1 %collective-permute-start.48 = (bf16[48,1280]{1,0:T(8,128)(2,1)S(1)}, bf16[48,1280]{1,0:T(8,128)(2,1)S(1)}, u32[]{:S(2)}, u32[]{:S(2)}) collective-permute-start(bf16[48,1280]{1,0:T(8,128)(2,1)S(1)} %get-tuple-element.150), channel_id=1, source_target_pairs={{0,16},{4,20},{8,24},{12,28},{16,0},{20,4},{24,8},{28,12},{1,17},{... | collective-permute-start | bytes 368648 | tf_op jit(solution)/shard_map/ppermute | solution.py:892
  298.9 9.5 %collective-permute-start.49 = (bf16[48,1280]{1,0:T(8,128)(2,1)S(1)}, bf16[48,1280]{1,0:T(8,128)(2,1)S(1)}, u32[]{:S(2)}, u32[]{:S(2)}) collective-permute-start(bf16[48,1280]{1,0:T(8,128)(2,1)S(1)} %get-tuple-element.149), channel_id=1, source_target_pairs={{0,24},{4,28},{8,16},{12,20},{16,8},{20,12},{24,0},{28,4},{1,25},{... | collective-permute-start | bytes 368648 | tf_op jit(solution)/shard_map/ppermute | solution.py:892
  (43 other events, 450.8 us)

commit v2 on v1

--- a/solution.py
+++ b/solution.py
@@ -410,7 +410,10 @@
     return jnp.where(middle < block, 0, block)
 
 
-def pack_kernel(place, wq, wk, wv, wo, w1, w2, v24, v96, send, keep, small, p1a, p1b, p2):
+def pack_kernel(
+    place, wq, wk, wv, wo, w1, w2, v0, v1, v2, v3, v4, v5, v6, v7, v96,
+    send, keep, small, p1, p2,
+):
     x = place[3]
     device = place[4]
     half = wq.shape[1] // 2
@@ -422,16 +425,20 @@
             keep[:, begin : begin + 128] = jnp.where(x == 0, left, right)
             send[:, begin : begin + 128] = jnp.where(x == 0, right, left)
     width = wo.shape[1]
-    split = p1a.shape[1] - width
-    p1a[:, :width] = wo[...].astype(BF)
-    p1a[:, width:] = w1[:, :split].astype(BF)
-    p1b[...] = w1[:, split:].astype(BF)
+    tall = keep.shape[1]
+    for ref, begin in ((send, tall), (p1, 0)):
+        ref[:, begin : begin + width] = wo[...].astype(BF)
+        ref[:, begin + width :] = w1[...].astype(BF)
     p2[...] = w2[...].astype(BF)
-    part = v24.shape[1]
+    part = v0.shape[1]
+    row = lax.broadcasted_iota(jnp.int32, (8, part), 0)
+    stacked = jnp.zeros((8, part), F32)
+    for index, ref in enumerate((v0, v1, v2, v3, v4, v5, v6, v7)):
+        stacked = jnp.where(row == index, ref[...], stacked)
     row = lax.broadcasted_iota(jnp.int32, (part, width), 0)
     lane = lax.broadcasted_iota(jnp.int32, (part, width), 1)
     spread = (row + device * part == lane).astype(BF)
-    first = dot(v24[...].astype(BF), spread)
+    first = dot(stacked.astype(BF), spread)
     part = v96.shape[1]
     row = lax.broadcasted_iota(jnp.int32, (part, width), 0)
     lane = lax.broadcasted_iota(jnp.int32, (part, width), 1)
@@ -439,7 +446,7 @@
     for index in range(8):
         if index < v96.shape[1] * 32 // width:
             spread = (row + device * part == lane + index * width).astype(BF)
-            rows.append(dot(v96[...].astype(BF), spread))
+            rows.append(dot(jnp.broadcast_to(v96[...], (8, part)).astype(BF), spread))
     tall = lax.broadcasted_iota(jnp.int32, (8, width), 0)
     second = jnp.zeros((8, width), F32)
     for index, value in enumerate(rows):
@@ -506,6 +513,8 @@
     allowed = (tags[0:1, pl.ds(start, wide)] == segment_of(ends, places)) | (key_places == places)
     bias = jnp.where(allowed, 0.0, -1e30)
     outs = []
+    lanes = lax.broadcasted_iota(jnp.int32, (block, 128), 1)
+    logs = jnp.zeros((block, 128), F32)
     for pair in range(q_ref.shape[1] // 128):
         columns = slice(pair * 128, pair * 128 + 128)
         queries = q_ref[pl.ds(begin, block), columns] * jnp.asarray(0.125, BF)
@@ -518,22 +527,25 @@
             scores = dot(jnp.where(mine, queries, 0), keys, 1, 1) + bias
             top = jnp.max(scores, axis=1, keepdims=True)
             raised = jnp.exp(scores - top)
-            scale = 1.0 / jnp.sum(raised, axis=1, keepdims=True)
-            probs = (raised * scale).astype(BF)
+            amount = jnp.sum(raised, axis=1, keepdims=True)
+            probs = (raised * (1.0 / amount)).astype(BF)
             total = total + dot(probs, jnp.where(key_mine, values, 0))
+            logs = jnp.where(lanes == pair * 2 + side, top + jnp.log(amount), logs)
         outs.append(total.astype(BF))
-    return jnp.concatenate(outs, axis=1)
-
-
-def attend_half(ends, tags, q_ref, k_ref, v_ref, side, out):
+    return jnp.concatenate(outs, axis=1), jnp.transpose(logs)[:8]
+
+
+def attend_half(ends, tags, q_ref, k_ref, v_ref, side, out, logs):
     block = out.shape[0] // 2
     special = window_start(ends, block)
 
     def turn(step, carry):
         spot = pl.multiple_of(step * block, block)
-        out[pl.ds(spot, block), :] = attend_block(
+        mixed, rows = attend_block(
             ends, tags, q_ref, k_ref, v_ref, side * 2 + step, block, special
         )
+        out[pl.ds(spot, block), :] = mixed
+        logs[:, pl.ds(spot, block)] = rows
         return carry
 
     lax.fori_loop(0, 2, turn, 0)
@@ -547,7 +559,7 @@
 
 def attend_kernel(
     place, lens, del_own, del_other, st_own, st_other, a0, a1, a2, a3,
-    q_out, k_out, v_out, mixed, small_out,
+    q_out, k_out, v_out, mixed, logs, small_out,
     store, rows, tags, sems, row_sems,
 ):
     x = place[3]
@@ -589,14 +601,14 @@
         return carry
 
     lax.fori_loop(0, 2, project, 0)
-    attend_half(ends, tags, q_out, k_out, v_out, 1 - x, mixed)
-
-
-def attend_own_kernel(place, lens, del_own, del_other, q_in, k_in, v_in, mixed, tags):
+    attend_half(ends, tags, q_out, k_out, v_out, 1 - x, mixed, logs)
+
+
+def attend_own_kernel(place, lens, del_own, del_other, q_in, k_in, v_in, mixed, logs, tags):
     x = place[3]
     ends = crop_ends_of(lens)
     fill_tags(ends, x, del_own, del_other, tags)
-    attend_half(ends, tags, q_in, k_in, v_in, x, mixed)
+    attend_half(ends, tags, q_in, k_in, v_in, x, mixed, logs)
 
 
 def norm_parts(values):
@@ -714,40 +726,66 @@
 
 
 def outer_sum_kernel(place, active, outer_low, ka, kb, sa, sb, store, sems):
+    step = pl.program_id(0)
     width = outer_low.shape[1]
-
-    def turn(index, carry):
-        product_ = dot(active[index], outer_low[...], 0, 0).astype(BF)
-        store[pl.ds(index * 8, 8)] = product_.reshape(8, width // 8, width)
-        return carry
-
-    lax.fori_loop(0, active.shape[0], turn, 0)
-    copies = blocks_out(place, (ka, kb, sa, sb), store, sems, FULL_FLIPS, 0)
-    for copy in copies:
-        copy.start()
-    for copy in copies:
-        copy.wait()
+    product_ = dot(active[0], outer_low[...], 0, 0).astype(BF)
+    store[pl.ds(step * 8, 8)] = product_.reshape(8, width // 8, width)
+    slot = lax.bitwise_xor(step, place[0])
+    refs = (ka, kb, sa, sb)
+
+    def copy(part, flip_y, spot, at, sem):
+        return pltpu.make_async_copy(store.at[spot], refs[part].at[flip_y * 4 + at], sems.at[sem])
+
+    for part in range(4):
+        for flip_y in range(2):
+            y = xor(place[1], flip_y)
+            c = xor(place[2], part // 2)
+            x = xor(place[3], part % 2)
+            spot = ((step * 2 + y) * 2 + c) * 2 + x
+            copy(part, flip_y, spot, slot, step * 8 + part * 2 + flip_y).start()
+
+    @pl.when(step == 3)
+    def _():
+        for index in range(32):
+            copy(0, 0, index, 0, index).wait()
 
 
 def inner_sum_kernel(
-    place, low, inner_low, branch_low, mix_own, mix_other, ka, kb, sa, sb, store, sems
+    place, low, inner_low, branch_low, mix_own, mix_other,
+    ka, kb, sa, sb, la, lb, ta, tb, store, low_t, sems,
 ):
     x = place[3]
     width = low.shape[1]
+    copies = []
+
+    def send(chunk):
+        begin = chunk * width
+        refs = (ka, kb, sa, sb)
+        into = begin
+        if begin >= ka.shape[2]:
+            refs = (la, lb, ta, tb)
+            into = begin - ka.shape[2]
+        for part, flip in enumerate(PAIR_FLIPS):
+            for slot in range(4):
+                spot = slot_place(place, flip, slot)
+                copy = pltpu.make_async_copy(
+                    store.at[spot, :, begin : begin + width],
+                    refs[part].at[slot, :, into : into + width],
+                    sems.at[chunk * 16 + part * 4 + slot],
+                )
+                copy.start()
+                copies.append(copy)
+
+    low_t[...] = jnp.transpose(low[...])
     for side, mix in ((x, mix_own), (1 - x, mix_other)):
         product_ = dot(mix[...], branch_low[...], 0, 0).astype(BF)
         store[pl.ds(side * 8, 8), :, :width] = product_.reshape(8, width // 16, width)
-
-    def turn(index, carry):
-        begin = pl.multiple_of((1 + index) * width, width)
-        product_ = dot(low[...], inner_low[index], 0, 0).astype(BF)
-        store[:, :, pl.ds(begin, width)] = product_.reshape(16, width // 16, width)
-        return carry
-
-    lax.fori_loop(0, inner_low.shape[0], turn, 0)
-    copies = blocks_out(place, (ka, kb, sa, sb), store, sems, PAIR_FLIPS, 0)
-    for copy in copies:
-        copy.start()
+    send(0)
+    for index in range(inner_low.shape[0]):
+        begin = (1 + index) * width
+        product_ = dot(low_t[...], inner_low[index]).astype(BF)
+        store[:, :, begin : begin + width] = product_.reshape(16, width // 16, width)
+        send(1 + index)
     for copy in copies:
         copy.wait()
 
@@ -766,11 +804,13 @@
 
 
 def retreat_kernel(
-    place, lens, del_own, del_other, q_in, k_in, v_in, mg_own, mg_other, low, tags, dk, dv
+    place, lens, del_own, del_other, q_in, k_in, v_in, mg_own, mg_other, mix_own, mix_other,
+    log_own, log_other, low, tags, dk, dv, *, pair,
 ):
     x = place[3]
     ends = crop_ends_of(lens)
     half = del_own.shape[1]
+
     for index, part in enumerate(tag_row(ends, x, del_own, del_other)):
         tall = jnp.transpose(jnp.broadcast_to(part.astype(F32), (8, half)))
         tags[index * half : (index + 1) * half, :] = tall[:, :1]
@@ -781,6 +821,9 @@
     special = window_start(ends, block)
     lane_low = lax.broadcasted_iota(jnp.int32, (block, 128), 1) < 64
     key_low = lax.broadcasted_iota(jnp.int32, (wide, 128), 1) < 64
+    heads = lax.div(lax.broadcasted_iota(jnp.int32, (8, 128), 1), 64)
+    picks = (heads == lax.broadcasted_iota(jnp.int32, (8, 128), 0)).astype(F32)
+    eighth = jnp.asarray(0.125, BF)
 
     def turn(index, carry):
         start = jnp.where(index <= 1, 0, jnp.where(index == 2, special, block))
@@ -793,11 +836,14 @@
             key_places == places
         )
         bias = jnp.where(allowed, 0.0, -1e30)
-        queries = q_in[pl.ds(begin, block), :]
+        queries = q_in[pl.ds(begin, block), :] * eighth
         keys = k_in[pl.ds(start, wide), :]
         values = v_in[pl.ds(start, wide), :]
         near = lax.div(index, 2) == x
-        grads = jnp.where(near, mg_own[pl.ds(spot, block), :], mg_other[pl.ds(spot, block), :])
+        rows = pl.ds(spot, block)
+        grads = jnp.where(near, mg_own[rows, :], mg_other[rows, :])
+        mixed = jnp.where(near, mix_own[rows, :], mix_other[rows, :])
+        deltas = exact_dot(picks, grads.astype(F32) * mixed.astype(F32), 1, 1)
         q_total = jnp.zeros((block, 128), F32)
         k_total = jnp.zeros((wide, 128), F32)
         v_total = jnp.zeros((wide, 128), F32)
@@ -806,16 +852,14 @@
             key_mine = key_low if side == 0 else ~key_low
             q_mine = jnp.where(mine, queries, 0)
             g_mine = jnp.where(mine, grads, 0)
-            scores = dot(keys, q_mine * jnp.asarray(0.125, BF), 1, 1) + bias
-            top = jnp.max(scores, axis=0, keepdims=True)
-            raised = jnp.exp(scores - top)
-            probs = raised * (1.0 / jnp.sum(raised, axis=0, keepdims=True))
-            prob_grad = dot(values, g_mine, 1, 1)
-            delta = jnp.sum(probs * prob_grad, axis=0, keepdims=True)
-            score_grad = (probs * (prob_grad - delta) * 0.125).astype(BF)
+            row = slice(pair * 2 + side, pair * 2 + side + 1)
+            log = jnp.where(near, log_own[row, rows], log_other[row, rows])
+            probs = jnp.exp(dot(keys, q_mine, 1, 1) + (bias - log))
+            prob_grad = dot(values, g_mine, 1, 1) - deltas[side : side + 1, :]
+            score_grad = (probs * prob_grad).astype(BF)
             v_total = v_total + dot(probs.astype(BF), g_mine)
             k_total = k_total + dot(score_grad, q_mine)
-            q_total = q_total + dot(score_grad, jnp.where(key_mine, keys, 0), 0, 0)
+            q_total = q_total + dot(score_grad, jnp.where(key_mine, keys * eighth, 0), 0, 0)
         low[pl.ds(begin, block), :128] = q_total.astype(BF)
         dk[pl.ds(start, wide), :] += k_total
         dv[pl.ds(start, wide), :] += v_total
@@ -827,7 +871,7 @@
 
 
 def project_sum_kernel(
-    place, st_own, st_other, low0, low1, low2, ka, kb, sa, sb, rows, store, row_sems, sems
+    place, st_own, st_other, low0, low1, low2, ka, kb, sa, sb, rows, store, rows_t, row_sems, sems
 ):
     x = place[3]
     row_copies = [
@@ -840,18 +884,19 @@
     wide = low0.shape[1]
     lane_rows = lax.broadcasted_iota(jnp.int32, (24, 128), 0)
     extra = jnp.zeros((24, 128), F32)
-    for index, ref in enumerate(lows):
-        sums = jnp.sum(ref[...].astype(F32), axis=0, keepdims=True)
-        extra = jnp.where(lane_rows == index, sums[:, :128], extra)
-        extra = jnp.where(lane_rows == 3 + index, sums[:, 256:], extra)
+    for index, low in enumerate(lows):
+        for kind in range(2):
+            begin = kind * 256
+            sums = jnp.sum(low[:, begin : begin + 128].astype(F32), axis=0, keepdims=True)
+            extra = jnp.where(lane_rows == kind * 3 + index, sums, extra)
     extra = jnp.concatenate([extra, extra], axis=0).astype(BF)
     store[:, :, 3 * wide :] = jnp.broadcast_to(extra[None], (16, 48, 128))
     for copy in row_copies:
         copy.wait()
-    tokens = rows[...].reshape(2 * st_own.shape[0], st_own.shape[1])
-    for index, ref in enumerate(lows):
+    rows_t[...] = jnp.transpose(rows[...].reshape(2 * st_own.shape[0], st_own.shape[1]))
+    for index, low in enumerate(lows):
         columns = slice(index * wide, (index + 1) * wide)
-        store[:, :, columns] = dot(tokens, ref[...], 0, 0).astype(BF).reshape(16, 48, wide)
+        store[:, :, columns] = dot(rows_t[...], low[...]).astype(BF).reshape(16, 48, wide)
     copies = blocks_out(place, (ka, kb, sa, sb), store, sems, PAIR_FLIPS, 0)
     for copy in copies:
         copy.start()
@@ -869,16 +914,13 @@
     for copy in copies:
         copy.wait()
     half = residual.shape[0]
-    lows = (low0, low1, low2)
     wide = low0.shape[1]
+    weight = store[:, :48, :].reshape(768, 3 * wide)
 
     def share(side):
         begin = pl.multiple_of(side * half, half)
-        total = jnp.zeros(residual.shape, F32)
-        for index, ref in enumerate(lows):
-            weight = store[:, :48, index * wide : (index + 1) * wide].reshape(768, wide)
-            total = total + dot(ref[pl.ds(begin, half), :], weight, 1, 1)
-        return total
+        low = jnp.concatenate([ref[pl.ds(begin, half), :] for ref in (low0, low1, low2)], axis=1)
+        return dot(low, weight, 1, 1)
 
     states_send[...] = share(1 - x).astype(BF)
     states_out[...] = residual[...] + share(x)
@@ -896,30 +938,47 @@
     return sum((term.astype(F32) for term in terms[1:]), terms[0].astype(F32)).astype(BF)
 
 
-def call(kernel, outs, inputs, specs, scratch, name, micros=0, grid=()):
+def here():
+    dp, c, x = lax.axis_index(DP), lax.axis_index(FSDP), lax.axis_index(SEQ)
+    return lax.div(dp, 2), lax.rem(dp, 2), c, x, (dp * 2 + c) * 2 + x
+
+
+def call(kernel, outs, inputs, specs, scratch, name, grid=()):
     return pl.pallas_call(
-        kernel,
+        lambda *refs: kernel(here(), *refs),
         out_shape=[jax.ShapeDtypeStruct(shape, kind) for shape, kind, _ in outs],
-        in_specs=[
-            pl.BlockSpec(memory_space=SPACES[key]) if isinstance(key, str) else key
-            for key in specs
-        ],
-        out_specs=[pl.BlockSpec(memory_space=SPACES[key]) for _, _, key in outs],
+        in_specs=[spec_of(key) for key in specs],
+        out_specs=[spec_of(key) for _, _, key in outs],
         scratch_shapes=scratch,
         grid=grid,
         compiler_params=pltpu.CompilerParams(vmem_limit_bytes=60 * MIB),
-        cost_estimate=pl.CostEstimate(
-            flops=int(micros * 1.1e9), bytes_accessed=int(micros * 3e6), transcendentals=0
-        ),
+        cost_estimate=pl.CostEstimate(flops=0, bytes_accessed=0, transcendentals=0),
         name=name,
     )(*inputs)
 
 
+def spec_of(key):
+    return pl.BlockSpec(memory_space=SPACES[key]) if isinstance(key, str) else key
+
+
 SPACES = {"s": pltpu.SMEM, "v": pltpu.VMEM, "a": pl.ANY}
 
 
 def after(value, *others):
     return lax.optimization_barrier((value,) + others)[0]
+
+
+class Order:
+    def __init__(self, last):
+        self.last = last
+
+    def take(self, *values):
+        values = lax.optimization_barrier(values + (self.last,))[:-1]
+        return values if len(values) > 1 else values[0]
+
+    def step(self, value):
+        self.last = value
+        return value
 
 
 def column(rows, index):
@@ -940,33 +999,33 @@
     long = outer_weight.shape[0]
     crops = crop_lengths.shape[1]
     tall = 3 * half
-    flat = (width + hidden) // 2
+    flat = width + hidden // 2
     dma = pltpu.SemaphoreType.DMA
     dp, c, x = lax.axis_index(DP), lax.axis_index(FSDP), lax.axis_index(SEQ)
     device = (dp * 2 + c) * 2 + x
-    place = jnp.stack([dp // 2, dp % 2, c, x, device]).astype(jnp.int32)
     lens = crop_lengths[0]
     own = states[0]
 
-    v24 = jnp.stack(
-        [query_bias, value_bias, output_bias, attn_gain, attn_shift, outer_bias, final_gain, final_shift]
-    )
-    v96 = jnp.broadcast_to(inner_bias[None], (8, long))
-    send, keep, small, p1a, p1b, p2 = call(
+    vectors = [
+        vector[None]
+        for vector in (
+            query_bias, value_bias, output_bias, attn_gain, attn_shift, outer_bias, final_gain,
+            final_shift, inner_bias,
+        )
+    ]
+    send, keep, small, p1, p2 = call(
         pack_kernel,
         [
-            ((part, tall), BF, "v"),
+            ((part, tall + width + hidden), BF, "v"),
             ((part, tall), BF, "v"),
             ((16, width), BF, "v"),
-            ((part, flat), BF, "v"),
-            ((part, flat), BF, "v"),
+            ((part, width + hidden), BF, "v"),
             ((long, width), BF, "v"),
         ],
-        (place, query_weight, key_weight, value_weight, output_weight, inner_weight, outer_weight, v24, v96),
-        "svvvvvvvv",
+        (query_weight, key_weight, value_weight, output_weight, inner_weight, outer_weight, *vectors),
+        "v" * 15,
         [],
         "pack",
-        2,
     )
 
     def pair_up(mine, theirs):
@@ -977,31 +1036,41 @@
         )
 
     def along_z(block):
-        return jnp.stack(
-            [block, hop(block, planes, 2), hop(block, planes, 4), hop(block, planes, 6)]
-        )
-
-    del_other = swap(deleted, SEQ)
-    both = pair_up(keep, swap(send, SEQ))
-    tail = jnp.pad(add(small, swap(small, SEQ)), ((0, 0), (0, tall - width)))
-    both_a = jnp.concatenate([both, tail], axis=0)
-    quad_2 = along_z(p2)
-    quad_a = along_z(both_a)
-    other = swap(after(own, both_a), SEQ)
-    quad_ay = after(hop(quad_a, planes, 1), other)
-    parts_a = (quad_a, quad_ay, swap(quad_a, FSDP), swap(quad_ay, FSDP))
-    octet = jnp.concatenate([quad_2, hop(quad_2, planes, 1)], axis=0)
-    from_x = after(swap(after(p1a, both_a), SEQ), quad_a, other, del_other)
-    quad_1 = along_z(pair_up(p1a, from_x))
-    from_x = after(swap(after(p1b, both_a), SEQ), quad_1)
-    quad_b = along_z(pair_up(p1b, from_x))
-
-    marks = (place, lens, deleted, del_other)
-    queries, keys, values, mix_send, small = call(
+        return tuple(hop(block, planes, bits) for bits in (2, 4, 6))
+
+    order = Order(p2)
+    sent_2 = along_z(p2)
+    del_other, from_x, small_x = order.take(swap(deleted, SEQ), swap(send, SEQ), swap(small, SEQ))
+    tail = jnp.pad(add(small, small_x), ((0, 0), (0, tall - width)))
+    both_a = jnp.concatenate([pair_up(keep, from_x[:, :tall]), tail], axis=0)
+    both_1 = pair_up(p1[:, :flat], from_x[:, tall : tall + flat])
+    both_b = pair_up(p1[:, flat:], from_x[:, tall + flat :])
+    order.step(both_a)
+    sent_a = along_z(both_a)
+    other = swap(order.take(own), SEQ)
+    quad_2 = order.step(jnp.stack([p2, *order.take(*sent_2)]))
+    octet = hop(quad_2, planes, 1)
+    quad_a = order.step(jnp.stack([both_a, *order.take(*sent_a)]))
+    quad_ay = hop(quad_a, planes, 1)
+    sent_1 = along_z(order.take(both_1))
+    octet = order.step(jnp.concatenate([quad_2, order.take(octet)], axis=0))
+    octet_x = swap(octet, SEQ)
+    quad_ay, other = order.take(quad_ay, other)
+    order.step(quad_ay)
+    quad_1 = order.step(jnp.stack([both_1, *order.take(*sent_1)]))
+    parts_a = order.take(swap(quad_a, FSDP), swap(quad_ay, FSDP))
+    parts_a = (quad_a, quad_ay) + parts_a
+    order.step(parts_a[-1])
+    quad_1y = hop(quad_1, planes, 1)
+    sent_b = along_z(after(both_b, quad_1))
+
+    marks = (lens, deleted, del_other)
+    queries, keys, values, mix_send, log_other, small = call(
         attend_kernel,
-        [((2 * count, half), BF, "v")] * 3 + [((count, half), BF, "v"), ((16, width), F32, "v")],
-        marks + (after(own, octet, quad_1), other) + parts_a,
-        "ssvvaaaaaa",
+        [((2 * count, half), BF, "v")] * 3
+        + [((count, half), BF, "v"), ((8, count), F32, "v"), ((16, width), F32, "v")],
+        marks + (order.take(own), other) + parts_a,
+        "svvaaaaaa",
         [
             pltpu.VMEM((16, 64, tall), BF),
             pltpu.VMEM((2, count, width), BF),
@@ -1010,24 +1079,26 @@
             dma((2,)),
         ],
         "attend",
-        0,
-    )
+    )
+    order.step(mix_send)
     mix_other = swap(mix_send, SEQ)
-    quad_1y = after(hop(quad_1, planes, 1), mix_send)
-    (mix_own,) = call(
+    quad_1y = order.step(order.take(quad_1y))
+    quad_b = order.step(jnp.stack([both_b, *order.take(*sent_b)]))
+    quad_by = hop(quad_b, planes, 1)
+    mix_own, log_own = call(
         attend_own_kernel,
-        [((count, half), BF, "v")],
-        marks + (after(queries, quad_b), keys, values),
-        "ssvvvvv",
+        [((count, half), BF, "v"), ((8, count), F32, "v")],
+        marks + (order.take(queries), keys, values),
+        "svvvvv",
         [pltpu.VMEM((1, 2 * count), jnp.int32)],
         "attend_own",
-        0,
-    )
-
-    octet_x = after(swap(octet, SEQ), mix_own)
-    quad_by = after(hop(quad_b, planes, 1), mix_own)
+    )
+    order.step(mix_own)
+    octet_x, mix_other = order.take(octet_x, mix_other)
+    order.step(octet_x)
     parts_2 = (octet, octet_x, swap(octet, FSDP), swap(octet_x, FSDP))
     parts_1 = (quad_1, quad_1y, swap(quad_1, FSDP), swap(quad_1y, FSDP))
+    quad_by = order.take(quad_by)
     parts_1 += (quad_b, quad_by, swap(quad_b, FSDP), swap(quad_by, FSDP))
     four = ((hidden // width, count, width), BF, "v")
     tokens = ((count, width), BF, "v")
@@ -1049,7 +1120,7 @@
         + (own, mix_own, mix_other, small, cotangent[0], pool_cotangent[0])
         + parts_1
         + parts_2,
-        "ssvvvvvvvv" + "a" * 12,
+        "svvvvvvvv" + "a" * 12,
         [
             pltpu.VMEM((16, 2 * part, width + hidden), BF),
             pltpu.VMEM((32, long, width), BF),
@@ -1062,7 +1133,6 @@
             dma((32,)),
         ],
         "feed",
-        28,
     )
     mg_other = swap(mg_send, SEQ)
 
@@ -1070,93 +1140,140 @@
     keep_2a, keep_2b, send_2a, send_2b = call(
         outer_sum_kernel,
         [blocks_2] * 4,
-        (place, active, outer_low),
-        "svv",
+        (active, outer_low),
+        [pl.BlockSpec((1, count, width), lambda step: (step, 0, 0)), "v"],
         [pltpu.VMEM((32, long, width), BF), dma((32,))],
         "outer_sum",
-        0,
-    )
-    blocks_1 = ((4, 2 * part, width + hidden), BF, "a")
-    keep_1a, keep_1b, send_1a, send_1b = call(
+        (hidden // width,),
+    )
+    order.step(send_2b)
+    core_2b, core_small = swap(send_2b, FSDP), swap(small_grad, FSDP)
+    blocks_a = ((4, 2 * part, flat), BF, "a")
+    blocks_b = ((4, 2 * part, width + hidden - flat), BF, "a")
+    keep_1a, keep_1b, send_1a, send_1b, keep_3a, keep_3b, send_3a, send_3b = call(
         inner_sum_kernel,
-        [blocks_1] * 4,
-        (place, after(low, keep_2a, mg_other), inner_low, branch_low, mix_own, mix_other),
-        "svvvvv",
-        [pltpu.VMEM((16, 2 * part, width + hidden), BF), dma((16,))],
+        [blocks_a] * 4 + [blocks_b] * 4,
+        (order.take(low), inner_low, branch_low, mix_own, mix_other),
+        "vvvvv",
+        [
+            pltpu.VMEM((16, 2 * part, width + hidden), BF),
+            pltpu.VMEM((width, count), BF),
+            dma((80,)),
+        ],
         "inner_sum",
-        0,
-    )
-
-    t1_2 = add(keep_2b, swap(send_2b, FSDP))
-    t1_1 = add(keep_1b, swap(send_1b, FSDP))
-    smalls = small_grad + swap(small_grad, FSDP)
-
-    lows = []
-    gates = [(t1_2, t1_1, smalls)]
-    for pair in range(half // 128):
-        queries = after(queries, *gates[pair])
-        specs = [pl.BlockSpec(memory_space=pltpu.SMEM)] * 2
-        specs += [pl.BlockSpec(memory_space=pltpu.VMEM)] * 2
-        specs += [column(2 * count, pair)] * 3 + [column(count, pair)] * 2
+    )
+    order.step(send_1b)
+    core_2b, core_small, mg_other = order.take(core_2b, core_small, mg_other)
+    t1_2 = order.step(add(keep_2b, core_2b))
+    sum_2x = swap(t1_2, SEQ)
+    smalls = small_grad + core_small
+    small_y = hop(smalls, planes, 1)
+    t1_1 = order.step(add(keep_1b, order.take(swap(send_1b, FSDP))))
+    sum_1y = hop(t1_1, planes, 1)
+    t1_3 = order.step(add(keep_3b, order.take(swap(send_3b, FSDP))))
+    sum_3y = hop(t1_3, planes, 1)
+    core_2, core_1, core_3 = (
+        swap(value, FSDP) for value in order.take(send_2a, send_1a, send_3a)
+    )
+
+    def retreat(pair):
+        specs = ["s", "v", "v"] + [column(2 * count, pair)] * 3 + [column(count, pair)] * 4
         (result,) = call(
-            retreat_kernel,
-            [((2 * count, 3 * 128), BF, "v")],
-            marks + (queries, keys, values, mg_own, mg_other),
-            specs,
+            partial(retreat_kernel, pair=pair),
+            [((2 * count, 384), BF, "v")],
+            marks
+            + (order.take(queries), keys, values)
+            + (mg_own, mg_other, mix_own, mix_send, log_own, log_other),
+            specs + ["v", "v"],
             [
                 pltpu.VMEM((2 * count, 1), F32),
                 pltpu.VMEM((2 * count, 128), F32),
                 pltpu.VMEM((2 * count, 128), F32),
             ],
             "retreat",
-            0,
             (1,),
         )
-        lows.append(result)
-        smalls = smalls + after(hop(smalls, planes, 1 << pair), result)
-        gates.append((result, smalls))
-
-    t0_2 = add(keep_2a, swap(send_2a, FSDP))
-    t0_1 = add(keep_1a, swap(send_1a, FSDP))
-    u_2 = add(t0_2, after(swap(t1_2, SEQ), lows[2]))
-    u_1 = add(t0_1, after(hop(t1_1, planes, 1), lows[2]))
-    lows = [after(value, u_2, u_1) for value in lows]
+        return order.step(result)
+
+    def split_x(v):
+        v = v.reshape((2, part) + v.shape[1:])
+        return jnp.where(x == 0, v[0], v[1]), swap(jnp.where(x == 0, v[1], v[0]), SEQ)
+
+    def to_z(u):
+        return tuple(hop(u[index], planes, 2 * index) for index in (1, 2, 3))
+
+    def split_x(v):
+        v = v.reshape((2, part) + v.shape[1:])
+        return jnp.where(x == 0, v[0], v[1]), swap(jnp.where(x == 0, v[1], v[0]), SEQ)
+
+    def to_z(u):
+        return tuple(hop(u[index], planes, 2 * index) for index in (1, 2, 3))
+
+    lows = [retreat(0), retreat(1)]
+    u_1 = order.step(add(keep_1a, *order.take(core_1, sum_1y)))
+    sum_1z = to_z(u_1)
+    lows.append(retreat(2))
+    u_3 = order.step(add(keep_3a, *order.take(core_3, sum_3y)))
+    sum_3z = to_z(u_3)
+    u_2 = order.step(add(keep_2a, *order.take(core_2, sum_2x)))
+    sum_2y = hop(u_2[4:], planes, 1)
     wide = tall + 128
     keep_a, keep_b, send_a, send_b = call(
         project_sum_kernel,
         [((4, 2 * part, wide), BF, "a")] * 4,
-        (place, own, other) + tuple(lows),
-        "saavvv",
+        (order.take(own), other, *lows),
+        "aavvv",
         [
             pltpu.VMEM((2, count, width), BF),
             pltpu.VMEM((16, 2 * part, wide), BF),
+            pltpu.VMEM((width, 2 * count), BF),
             dma((2,)),
             dma((16,)),
         ],
         "project_sum",
-        0,
-    )
+    )
+    order.step(send_b)
+    core_b, core_a = swap(send_b, FSDP), swap(send_a, FSDP)
+    v_1 = order.step(add(u_1[0], *order.take(*sum_1z)))
+    smalls = smalls + order.take(small_y)
+    small_z = hop(smalls, planes, 2)
+    v_2 = order.step(add(u_2[:4], order.take(sum_2y)))
+    sum_2z = to_z(v_2)
+    t1_a = order.step(add(keep_b, order.take(core_b)))
+    sum_ay = hop(t1_a, planes, 1)
     states_part, states_send = call(
         states_sum_kernel,
         [((count, width), F32, "v"), tokens],
-        (place,) + tuple(after(value, keep_a) for value in lows) + (residual,) + parts_a,
-        "svvvvaaaa",
+        (order.take(lows[0]), lows[1], lows[2], residual) + parts_a,
+        "vvvvaaaa",
         [pltpu.VMEM((16, 64, tall), BF), dma((16,))],
         "states_sum",
-        0,
-    )
-    states_grad = states_part + swap(states_send, SEQ).astype(F32)
-
-    def last_z(u):
-        return add(u[0], hop(u[1], planes, 2), hop(u[2], planes, 4), hop(u[3], planes, 6))
-
-    t1 = add(keep_b, swap(send_b, FSDP))
-    t0 = add(keep_a, swap(send_a, FSDP))
-    v = last_z(add(t0, hop(t1, planes, 1))).reshape(2, part, wide)
-    mine = jnp.where(x == 0, v[0], v[1])
-    theirs = swap(jnp.where(x == 0, v[1], v[0]), SEQ)
-    left = jnp.where(x == 0, mine, theirs).astype(F32)
-    right = jnp.where(x == 0, theirs, mine).astype(F32)
+    )
+    order.step(states_send)
+    states_x = swap(states_send, SEQ)
+    u_a = order.step(add(keep_a, *order.take(core_a, sum_ay)))
+    sum_az = to_z(u_a)
+    v = order.step(jnp.concatenate([v_1, add(u_3[0], *order.take(*sum_3z))], axis=1))
+    mine_1, theirs_1 = split_x(v)
+    smalls = order.step(smalls + order.take(small_z))
+    small_z = hop(smalls, planes, 4)
+    pooled_x = swap(pooled, SEQ)
+    states_grad = order.step(states_part + order.take(states_x).astype(F32))
+    v = order.step(add(u_a[0], *order.take(*sum_az)))
+    mine_a, theirs_a = split_x(v)
+    smalls = order.step(smalls + order.take(small_z))
+    small_x = swap(smalls, SEQ)
+    total = mine_1.astype(F32) + order.take(theirs_1).astype(F32)
+    order.step(total)
+    grad_output_weight, grad_inner_weight = total[:, :width], total[:, width:]
+    sum_2z = order.take(*sum_2z)
+    grad_outer_weight = v_2[0].astype(F32) + sum(term.astype(F32) for term in sum_2z)
+    order.step(grad_outer_weight)
+    pooled = pooled + order.take(pooled_x)
+    smalls = smalls + order.take(small_x)
+    theirs = order.take(theirs_a)
+    left = jnp.where(x == 0, mine_a, theirs).astype(F32)
+    right = jnp.where(x == 0, theirs, mine_a).astype(F32)
 
     def gathered(index):
         columns = [
@@ -1169,28 +1286,11 @@
     grad_query_weight, grad_key_weight, grad_value_weight = (gathered(i) for i in range(3))
     bias_grads = jnp.stack([left[:6, tall:], right[:6, tall:]]).reshape(2, 2, half)
     bias_grads = jnp.transpose(bias_grads, (1, 0, 2)).reshape(2, width)
-
-    u1_2, u0_2 = u_2[4:], u_2[:4]
-    v = add(u0_2, hop(u1_2, planes, 1))
-    grad_outer_weight = (
-        v[0].astype(F32)
-        + hop(v[1], planes, 2).astype(F32)
-        + hop(v[2], planes, 4).astype(F32)
-        + hop(v[3], planes, 6).astype(F32)
-    )
-    v = last_z(u_1).reshape(2, part, width + hidden)
-    mine = jnp.where(x == 0, v[0], v[1])
-    theirs = swap(jnp.where(x == 0, v[1], v[0]), SEQ)
-    total = mine.astype(F32) + theirs.astype(F32)
-    grad_output_weight, grad_inner_weight = total[:, :width], total[:, width:]
-
-    smalls = smalls + swap(smalls, SEQ)
     vectors = lax.dynamic_slice(smalls[:8], (0, device * part), (8, part))
     bias_grads = lax.dynamic_slice(bias_grads, (0, device * part), (2, part))
     grad_inner_bias = lax.dynamic_slice(
         smalls[8:12].reshape(hidden), (device * long,), (long,)
     )
-    pooled = pooled + swap(pooled, SEQ)
     return (
         output[None],
         pooled[None],

time: 319 us -> 284 us (0.89)
  waiting for transfers between devices: 87.6 us -> 68.6 us
  Pallas kernels: 115 us -> 105 us
  starting transfers between devices: 79.8 us -> 70.7 us
    ppermute x31 -> x35, waiting for transfers between devices: 61.9 us -> 35.2 us  [hop(): return lax.ppermute(value, DP, [(i, i ^ bits) for i in range(planes)])]
    ppermute x31 -> x35, starting transfers between devices: 58.1 us -> 48.3 us  [hop(): return lax.ppermute(value, DP, [(i, i ^ bits) for i in range(planes)])]
    pallas_call x11, Pallas kernels: 115 us -> 105 us  [call(): pl.pallas_call(lambda *refs: kernel(here(), *refs), out_shape=[jax.ShapeD...]
    ppermute x30, waiting for transfers between devices: 25.8 us -> 33.4 us  [swap(): return lax.ppermute(value, axis, [(0, 1), (1, 0)])]
    convert_element_type x10 -> x13, other arithmetic: 7.23 us -> 10.5 us  [add(): sum((term.astype(F32) for term in terms[1:]), terms[0].astype(F32))]
    unnamed x69 -> x85, local copies, waits for them, and re-layouts: 6.2 us -> 9.23 us
  transfers between devices with their start and end apart: 61 -> 65, of which waited for: 21 -> 18; matrix products, arithmetic and copies ran while one was open for 8% -> 10% of each run, Pallas kernels for 27% -> 24%
where the time goes in v2:
time: 284 us; the launch traced here: 280 us
  Pallas kernels  105 us (37%)
  starting transfers between devices  70.7 us (25%)
  waiting for transfers between devices  68.6 us (24%)
  other arithmetic  17.3 us (6%)
  local copies, waits for them, and re-layouts  17.2 us (6%)
    pallas_call x11, Pallas kernels, call(): pl.pallas_call(lambda *refs: kernel(here(), *refs), out_shape=[jax.ShapeD...  105 us
    ppermute x35, starting transfers between devices, hop(): return lax.ppermute(value, DP, [(i, i ^ bits) for i in range(planes)])  48.3 us
    ppermute x35, waiting for transfers between devices, hop(): return lax.ppermute(value, DP, [(i, i ^ bits) for i in range(planes)])  35.2 us
    ppermute x30, waiting for transfers between devices, swap(): return lax.ppermute(value, axis, [(0, 1), (1, 0)])  33.4 us
    ppermute x30, starting transfers between devices, swap(): return lax.ppermute(value, axis, [(0, 1), (1, 0)])  22.4 us
    convert_element_type x13, other arithmetic, add(): sum((term.astype(F32) for term in terms[1:]), terms[0].astype(F32))  10.5 us
    unnamed x85, local copies, waits for them, and re-layouts  9.23 us
  transfers between devices with their start and end apart: 65, of which 18 were waited for; matrix products, arithmetic and copies ran while one was open for 10% of the time, Pallas kernels for 24%

profile of v2, /device:TPU:0, one launch (start us, length us, event | category | flops | bytes accessed | tf_op | source)
XLA Modules:
  0.0 280.5 jit_solution(17289881283041859075)
XLA Ops:
  0.7 2.2 pack.1
  2.9 5.1 %collective-permute-start.8 = (bf16[96,768]{1,0:T(8,128)(2,1)}, bf16[96,768]{1,0:T(8,128)(2,1)S(1)}, u32[]{:S(2)}, u32[]{:S(2)}) collective-permute-start(bf16[96,768]{1,0:T(8,128)(2,1)} %get-tuple-element.135), channel_id=1, source_target_pairs={{0,24},{4,28},{8,16},{12,20},{16,8},{20,12},{24,0},{28,4},{1,25},{... | collective-permute-start | bytes 442376 | tf_op jit(solution)/shard_map/ppermute | solution.py:934
  14.9 2.4 collective-permute-done.1
  18.2 1.7 collective-permute-start.5
  21.0 1.7 collective-permute-start.3
  22.6 1.8 collective-permute-done.6
  24.5 1.6 collective-permute-start.12
  26.1 3.1 %collective-permute-start.11 = (bf16[512,768]{1,0:T(8,128)(2,1)S(1)}, bf16[512,768]{1,0:T(8,128)(2,1)S(1)}, u32[]{:S(2)}, u32[]{:S(2)}) collective-permute-start(bf16[512,768]{1,0:T(8,128)(2,1)S(1)} %bitcast.110), channel_id=1, source_target_pairs={{0,1},{1,0},{2,3},{3,2},{4,5},{5,4},{6,7},{7,6},{8,9},{9,8},{10,11... | collective-permute-start | bytes 2359304 | tf_op jit(solution)/shard_map/ppermute | solution.py:930
  29.9 3.5 %collective-permute-done.4 = bf16[64,1152]{1,0:T(8,128)(2,1)S(1)} collective-permute-done((bf16[64,1152]{1,0:T(8,128)(2,1)S(1)}, bf16[64,1152]{1,0:T(8,128)(2,1)S(1)}, u32[]{:S(2)}, u32[]{:S(2)}) %collective-permute-start.4) | collective-permute-done | bytes 147488 | tf_op jit(solution)/shard_map/ppermute | solution.py:934
  33.5 1.6 collective-permute-start.10
  35.8 2.5 collective-permute-start.16
  38.3 1.9 collective-permute-start.14
  41.7 6.5 %collective-permute-done.10.refs_6_.refs_5_ = bf16[4,64,1152]{2,1,0:T(8,128)(2,1)S(1)} collective-permute-done((bf16[4,64,1152]{2,1,0:T(8,128)(2,1)S(1)}, bf16[4,64,1152]{2,1,0:T(8,128)(2,1)S(1)}, u32[]{:S(2)}, u32[]{:S(2)}) %collective-permute-start.10) | collective-permute-done | bytes 589856 | tf_op jit(solution)/shard_map/ppermute | solution.py:934
  48.2 7.3 %collective-permute-done.15 = bf16[48,2304]{1,0:T(8,128)(2,1)S(1)} collective-permute-done((bf16[48,2304]{1,0:T(8,128)(2,1)S(1)}, bf16[48,2304]{1,0:T(8,128)(2,1)S(1)}, u32[]{:S(2)}, u32[]{:S(2)}) %collective-permute-start.15) | collective-permute-done | bytes 221216 | tf_op jit(solution)/shard_map/ppermute | solution.py:934
  62.6 3.1 %collective-permute-start.17 = (bf16[48,1536]{1,0:T(8,128)(2,1)}, bf16[48,1536]{1,0:T(8,128)(2,1)S(1)}, u32[]{:S(2)}, u32[]{:S(2)}) collective-permute-start(bf16[48,1536]{1,0:T(8,128)(2,1)} %maximum_select_fusion.3), channel_id=1, source_target_pairs={{0,8},{4,12},{8,0},{12,4},{16,24},{20,28},{24,16},{28,20},{1,9},{5... | collective-permute-start | bytes 442376 | tf_op jit(solution)/shard_map/ppermute | solution.py:934
  65.7 12.2 %attend.1 = (bf16[1024,384]{1,0:T(8,128)(2,1)}, bf16[1024,384]{1,0:T(8,128)(2,1)}, bf16[1024,384]{1,0:T(8,128)(2,1)}, bf16[512,384]{1,0:T(8,128)(2,1)}, f32[8,512]{1,0:T(8,128)}, /*index=5*/f32[16,768]{1,0:T(8,128)}) custom-call(s32[8]{0:T(128)} %bitcast.127, s32[1,512]{1,0:T(1,128)} %refs_1_.13, s32[1,512]{1,0:T(1,128)} %copy-done.28, ...), custom_call_target="tpu_custom_call" | custom-call | tf_op jit(solution)/shard_map/attend/pallas_call | solution.py:947
  80.8 1.6 collective-permute-start.25
  82.3 8.2 %attend_own.1 = (bf16[512,384]{1,0:T(8,128)(2,1)}, f32[8,512]{1,0:T(8,128)}) custom-call(s32[8]{0:T(128)} %bitcast.128, s32[1,512]{1,0:T(1,128)} %refs_1_.13, s32[1,512]{1,0:T(1,128)} %copy-done.28, bf16[1024,384]{1,0:T(8,128)(2,1)} %get-tuple-element.209.refs_3_, bf16[1024,384]{1,0:T(8,128)(2,1)} %get-tuple-element.166.refs_4_, ...), custom_call_target="tpu_custom_call" | custom-call | tf_op jit(solution)/shard_map/attend_own/pallas_call | solution.py:947
  90.6 3.7 %collective-permute-done.22.refs_5_.refs_4_ = bf16[512,384]{1,0:T(8,128)(2,1)S(1)} collective-permute-done((bf16[512,384]{1,0:T(8,128)(2,1)}, bf16[512,384]{1,0:T(8,128)(2,1)S(1)}, u32[]{:S(2)}, u32[]{:S(2)}) %collective-permute-start.22) | collective-permute-done | bytes 393248 | tf_op jit(solution)/shard_map/ppermute | solution.py:930
  94.8 1.8 collective-permute-done.25.refs_14_
  97.0 3.0 %collective-permute-done.26.refs_15_ = bf16[4,48,1536]{2,1,0:T(8,128)(2,1)S(1)} collective-permute-done((bf16[4,48,1536]{2,1,0:T(8,128)(2,1)S(1)}, bf16[4,48,1536]{2,1,0:T(8,128)(2,1)S(1)}, u32[]{:S(2)}, u32[]{:S(2)}) %collective-permute-start.26) | collective-permute-done | bytes 589856 | tf_op jit(solution)/shard_map/ppermute | solution.py:930
  101.7 28.5 %feed.1 = (bf16[512,768]{1,0:T(8,128)(2,1)}, f32[8,768]{1,0:T(8,128)}, f32[512,768]{1,0:T(8,128)}, bf16[512,384]{1,0:T(8,128)(2,1)}, bf16[512,384]{1,0:T(8,128)(...) custom-call(s32[8]{0:T(128)} %bitcast.129, ...), custom_call_target="tpu_custom_call" | custom-call | tf_op jit(solution)/shard_map/feed/pallas_call | solution.py:947
  130.2 6.9 %outer_sum.1 = (bf16[8,96,768]{2,1,0:T(8,128)(2,1)}, bf16[8,96,768]{2,1,0:T(8,128)(2,1)}, bf16[8,96,768]{2,1,0:T(8,128)(2,1)}, bf16[8,96,768]{2,1,0:T(8,128)(2,1)}) custom-call(bf16[4,512,768]{2,1,0:T(8,128)(2,1)} %get-tuple-element.175.refs_0_, bf16[512,768]{1,0:T(8,128)(2,1)} %get-tuple-element.176.refs_1_), custom_call_target="tpu_custom_call" | custom-call | tf_op jit(solution)/shard_map/outer_sum/pallas_call | solution.py:947
  137.3 7.7 %inner_sum.1 = (bf16[4,48,2304]{2,1,0:T(8,128)(2,1)}, bf16[4,48,2304]{2,1,0:T(8,128)(2,1)}, bf16[4,48,2304]{2,1,0:T(8,128)(2,1)}, bf16[4,48,2304]{2,1,0:T(8,128)...) custom-call(bf16[512,768]{1,0:T(8,128)(2,1)} %get-tuple-element.181., ...), custom_call_target="tpu_custom_call" | custom-call | tf_op jit(solution)/shard_map/inner_sum/pallas_call | solution.py:947
  148.2 8.4 %collective-permute-done.35.refs_7_ = bf16[512,384]{1,0:T(8,128)(2,1)S(1)} collective-permute-done((bf16[512,384]{1,0:T(8,128)(2,1)S(1)}, bf16[512,384]{1,0:T(8,128)(2,1)S(1)}, u32[]{:S(2)}, u32[]{:S(2)}) %collective-permute-start.35) | collective-permute-done | bytes 393248 | tf_op jit(solution)/shard_map/ppermute | solution.py:930
  156.7 1.7 add_convert_fusion.1
  159.7 1.6 collective-permute-start.41
  163.9 8.3 %retreat.3.refs_2_.refs_0_ = bf16[1024,384]{1,0:T(8,128)(2,1)} custom-call(s32[8]{0:T(128)} %bitcast.130, s32[1,512]{1,0:T(1,128)} %refs_1_.13, s32[1,512]{1,0:T(1,128)} %copy-done.28, bf16[1024,384]{1,0:T(8,128)(2,1)} %get-tuple-element.209.refs_3_, bf16[1024,384]{1,0:T(8,128)(2,1)} %get-tuple-element.166.refs_4_, ...), custom_call_target="tpu_custom_call" | custom-call | tf_op jit(solution)/shard_map/retreat/pallas_call | solution.py:947
  172.2 8.2 %retreat.4.refs_3_.refs_1_ = bf16[1024,384]{1,0:T(8,128)(2,1)} custom-call(s32[8]{0:T(128)} %bitcast.131, s32[1,512]{1,0:T(1,128)} %refs_1_.13, s32[1,512]{1,0:T(1,128)} %copy-done.28, bf16[1024,384]{1,0:T(8,128)(2,1)} %get-tuple-element.209.refs_3_, bf16[1024,384]{1,0:T(8,128)(2,1)} %get-tuple-element.166.refs_4_, ...), custom_call_target="tpu_custom_call" | custom-call | tf_op jit(solution)/shard_map/retreat/pallas_call | solution.py:947
  182.4 1.8 add_convert_fusion.2
  184.1 8.2 %retreat.5.refs_4_.refs_2_ = bf16[1024,384]{1,0:T(8,128)(2,1)} custom-call(s32[8]{0:T(128)} %bitcast.132, s32[1,512]{1,0:T(1,128)} %refs_1_.13, s32[1,512]{1,0:T(1,128)} %copy-done.28, bf16[1024,384]{1,0:T(8,128)(2,1)} %get-tuple-element.209.refs_3_, bf16[1024,384]{1,0:T(8,128)(2,1)} %get-tuple-element.166.refs_4_, ...), custom_call_target="tpu_custom_call" | custom-call | tf_op jit(solution)/shard_map/retreat/pallas_call | solution.py:947
  192.9 2.1 collective-permute-done.39
  198.7 3.1 %collective-permute-start.43 = (bf16[48,2304]{1,0:T(8,128)(2,1)}, bf16[48,2304]{1,0:T(8,128)(2,1)S(1)}, u32[]{:S(2)}, u32[]{:S(2)}) collective-permute-start(bf16[48,2304]{1,0:T(8,128)(2,1)} %get-tuple-element.250), channel_id=1, source_target_pairs={{0,8},{4,12},{8,0},{12,4},{16,24},{20,28},{24,16},{28,20},{1,9},{5... | collective-permute-start | bytes 663560 | tf_op jit(solution)/shard_map/ppermute | solution.py:934
  201.9 1.8 add_convert_fusion
  203.7 7.1 %project_sum.1 = (bf16[4,48,1280]{2,1,0:T(8,128)(2,1)}, bf16[4,48,1280]{2,1,0:T(8,128)(2,1)}, bf16[4,48,1280]{2,1,0:T(8,128)(2,1)}, bf16[4,48,1280]{2,1,0:T(8,128)(2,1)}) custom-call(bf16[512,768]{1,0:T(8,128)(2,1)} %bitcast.109, bf16[512,768]{1,0:T(8,128)(2,1)} %copy-done.4, bf16[1024,384]{1,0:T(8,128)(2,1)} %retreat.3.refs_2_.refs_0_, ...), custom_call_target="tpu_custom_call" | custom-call | tf_op jit(solution)/shard_map/project_sum/pallas_call | solution.py:947
  212.3 2.7 collective-permute-done.44
  217.5 6.9 %collective-permute-done.42 = bf16[4,96,768]{2,1,0:T(8,128)(2,1)S(1)} collective-permute-done((bf16[4,96,768]{2,1,0:T(8,128)(2,1)S(1)}, bf16[4,96,768]{2,1,0:T(8,128)(2,1)S(1)}, u32[]{:S(2)}, u32[]{:S(2)}) %collective-permute-start.42) | collective-permute-done | bytes 589856 | tf_op jit(solution)/shard_map/ppermute | solution.py:934
  224.7 1.6 collective-permute-start.54
  228.8 7.3 %states_sum.1 = (f32[512,768]{1,0:T(8,128)}, bf16[512,768]{1,0:T(8,128)(2,1)}) custom-call(bf16[1024,384]{1,0:T(8,128)(2,1)} %retreat.3.refs_2_.refs_0_, bf16[1024,384]{1,0:T(8,128)(2,1)} %retreat.4.refs_3_.refs_1_, bf16[1024,384]{1,0:T(8,128)(2,1)} %retreat.5.refs_4_.refs_2_, f32[512,768]{1,0:T(8,128)} %get-tuple-element.225.refs_3_, ...), custom_call_target="tpu_custom_call" | custom-call | tf_op jit(solution)/shard_map/states_sum/pallas_call | solution.py:947
  236.2 2.6 collective-permute-start.49
  242.3 1.9 collective-permute-start.61
  246.6 9.2 %collective-permute-done.62 = bf16[512,768]{1,0:T(8,128)(2,1)S(1)} collective-permute-done((bf16[512,768]{1,0:T(8,128)(2,1)S(1)}, bf16[512,768]{1,0:T(8,128)(2,1)S(1)}, u32[]{:S(2)}, u32[]{:S(2)}) %collective-permute-start.62) | collective-permute-done | bytes 786464 | tf_op jit(solution)/shard_map/ppermute | solution.py:930
  258.6 2.6 collective-permute-start.48
  261.2 2.2 collective-permute-done.59
  263.3 1.8 collective-permute-start.55
  265.3 3.6 %collective-permute-done.55 = bf16[24,3840]{1,0:T(8,128)(2,1)S(1)} collective-permute-done((bf16[24,3840]{1,0:T(8,128)(2,1)S(1)}, bf16[24,3840]{1,0:T(8,128)(2,1)S(1)}, u32[]{:S(2)}, u32[]{:S(2)}) %collective-permute-start.55) | collective-permute-done | bytes 184352 | tf_op jit(solution)/shard_map/ppermute | solution.py:930
  268.9 1.8 collective-permute-start.64
  276.2 2.3 collective-permute-done.63
  (239 shorter events, 60.4 us)
Async XLA Ops:
  2.9 18.0 %collective-permute-start.8 = (bf16[96,768]{1,0:T(8,128)(2,1)}, bf16[96,768]{1,0:T(8,128)(2,1)S(1)}, u32[]{:S(2)}, u32[]{:S(2)}) collective-permute-start(bf16[96,768]{1,0:T(8,128)(2,1)} %get-tuple-element.135), channel_id=1, source_target_pairs={{0,24},{4,28},{8,16},{12,20},{16,8},{20,12},{24,0},{28,4},{1,25},{... | collective-permute-start | bytes 442376 | tf_op jit(solution)/shard_map/ppermute | solution.py:934
  8.0 14.6 %collective-permute-start.7 = (bf16[96,768]{1,0:T(8,128)(2,1)}, bf16[96,768]{1,0:T(8,128)(2,1)S(1)}, u32[]{:S(2)}, u32[]{:S(2)}) collective-permute-start(bf16[96,768]{1,0:T(8,128)(2,1)} %get-tuple-element.135), channel_id=1, source_target_pairs={{0,16},{4,20},{8,24},{12,28},{16,0},{20,4},{24,8},{28,12},{1,17},{... | collective-permute-start | bytes 442376 | tf_op jit(solution)/shard_map/ppermute | solution.py:934
  14.1 10.4 %collective-permute-start.6 = (bf16[96,768]{1,0:T(8,128)(2,1)}, bf16[96,768]{1,0:T(8,128)(2,1)S(1)}, u32[]{:S(2)}, u32[]{:S(2)}) collective-permute-start(bf16[96,768]{1,0:T(8,128)(2,1)} %get-tuple-element.135), channel_id=1, source_target_pairs={{0,8},{4,12},{8,0},{12,4},{16,24},{20,28},{24,16},{28,20},{1,9},{5... | collective-permute-start | bytes 442376 | tf_op jit(solution)/shard_map/ppermute | solution.py:934
  18.2 11.8 %collective-permute-start.5 = (bf16[64,1152]{1,0:T(8,128)(2,1)S(1)}, bf16[64,1152]{1,0:T(8,128)(2,1)S(1)}, u32[]{:S(2)}, u32[]{:S(2)}) collective-permute-start(bf16[64,1152]{1,0:T(8,128)(2,1)S(1)} %get-tuple-element.271), channel_id=1, source_target_pairs={{0,24},{4,28},{8,16},{12,20},{16,8},{20,12},{24,0},{28,4},{1,25},{... | collective-permute-start | bytes 442376 | tf_op jit(solution)/shard_map/ppermute | solution.py:934
  19.9 13.5 %collective-permute-start.4 = (bf16[64,1152]{1,0:T(8,128)(2,1)S(1)}, bf16[64,1152]{1,0:T(8,128)(2,1)S(1)}, u32[]{:S(2)}, u32[]{:S(2)}) collective-permute-start(bf16[64,1152]{1,0:T(8,128)(2,1)S(1)} %get-tuple-element.271), channel_id=1, source_target_pairs={{0,16},{4,20},{8,24},{12,28},{16,0},{20,4},{24,8},{28,12},{1,17},{... | collective-permute-start | bytes 442376 | tf_op jit(solution)/shard_map/ppermute | solution.py:934
  21.0 12.4 %collective-permute-start.3 = (bf16[64,1152]{1,0:T(8,128)(2,1)S(1)}, bf16[64,1152]{1,0:T(8,128)(2,1)S(1)}, u32[]{:S(2)}, u32[]{:S(2)}) collective-permute-start(bf16[64,1152]{1,0:T(8,128)(2,1)S(1)} %get-tuple-element.271), channel_id=1, source_target_pairs={{0,8},{4,12},{8,0},{12,4},{16,24},{20,28},{24,16},{28,20},{1,9},{5... | collective-permute-start | bytes 442376 | tf_op jit(solution)/shard_map/ppermute | solution.py:934
  24.5 13.7 %collective-permute-start.12 = (bf16[4,96,768]{2,1,0:T(8,128)(2,1)S(1)}, bf16[4,96,768]{2,1,0:T(8,128)(2,1)S(1)}, u32[]{:S(2)}, u32[]{:S(2)}) collective-permute-start(bf16[4,96,768]{2,1,0:T(8,128)(2,1)S(1)} %pad_maximum_fusion.1), channel_id=1, source_target_pairs={{0,4},{4,0},{8,12},{12,8},{16,20},{20,16},{24,28},{28,24},{1,5},{5... | collective-permute-start | bytes 1769480 | tf_op jit(solution)/shard_map/ppermute | solution.py:934
  26.1 22.1 %collective-permute-start.11 = (bf16[512,768]{1,0:T(8,128)(2,1)S(1)}, bf16[512,768]{1,0:T(8,128)(2,1)S(1)}, u32[]{:S(2)}, u32[]{:S(2)}) collective-permute-start(bf16[512,768]{1,0:T(8,128)(2,1)S(1)} %bitcast.110), channel_id=1, source_target_pairs={{0,1},{1,0},{2,3},{3,2},{4,5},{5,4},{6,7},{7,6},{8,9},{9,8},{10,11... | collective-permute-start | bytes 2359304 | tf_op jit(solution)/shard_map/ppermute | solution.py:930
  33.5 14.7 %collective-permute-start.10 = (bf16[4,64,1152]{2,1,0:T(8,128)(2,1)S(1)}, bf16[4,64,1152]{2,1,0:T(8,128)(2,1)S(1)}, u32[]{:S(2)}, u32[]{:S(2)}) collective-permute-start(bf16[4,64,1152]{2,1,0:T(8,128)(2,1)S(1)} %pad_maximum_fusion.2.refs_5_.refs_4_), channel_id=1, source_target_pairs={{0,4},{4,0},{8,12},{12,8},{16,20},{20,16},{24,28},{28,24},{1,5},{5... | collective-permute-start | bytes 1769480 | tf_op jit(solution)/shard_map/ppermute | solution.py:934
  35.8 12.5 %collective-permute-start.16 = (bf16[48,2304]{1,0:T(8,128)(2,1)S(1)}, bf16[48,2304]{1,0:T(8,128)(2,1)S(1)}, u32[]{:S(2)}, u32[]{:S(2)}) collective-permute-start(bf16[48,2304]{1,0:T(8,128)(2,1)S(1)} %maximum_select_fusion.1), channel_id=1, source_target_pairs={{0,24},{4,28},{8,16},{12,20},{16,8},{20,12},{24,0},{28,4},{1,25},{... | collective-permute-start | bytes 663560 | tf_op jit(solution)/shard_map/ppermute | solution.py:934
  38.3 17.3 %collective-permute-start.15 = (bf16[48,2304]{1,0:T(8,128)(2,1)S(1)}, bf16[48,2304]{1,0:T(8,128)(2,1)S(1)}, u32[]{:S(2)}, u32[]{:S(2)}) collective-permute-start(bf16[48,2304]{1,0:T(8,128)(2,1)S(1)} %maximum_select_fusion.1), channel_id=1, source_target_pairs={{0,16},{4,20},{8,24},{12,28},{16,0},{20,4},{24,8},{28,12},{1,17},{... | collective-permute-start | bytes 663560 | tf_op jit(solution)/shard_map/ppermute | solution.py:934
  38.3 17.3 %collective-permute-start.14 = (bf16[48,2304]{1,0:T(8,128)(2,1)S(1)}, bf16[48,2304]{1,0:T(8,128)(2,1)S(1)}, u32[]{:S(2)}, u32[]{:S(2)}) collective-permute-start(bf16[48,2304]{1,0:T(8,128)(2,1)S(1)} %maximum_select_fusion.1), channel_id=1, source_target_pairs={{0,8},{4,12},{8,0},{12,4},{16,24},{20,28},{24,16},{28,20},{1,9},{5... | collective-permute-start | bytes 663560 | tf_op jit(solution)/shard_map/ppermute | solution.py:934
  55.7 22.4 %collective-permute-start.20 = (bf16[4,48,2304]{2,1,0:T(8,128)(2,1)S(1)}, bf16[4,48,2304]{2,1,0:T(8,128)(2,1)}, u32[]{:S(2)}, u32[]{:S(2)}) collective-permute-start(bf16[4,48,2304]{2,1,0:T(8,128)(2,1)S(1)} %pad_maximum_fusion.refs_9_), channel_id=1, source_target_pairs={{0,4},{4,0},{8,12},{12,8},{16,20},{20,16},{24,28},{28,24},{1,5},{5... | collective-permute-start | bytes 2654216 | tf_op jit(solution)/shard_map/ppermute | solution.py:934
  57.2 33.4 %collective-permute-start.21 = (bf16[8,96,768]{2,1,0:T(8,128)(2,1)}, bf16[8,96,768]{2,1,0:T(8,128)(2,1)}, u32[]{:S(2)}, u32[]{:S(2)}) collective-permute-start(bf16[8,96,768]{2,1,0:T(8,128)(2,1)} %constant_dynamic-update-slice_fusion.refs_17_), channel_id=1, source_target_pairs={{0,1},{1,0},{2,3},{3,2},{4,5},{5,4},{6,7},{7,6},{8,9},{9,8},{10,11... | collective-permute-start | bytes 3538952 | tf_op jit(solution)/shard_map/ppermute | solution.py:930
  60.5 17.4 %collective-permute-start.19 = (bf16[48,1536]{1,0:T(8,128)(2,1)}, bf16[48,1536]{1,0:T(8,128)(2,1)S(1)}, u32[]{:S(2)}, u32[]{:S(2)}) collective-permute-start(bf16[48,1536]{1,0:T(8,128)(2,1)} %maximum_select_fusion.3), channel_id=1, source_target_pairs={{0,24},{4,28},{8,16},{12,20},{16,8},{20,12},{24,0},{28,4},{1,25},{... | collective-permute-start | bytes 442376 | tf_op jit(solution)/shard_map/ppermute | solution.py:934
  61.8 17.0 %collective-permute-start.18 = (bf16[48,1536]{1,0:T(8,128)(2,1)}, bf16[48,1536]{1,0:T(8,128)(2,1)S(1)}, u32[]{:S(2)}, u32[]{:S(2)}) collective-permute-start(bf16[48,1536]{1,0:T(8,128)(2,1)} %maximum_select_fusion.3), channel_id=1, source_target_pairs={{0,16},{4,20},{8,24},{12,28},{16,0},{20,4},{24,8},{28,12},{1,17},{... | collective-permute-start | bytes 442376 | tf_op jit(solution)/shard_map/ppermute | solution.py:934
  62.6 16.3 %collective-permute-start.17 = (bf16[48,1536]{1,0:T(8,128)(2,1)}, bf16[48,1536]{1,0:T(8,128)(2,1)S(1)}, u32[]{:S(2)}, u32[]{:S(2)}) collective-permute-start(bf16[48,1536]{1,0:T(8,128)(2,1)} %maximum_select_fusion.3), channel_id=1, source_target_pairs={{0,8},{4,12},{8,0},{12,4},{16,24},{20,28},{24,16},{28,20},{1,9},{5... | collective-permute-start | bytes 442376 | tf_op jit(solution)/shard_map/ppermute | solution.py:934
  78.0 18.6 %collective-permute-start.23 = (bf16[4,48,2304]{2,1,0:T(8,128)(2,1)S(1)}, bf16[4,48,2304]{2,1,0:T(8,128)(2,1)S(1)}, u32[]{:S(2)}, u32[]{:S(2)}) collective-permute-start(bf16[4,48,2304]{2,1,0:T(8,128)(2,1)S(1)} %pad_maximum_fusion.refs_9_), channel_id=1, source_target_pairs={{0,2},{2,0},{1,3},{3,1},{4,6},{6,4},{5,7},{7,5},{8,10},{10,8},{9,1... | collective-permute-start | bytes 2654216 | tf_op jit(solution)/shard_map/ppermute | solution.py:930
  78.0 16.2 %collective-permute-start.22 = (bf16[512,384]{1,0:T(8,128)(2,1)}, bf16[512,384]{1,0:T(8,128)(2,1)S(1)}, u32[]{:S(2)}, u32[]{:S(2)}) collective-permute-start(bf16[512,384]{1,0:T(8,128)(2,1)} %get-tuple-element.160.refs_9_), channel_id=1, source_target_pairs={{0,1},{1,0},{2,3},{3,2},{4,5},{5,4},{6,7},{7,6},{8,9},{9,8},{10,11... | collective-permute-start | bytes 1179656 | tf_op jit(solution)/shard_map/ppermute | solution.py:930
  78.7 18.3 %collective-permute-start.28 = (bf16[8,96,768]{2,1,0:T(8,128)(2,1)}, bf16[8,96,768]{2,1,0:T(8,128)(2,1)S(1)}, u32[]{:S(2)}, u32[]{:S(2)}) collective-permute-start(bf16[8,96,768]{2,1,0:T(8,128)(2,1)} %constant_dynamic-update-slice_fusion.refs_17_), channel_id=1, source_target_pairs={{0,2},{2,0},{1,3},{3,1},{4,6},{6,4},{5,7},{7,5},{8,10},{10,8},{9,1... | collective-permute-start | bytes 3538952 | tf_op jit(solution)/shard_map/ppermute | solution.py:930
  80.8 15.8 %collective-permute-start.25 = (bf16[4,48,1536]{2,1,0:T(8,128)(2,1)S(1)}, bf16[4,48,1536]{2,1,0:T(8,128)(2,1)}, u32[]{:S(2)}, u32[]{:S(2)}) collective-permute-start(bf16[4,48,1536]{2,1,0:T(8,128)(2,1)S(1)} %pad_maximum_fusion.3.refs_13_), channel_id=1, source_target_pairs={{0,4},{4,0},{8,12},{12,8},{16,20},{20,16},{24,28},{28,24},{1,5},{5... | collective-permute-start | bytes 1769480 | tf_op jit(solution)/shard_map/ppermute | solution.py:934
  137.1 19.6 %collective-permute-start.33 = (bf16[8,96,768]{2,1,0:T(8,128)(2,1)}, bf16[8,96,768]{2,1,0:T(8,128)(2,1)}, u32[]{:S(2)}, u32[]{:S(2)}) collective-permute-start(bf16[8,96,768]{2,1,0:T(8,128)(2,1)} %get-tuple-element.180), channel_id=1, source_target_pairs={{0,2},{2,0},{1,3},{3,1},{4,6},{6,4},{5,7},{7,5},{8,10},{10,8},{9,1... | collective-permute-start | bytes 3538952 | tf_op jit(solution)/shard_map/ppermute | solution.py:930
  145.1 13.3 %collective-permute-start.32 = (bf16[4,48,2304]{2,1,0:T(8,128)(2,1)}, bf16[4,48,2304]{2,1,0:T(8,128)(2,1)S(1)}, u32[]{:S(2)}, u32[]{:S(2)}) collective-permute-start(bf16[4,48,2304]{2,1,0:T(8,128)(2,1)} %get-tuple-element.189), channel_id=1, source_target_pairs={{0,2},{2,0},{1,3},{3,1},{4,6},{6,4},{5,7},{7,5},{8,10},{10,8},{9,1... | collective-permute-start | bytes 2654216 | tf_op jit(solution)/shard_map/ppermute | solution.py:930
  145.5 11.2 %collective-permute-start.35 = (bf16[512,384]{1,0:T(8,128)(2,1)S(1)}, bf16[512,384]{1,0:T(8,128)(2,1)S(1)}, u32[]{:S(2)}, u32[]{:S(2)}) collective-permute-start(bf16[512,384]{1,0:T(8,128)(2,1)S(1)} %copy-done.37), channel_id=1, source_target_pairs={{0,1},{1,0},{2,3},{3,2},{4,5},{5,4},{6,7},{7,6},{8,9},{9,8},{10,11... | collective-permute-start | bytes 1179656 | tf_op jit(solution)/shard_map/ppermute | solution.py:930
  147.0 11.7 %collective-permute-start.31 = (bf16[4,48,1536]{2,1,0:T(8,128)(2,1)}, bf16[4,48,1536]{2,1,0:T(8,128)(2,1)S(1)}, u32[]{:S(2)}, u32[]{:S(2)}) collective-permute-start(bf16[4,48,1536]{2,1,0:T(8,128)(2,1)} %get-tuple-element.187), channel_id=1, source_target_pairs={{0,2},{2,0},{1,3},{3,1},{4,6},{6,4},{5,7},{7,5},{8,10},{10,8},{9,1... | collective-permute-start | bytes 1769480 | tf_op jit(solution)/shard_map/ppermute | solution.py:930
  159.7 20.7 %collective-permute-start.40 = (bf16[4,48,2304]{2,1,0:T(8,128)(2,1)}, bf16[4,48,2304]{2,1,0:T(8,128)(2,1)}, u32[]{:S(2)}, u32[]{:S(2)}) collective-permute-start(bf16[4,48,2304]{2,1,0:T(8,128)(2,1)} %get-tuple-element.200), channel_id=1, source_target_pairs={{0,2},{2,0},{1,3},{3,1},{4,6},{6,4},{5,7},{7,5},{8,10},{10,8},{9,1... | collective-permute-start | bytes 2654216 | tf_op jit(solution)/shard_map/ppermute | solution.py:930
  159.7 22.6 %collective-permute-start.41 = (bf16[4,48,2304]{2,1,0:T(8,128)(2,1)S(1)}, bf16[4,48,2304]{2,1,0:T(8,128)(2,1)}, u32[]{:S(2)}, u32[]{:S(2)}) collective-permute-start(bf16[4,48,2304]{2,1,0:T(8,128)(2,1)S(1)} %add_convert_fusion.3), channel_id=1, source_target_pairs={{0,4},{4,0},{8,12},{12,8},{16,20},{20,16},{24,28},{28,24},{1,5},{5... | collective-permute-start | bytes 2654216 | tf_op jit(solution)/shard_map/ppermute | solution.py:934
  161.3 110.3 %collective-permute-start.30 = (f32[8,768]{1,0:T(8,128)S(1)}, f32[8,768]{1,0:T(8,128)}, u32[]{:S(2)}, u32[]{:S(2)}) collective-permute-start(f32[8,768]{1,0:T(8,128)S(1)} %copy-done.31), channel_id=1, source_target_pairs={{0,1},{1,0},{2,3},{3,2},{4,5},{5,4},{6,7},{7,6},{8,9},{9,8},{10,11... | collective-permute-start | bytes 73736 | tf_op jit(solution)/shard_map/ppermute | solution.py:930
  162.8 32.2 %collective-permute-start.39 = (bf16[4,48,1536]{2,1,0:T(8,128)(2,1)S(1)}, bf16[4,48,1536]{2,1,0:T(8,128)(2,1)}, u32[]{:S(2)}, u32[]{:S(2)}) collective-permute-start(bf16[4,48,1536]{2,1,0:T(8,128)(2,1)S(1)} %add_convert_fusion.6), channel_id=1, source_target_pairs={{0,4},{4,0},{8,12},{12,8},{16,20},{20,16},{24,28},{28,24},{1,5},{5... | collective-permute-start | bytes 1769480 | tf_op jit(solution)/shard_map/ppermute | solution.py:934
  163.3 35.4 %collective-permute-start.37 = (bf16[8,96,768]{2,1,0:T(8,128)(2,1)S(1)}, bf16[8,96,768]{2,1,0:T(8,128)(2,1)}, u32[]{:S(2)}, u32[]{:S(2)}) collective-permute-start(bf16[8,96,768]{2,1,0:T(8,128)(2,1)S(1)} %add_convert_fusion.1), channel_id=1, source_target_pairs={{0,1},{1,0},{2,3},{3,2},{4,5},{5,4},{6,7},{7,6},{8,9},{9,8},{10,11... | collective-permute-start | bytes 3538952 | tf_op jit(solution)/shard_map/ppermute | solution.py:930
  180.4 35.7 %collective-permute-start.56 = (f32[16,768]{1,0:T(8,128)S(1)}, f32[16,768]{1,0:T(8,128)}, u32[]{:S(2)}, u32[]{:S(2)}) collective-permute-start(f32[16,768]{1,0:T(8,128)S(1)} %add.137), channel_id=1, source_target_pairs={{0,4},{4,0},{8,12},{12,8},{16,20},{20,16},{24,28},{28,24},{1,5},{5... | collective-permute-start | bytes 147464 | tf_op jit(solution)/shard_map/ppermute | solution.py:934
  182.4 10.0 %collective-permute-start.38 = (bf16[4,48,1536]{2,1,0:T(8,128)(2,1)}, bf16[4,48,1536]{2,1,0:T(8,128)(2,1)}, u32[]{:S(2)}, u32[]{:S(2)}) collective-permute-start(bf16[4,48,1536]{2,1,0:T(8,128)(2,1)} %get-tuple-element.198), channel_id=1, source_target_pairs={{0,2},{2,0},{1,3},{3,1},{4,6},{6,4},{5,7},{7,5},{8,10},{10,8},{9,1... | collective-permute-start | bytes 1769480 | tf_op jit(solution)/shard_map/ppermute | solution.py:930
  195.8 14.9 %collective-permute-start.45 = (bf16[48,2304]{1,0:T(8,128)(2,1)}, bf16[48,2304]{1,0:T(8,128)(2,1)S(1)}, u32[]{:S(2)}, u32[]{:S(2)}) collective-permute-start(bf16[48,2304]{1,0:T(8,128)(2,1)} %get-tuple-element.248), channel_id=1, source_target_pairs={{0,24},{4,28},{8,16},{12,20},{16,8},{20,12},{24,0},{28,4},{1,25},{... | collective-permute-start | bytes 663560 | tf_op jit(solution)/shard_map/ppermute | solution.py:934
  198.6 16.4 %collective-permute-start.44 = (bf16[48,2304]{1,0:T(8,128)(2,1)}, bf16[48,2304]{1,0:T(8,128)(2,1)}, u32[]{:S(2)}, u32[]{:S(2)}) collective-permute-start(bf16[48,2304]{1,0:T(8,128)(2,1)} %get-tuple-element.249), channel_id=1, source_target_pairs={{0,16},{4,20},{8,24},{12,28},{16,0},{20,4},{24,8},{28,12},{1,17},{... | collective-permute-start | bytes 663560 | tf_op jit(solution)/shard_map/ppermute | solution.py:934
  198.7 16.3 %collective-permute-start.43 = (bf16[48,2304]{1,0:T(8,128)(2,1)}, bf16[48,2304]{1,0:T(8,128)(2,1)S(1)}, u32[]{:S(2)}, u32[]{:S(2)}) collective-permute-start(bf16[48,2304]{1,0:T(8,128)(2,1)} %get-tuple-element.250), channel_id=1, source_target_pairs={{0,8},{4,12},{8,0},{12,4},{16,24},{20,28},{24,16},{28,20},{1,9},{5... | collective-permute-start | bytes 663560 | tf_op jit(solution)/shard_map/ppermute | solution.py:934
  210.8 13.7 %collective-permute-start.42 = (bf16[4,96,768]{2,1,0:T(8,128)(2,1)S(1)}, bf16[4,96,768]{2,1,0:T(8,128)(2,1)S(1)}, u32[]{:S(2)}, u32[]{:S(2)}) collective-permute-start(bf16[4,96,768]{2,1,0:T(8,128)(2,1)S(1)} %slice.245), channel_id=1, source_target_pairs={{0,4},{4,0},{8,12},{12,8},{16,20},{20,16},{24,28},{28,24},{1,5},{5... | collective-permute-start | bytes 1769480 | tf_op jit(solution)/shard_map/ppermute | solution.py:934
  215.0 9.6 %collective-permute-start.53 = (bf16[4,48,1280]{2,1,0:T(8,128)(2,1)}, bf16[4,48,1280]{2,1,0:T(8,128)(2,1)S(1)}, u32[]{:S(2)}, u32[]{:S(2)}) collective-permute-start(bf16[4,48,1280]{2,1,0:T(8,128)(2,1)} %get-tuple-element.215), channel_id=1, source_target_pairs={{0,2},{2,0},{1,3},{3,1},{4,6},{6,4},{5,7},{7,5},{8,10},{10,8},{9,1... | collective-permute-start | bytes 1474568 | tf_op jit(solution)/shard_map/ppermute | solution.py:930
  216.9 11.3 %collective-permute-start.57 = (f32[16,768]{1,0:T(8,128)S(1)}, f32[16,768]{1,0:T(8,128)S(1)}, u32[]{:S(2)}, u32[]{:S(2)}) collective-permute-start(f32[16,768]{1,0:T(8,128)S(1)} %add.138), channel_id=1, source_target_pairs={{0,8},{4,12},{8,0},{12,4},{16,24},{20,28},{24,16},{28,20},{1,9},{5... | collective-permute-start | bytes 147464 | tf_op jit(solution)/shard_map/ppermute | solution.py:934
  216.9 19.3 %collective-permute-start.52 = (bf16[4,48,1280]{2,1,0:T(8,128)(2,1)}, bf16[4,48,1280]{2,1,0:T(8,128)(2,1)S(1)}, u32[]{:S(2)}, u32[]{:S(2)}) collective-permute-start(bf16[4,48,1280]{2,1,0:T(8,128)(2,1)} %get-tuple-element.221), channel_id=1, source_target_pairs={{0,2},{2,0},{1,3},{3,1},{4,6},{6,4},{5,7},{7,5},{8,10},{10,8},{9,1... | collective-permute-start | bytes 1474568 | tf_op jit(solution)/shard_map/ppermute | solution.py:930
  224.7 14.2 %collective-permute-start.54 = (bf16[4,48,1280]{2,1,0:T(8,128)(2,1)S(1)}, bf16[4,48,1280]{2,1,0:T(8,128)(2,1)S(1)}, u32[]{:S(2)}, u32[]{:S(2)}) collective-permute-start(bf16[4,48,1280]{2,1,0:T(8,128)(2,1)S(1)} %add_convert_fusion.8), channel_id=1, source_target_pairs={{0,4},{4,0},{8,12},{12,8},{16,20},{20,16},{24,28},{28,24},{1,5},{5... | collective-permute-start | bytes 1474568 | tf_op jit(solution)/shard_map/ppermute | solution.py:934
  227.0 13.0 %collective-permute-start.51 = (bf16[48,1536]{1,0:T(8,128)(2,1)}, bf16[48,1536]{1,0:T(8,128)(2,1)}, u32[]{:S(2)}, u32[]{:S(2)}) collective-permute-start(bf16[48,1536]{1,0:T(8,128)(2,1)} %get-tuple-element.251), channel_id=1, source_target_pairs={{0,24},{4,28},{8,16},{12,20},{16,8},{20,12},{24,0},{28,4},{1,25},{... | collective-permute-start | bytes 442376 | tf_op jit(solution)/shard_map/ppermute | solution.py:934
  228.2 14.1 %collective-permute-start.50 = (bf16[48,1536]{1,0:T(8,128)(2,1)S(1)}, bf16[48,1536]{1,0:T(8,128)(2,1)}, u32[]{:S(2)}, u32[]{:S(2)}) collective-permute-start(bf16[48,1536]{1,0:T(8,128)(2,1)S(1)} %get-tuple-element.252), channel_id=1, source_target_pairs={{0,16},{4,20},{8,24},{12,28},{16,0},{20,4},{24,8},{28,12},{1,17},{... | collective-permute-start | bytes 442376 | tf_op jit(solution)/shard_map/ppermute | solution.py:934
  238.9 26.4 %collective-permute-start.58 = (f32[16,768]{1,0:T(8,128)S(1)}, f32[16,768]{1,0:T(8,128)S(1)}, u32[]{:S(2)}, u32[]{:S(2)}) collective-permute-start(f32[16,768]{1,0:T(8,128)S(1)} %add.139), channel_id=1, source_target_pairs={{0,16},{4,20},{8,24},{12,28},{16,0},{20,4},{24,8},{28,12},{1,17},{... | collective-permute-start | bytes 147464 | tf_op jit(solution)/shard_map/ppermute | solution.py:934
  240.8 14.9 %collective-permute-start.62 = (bf16[512,768]{1,0:T(8,128)(2,1)S(1)}, bf16[512,768]{1,0:T(8,128)(2,1)S(1)}, u32[]{:S(2)}, u32[]{:S(2)}) collective-permute-start(bf16[512,768]{1,0:T(8,128)(2,1)S(1)} %copy-done.36), channel_id=1, source_target_pairs={{0,1},{1,0},{2,3},{3,2},{4,5},{5,4},{6,7},{7,6},{8,9},{9,8},{10,11... | collective-permute-start | bytes 2359304 | tf_op jit(solution)/shard_map/ppermute | solution.py:930
  242.3 16.2 %collective-permute-start.61 = (bf16[48,1280]{1,0:T(8,128)(2,1)S(1)}, bf16[48,1280]{1,0:T(8,128)(2,1)S(1)}, u32[]{:S(2)}, u32[]{:S(2)}) collective-permute-start(bf16[48,1280]{1,0:T(8,128)(2,1)S(1)} %get-tuple-element.257), channel_id=1, source_target_pairs={{0,24},{4,28},{8,16},{12,20},{16,8},{20,12},{24,0},{28,4},{1,25},{... | collective-permute-start | bytes 368648 | tf_op jit(solution)/shard_map/ppermute | solution.py:934
  244.3 16.9 %collective-permute-start.60 = (bf16[48,1280]{1,0:T(8,128)(2,1)S(1)}, bf16[48,1280]{1,0:T(8,128)(2,1)S(1)}, u32[]{:S(2)}, u32[]{:S(2)}) collective-permute-start(bf16[48,1280]{1,0:T(8,128)(2,1)S(1)} %get-tuple-element.258), channel_id=1, source_target_pairs={{0,16},{4,20},{8,24},{12,28},{16,0},{20,4},{24,8},{28,12},{1,17},{... | collective-permute-start | bytes 368648 | tf_op jit(solution)/shard_map/ppermute | solution.py:934
  258.6 12.2 %collective-permute-start.48 = (bf16[96,768]{1,0:T(8,128)(2,1)S(1)}, bf16[96,768]{1,0:T(8,128)(2,1)S(1)}, u32[]{:S(2)}, u32[]{:S(2)}) collective-permute-start(bf16[96,768]{1,0:T(8,128)(2,1)S(1)} %get-tuple-element.254), channel_id=1, source_target_pairs={{0,24},{4,28},{8,16},{12,20},{16,8},{20,12},{24,0},{28,4},{1,25},{... | collective-permute-start | bytes 442376 | tf_op jit(solution)/shard_map/ppermute | solution.py:934
  261.2 9.6 %collective-permute-start.47 = (bf16[96,768]{1,0:T(8,128)(2,1)S(1)}, bf16[96,768]{1,0:T(8,128)(2,1)S(1)}, u32[]{:S(2)}, u32[]{:S(2)}) collective-permute-start(bf16[96,768]{1,0:T(8,128)(2,1)S(1)} %get-tuple-element.255), channel_id=1, source_target_pairs={{0,16},{4,20},{8,24},{12,28},{16,0},{20,4},{24,8},{28,12},{1,17},{... | collective-permute-start | bytes 442376 | tf_op jit(solution)/shard_map/ppermute | solution.py:934
  (55 other events, 372.3 us)
